TPU v7x, 512 devices: a whole 4x4x16 slice. The times are simulated.
512 devices in a mesh: ctx: 64 (over z, y), tp: 8 (over x, core).
Axes of the slice: x: 4, y: 4, z: 16, core: 2. Of those that a mesh axis runs over, the one named last changes fastest.
Arguments:
- queries: bfloat16 [16384, 4096], P('ctx', 'tp'), may hold values from -1.796875 to 1.796875
- keys: bfloat16 [16384, 4096], P('ctx', 'tp'), may hold values from -1.796875 to 1.796875
- values: bfloat16 [16384, 4096], P('ctx', 'tp'), may hold values from -6 to 6
- grad_out: bfloat16 [16384, 4096], P('ctx', 'tp'), may hold values from -6 to 6
- out_weight: bfloat16 [4096, 4096], P('ctx', 'tp'), may hold values from -0.09375 to 0.09375
Outputs:
- grad_queries: bfloat16 [16384, 4096], P('ctx', 'tp')
- grad_keys: bfloat16 [16384, 4096], P('ctx', 'tp')
- grad_values: bfloat16 [16384, 4096], P('ctx', 'tp')
All inputs are finite; a program needn't handle non-finite values.
Results may differ from a plain program's by a relative error of at most 0.014.
Values may be sent and summed in bfloat16 or wider, within the bound.
No kernel may reach another device: no remote copies, remote signals or barrier semaphores. Data moves between devices by JAX's collectives and lax.ppermute only.
A program may use at most 128 MiB of HBM per device.

v0:
```python
import math

import jax
import jax.numpy as jnp
from jax import lax
from jax.sharding import PartitionSpec as P

DH = 128


def entering(value, axis, join, neutral, backward):
    count = lax.axis_size(axis)
    place = lax.axis_index(axis)
    ahead = count - 1 - place if backward else place
    gathered = lax.all_gather(value.astype(jnp.bfloat16), axis)
    state = jnp.zeros_like(value) + jnp.asarray(neutral, value.dtype)

    def one(hop, state):
        source = count - 1 - hop if backward else hop
        return join(state, lax.dynamic_index_in_dim(gathered, source, 0, False).astype(value.dtype))

    return lax.fori_loop(0, ahead, one, state)


def add_states(earlier, later):
    return jax.tree.map(jnp.add, earlier, later)


def local(queries, keys, values, grad_out, out_weight):
    tok_rows = queries.shape[0]
    local_width = queries.shape[1]
    local_heads = local_width // DH
    factor = 1.0 / math.sqrt(tok_rows * lax.axis_size("ctx"))
    full_grad = lax.all_gather(grad_out, "tp", axis=1, tiled=True)
    head_grad = jnp.dot(
        full_grad,
        lax.all_gather(out_weight, "ctx", axis=0, tiled=True),
        preferred_element_type=jnp.float32,
    ).astype(jnp.bfloat16)
    shaped = (tok_rows, local_heads, DH)
    query_rows = queries.reshape(shaped)
    key_rows = keys.reshape(shaped)
    value_rows = values.reshape(shaped)
    grad_rows = head_grad.reshape(shaped)
    key_local = jnp.einsum("thi,thj->hij", key_rows, value_rows, preferred_element_type=jnp.float32)
    query_local = jnp.einsum(
        "thi,thj->hij", query_rows, grad_rows, preferred_element_type=jnp.float32
    )
    zero_state = jnp.zeros((local_heads, DH, DH), jnp.float32)
    prefix = entering(key_local, "ctx", add_states, zero_state, False)
    suffix = entering(query_local, "ctx", add_states, zero_state, True)
    prefix_low = prefix.astype(jnp.bfloat16)
    suffix_low = suffix.astype(jnp.bfloat16)
    positions = jnp.arange(tok_rows, dtype=jnp.int32)
    causal = (positions[:, None] >= positions[None, :])[None]
    scores_grad = jnp.einsum(
        "thj,shj->hts", grad_rows, value_rows, preferred_element_type=jnp.float32
    )
    scores_grad = jnp.where(causal, scores_grad, 0.0).astype(jnp.bfloat16)
    scores = jnp.einsum("thi,shi->hts", query_rows, key_rows, preferred_element_type=jnp.float32)
    scores = jnp.where(causal, scores, 0.0).astype(jnp.bfloat16)
    grad_query = jnp.einsum(
        "hts,shi->thi", scores_grad, key_rows, preferred_element_type=jnp.float32
    )
    grad_query = grad_query + jnp.einsum(
        "thj,hij->thi", grad_rows, prefix_low, preferred_element_type=jnp.float32
    )
    grad_key = jnp.einsum(
        "hts,thi->shi", scores_grad, query_rows, preferred_element_type=jnp.float32
    )
    grad_key = grad_key + jnp.einsum(
        "shj,hij->shi", value_rows, suffix_low, preferred_element_type=jnp.float32
    )
    grad_value = jnp.einsum("hts,thj->shj", scores, grad_rows, preferred_element_type=jnp.float32)
    grad_value = grad_value + jnp.einsum(
        "shi,hij->shj", key_rows, suffix_low, preferred_element_type=jnp.float32
    )
    grad_queries = (factor * grad_query).astype(jnp.bfloat16).reshape(tok_rows, local_width)
    grad_keys = (factor * grad_key).astype(jnp.bfloat16).reshape(tok_rows, local_width)
    grad_values = (factor * grad_value).astype(jnp.bfloat16).reshape(tok_rows, local_width)
    return (grad_queries, grad_keys, grad_values)


def solution(mesh):
    placed = (P("ctx", "tp"), P("ctx", "tp"), P("ctx", "tp"), P("ctx", "tp"), P("ctx", "tp"))
    return jax.shard_map(
        local,
        mesh=mesh,
        in_specs=placed,
        out_specs=(P("ctx", "tp"), P("ctx", "tp"), P("ctx", "tp")),
        check_vma=False,
    )
```

profile of v0, /device:TPU:2, one launch (start us, length us, event | category | flops | bytes accessed | tf_op | source)
XLA Modules:
  0.0 579.1 jit_solution(2945502359002377975)
XLA Ops:
  8.7 1.9 convolution_convert_fusion.2
  10.7 35.8 %all-gather.7.cloned.1.call-done = bf16[256,4096]{1,0:T(8,128)(2,1)} async-done(((bf16[256,512]{1,0:T(8,128)(2,1)}), bf16[256,4096]{1,0:T(8,128)(2,1)}) %all-gather.7.cloned.1.call-update) | async-done | bytes 2097168 | tf_op jit(solution)/shard_map/all_gather | solution.py:34
  46.5 150.9 %all-gather.9.cloned.1.call-done = bf16[4096,512]{1,0:T(8,128)(2,1)} async-done(((bf16[64,512]{1,0:T(8,128)(2,1)}), bf16[4096,512]{1,0:T(8,128)(2,1)}) %all-gather.9.cloned.1.call-update) | async-done | bytes 4194320 | tf_op jit(solution)/shard_map/all_gather | solution.py:37
  197.4 4.1 convolution_convert_fusion
  203.6 148.9 %all-gather.11.cloned.1.call-done = bf16[256,128,128]{2,1,0:T(8,128)(2,1)} async-done(((bf16[4,128,128]{2,1,0:T(8,128)(2,1)}), bf16[256,128,128]{2,1,0:T(8,128)(2,1)}) %all-gather.11.cloned.1.call-update) | async-done | bytes 8388624 | tf_op jit(solution)/shard_map/all_gather | solution.py:15
  353.7 154.1 %all-gather.13.cloned.1.call-done = bf16[256,128,128]{2,1,0:T(8,128)(2,1)} async-done(((bf16[4,128,128]{2,1,0:T(8,128)(2,1)}), bf16[256,128,128]{2,1,0:T(8,128)(2,1)}) %all-gather.13.cloned.1.call-update) | async-done | bytes 8388624 | tf_op jit(solution)/shard_map/all_gather | solution.py:15
  507.8 62.1 %while.23 = (s32[]{:T(128)}, f32[4,128,128]{2,1,0:T(8,128)S(1)}, s32[]{:T(128)}, bf16[64,4,128,128]{3,2,1,0:T(8,128)(2,1)}, s32[]{:T(128)}, /*index=5*/s32[]{:T(128)}, s32[]{:T(128)}, s32[]{:T(128)}) while((s32[]{:T(128)}, f32[4,128,128]{2,1,0:T(8,128)S(1)}, s32[]{:T(128)}, bf16[64,4,128,128]{3,2,1,0:T(8,128)(2,1)}, s32[]{:T(128)}, ...), condition=%wide.region_3.4_spmd, body=%wide.region_2.3_spmd.sunk | while | flops 131078 | bytes 655503 | solution.py:22
  507.8 1.0 convert_add_fusion.5
  508.8 1.0 convert_add_fusion.5
  509.8 1.0 convert_add_fusion.5
  510.8 1.0 convert_add_fusion.5
  511.7 1.0 convert_add_fusion.5
  512.7 1.0 convert_add_fusion.5
  513.7 1.0 convert_add_fusion.5
  514.7 1.0 convert_add_fusion.5
  515.7 1.0 convert_add_fusion.5
  516.7 1.0 convert_add_fusion.5
  517.7 1.0 convert_add_fusion.5
  518.7 1.0 convert_add_fusion.5
  519.6 1.0 convert_add_fusion.5
  520.6 1.0 convert_add_fusion.5
  521.6 1.0 convert_add_fusion.5
  522.6 1.0 convert_add_fusion.5
  523.6 1.0 convert_add_fusion.5
  524.6 1.0 convert_add_fusion.5
  525.6 1.0 convert_add_fusion.5
  526.5 1.0 convert_add_fusion.5
  527.5 1.0 convert_add_fusion.5
  528.5 1.0 convert_add_fusion.5
  529.5 1.0 convert_add_fusion.5
  530.5 1.0 convert_add_fusion.5
  531.5 1.0 convert_add_fusion.5
  532.5 1.0 convert_add_fusion.5
  533.4 1.0 convert_add_fusion.5
  534.4 1.0 convert_add_fusion.5
  535.4 1.0 convert_add_fusion.5
  536.4 1.0 convert_add_fusion.5
  537.4 1.0 convert_add_fusion.5
  538.4 1.0 convert_add_fusion.5
  539.4 1.0 convert_add_fusion.5
  540.3 1.0 convert_add_fusion.5
  541.3 1.0 convert_add_fusion.5
  542.3 1.0 convert_add_fusion.5
  543.3 1.0 convert_add_fusion.5
  544.3 1.0 convert_add_fusion.5
  545.3 1.0 convert_add_fusion.5
  546.3 1.0 convert_add_fusion.5
  547.3 1.0 convert_add_fusion.5
  548.2 1.0 convert_add_fusion.5
  549.2 1.0 convert_add_fusion.5
  550.2 1.0 convert_add_fusion.5
  551.2 1.0 convert_add_fusion.5
  552.2 1.0 convert_add_fusion.5
  553.2 1.0 convert_add_fusion.5
  554.2 1.0 convert_add_fusion.5
  555.1 1.0 convert_add_fusion.5
  556.1 1.0 convert_add_fusion.5
  557.1 1.0 convert_add_fusion.5
  558.1 1.0 convert_add_fusion.5
  559.1 1.0 convert_add_fusion.5
  560.1 1.0 convert_add_fusion.5
  561.1 1.0 convert_add_fusion.5
  562.0 1.0 convert_add_fusion.5
  567.0 1.0 convert_add_fusion.5
  (37 shorter events, 13.2 us)
Async XLA Ops:
  7.2 1.5 copy-start
  7.2 39.4 %all-gather.7.cloned.1.call-start = ((), (), s32[]{:S(2)}) async-start(), calls=%async_computation | async-start | bytes 2359296 | tf_op jit(solution)/shard_map/all_gather | solution.py:34
  7.9 189.5 %all-gather.9.cloned.1.call-start = ((), (), s32[]{:S(2)}) async-start(), calls=%async_computation.1 | async-start | bytes 4259840 | tf_op jit(solution)/shard_map/all_gather | solution.py:37
  8.7 343.9 %all-gather.11.cloned.1.call-start = ((), (), s32[]{:S(2)}) async-start(), calls=%async_computation.2 | async-start | bytes 8519680 | tf_op jit(solution)/shard_map/all_gather | solution.py:15
  10.6 191.0 %copy-start.1 = (bf16[256,512]{1,0:T(8,128)(2,1)S(1)}, bf16[256,512]{1,0:T(8,128)(2,1)}, u32[]{:S(2)}) copy-start(bf16[256,512]{1,0:T(8,128)(2,1)} %param.9) | copy-start | bytes 786436
  10.6 192.4 %copy-start.2 = (bf16[256,512]{1,0:T(8,128)(2,1)S(1)}, bf16[256,512]{1,0:T(8,128)(2,1)}, u32[]{:S(2)}) copy-start(bf16[256,512]{1,0:T(8,128)(2,1)} %param.10) | copy-start | bytes 786436
  10.6 497.1 %all-gather.13.cloned.1.call-start = ((), (), s32[]{:S(2)}) async-start(), calls=%async_computation.3 | async-start | bytes 8519680 | tf_op jit(solution)/shard_map/all_gather | solution.py:15
Sparse Core Ops, SparseCore 0:
  10.1 36.3 all-gather.6
  49.5 147.8 all-gather.8
  200.9 151.5 all-gather.10
  355.9 151.7 all-gather.12
where the time goes:
time: 580 us; the launch traced here: 579 us
  waiting for transfers between devices  491 us (85%)
  other arithmetic  60.7 us (10%)
  between operations  13.9 us (2%)
  matrix products  8.26 us (1%)
    all_gather x2, waiting for transfers between devices, entering(): gathered = lax.all_gather(value.astype(jnp.bfloat16), axis)  303 us
    all_gather x1, waiting for transfers between devices, local(): lax.all_gather(out_weight, 'ctx', axis=0, tiled=True)  151 us
    add x63, other arithmetic, add_states(): return jax.tree.map(jnp.add, earlier, later)  60.7 us
    all_gather x1, waiting for transfers between devices, local(): full_grad = lax.all_gather(grad_out, 'tp', axis=1, tiled=True)  35.8 us
  transfers between devices with their start and end apart: 4, of which 4 were waited for; matrix products, arithmetic and copies ran while one was open for 2% of the time, Pallas kernels for 0%

commit v1 on v0

v1 whole, which is shorter than its diff:
```python
import math

import jax
import jax.numpy as jnp
from jax import lax
from jax.experimental import pallas as pl
from jax.experimental.pallas import tpu as pltpu
from jax.sharding import PartitionSpec as P

DH = 128
NY = 4
ZG = 4
F32 = jnp.float32
BF16 = jnp.bfloat16


def groups(ctx):
    nz = ctx // NY
    y_line = [[z * NY + y for y in range(NY)] for z in range(nz)]
    z_line = [[z * NY + y for z in range(nz)] for y in range(NY)]
    z_near = [[(g * ZG + i) * NY + y for i in range(ZG)] for g in range(nz // ZG) for y in range(NY)]
    z_far = [[(g * ZG + i) * NY + y for g in range(nz // ZG)] for i in range(ZG) for y in range(NY)]
    return y_line, z_line, z_near, z_far


def exchange(pieces, group):
    return lax.all_to_all(pieces, "ctx", 0, 0, axis_index_groups=group)


def call(kernel, out_shape, flops, size, smem=()):
    def run(*operands):
        specs = [
            pl.BlockSpec(memory_space=pltpu.SMEM if i in smem else pltpu.VMEM) for i in range(len(operands))
        ]
        many = isinstance(out_shape, (list, tuple))
        out_specs = [pl.BlockSpec(memory_space=pltpu.VMEM)] * len(out_shape) if many else pl.BlockSpec(memory_space=pltpu.VMEM)
        return pl.pallas_call(
            kernel,
            out_shape=out_shape,
            in_specs=specs,
            out_specs=out_specs,
            compiler_params=pltpu.CompilerParams(vmem_limit_bytes=40 * 1024 * 1024),
            cost_estimate=pl.CostEstimate(flops=flops, bytes_accessed=size, transcendentals=0),
        )(*operands)

    return run


def shape(dims, dtype=BF16):
    return jax.ShapeDtypeStruct(dims, dtype)


def dot(a, b, ca, cb):
    return lax.dot_general(a, b, (((ca,), (cb,)), ((), ())), preferred_element_type=F32)


def pack_kernel(q_ref, k_ref, v_ref, g_ref, out_ref):
    for y in range(NY):
        for at, ref in enumerate((q_ref, k_ref, v_ref)):
            out_ref[y, at] = ref[:, y * DH : (y + 1) * DH]
        rows = g_ref.shape[1] // (2 * NY)
        low = g_ref[:, y * rows : (y + 1) * rows]
        high = g_ref[:, (NY + y) * rows : (NY + y + 1) * rows]
        out_ref[y, 3] = jnp.concatenate([low, high], axis=1)


def product_kernel(a_ref, b_ref, out_ref):
    tokens = a_ref.shape[0]
    step = tokens // NY
    for t in range(NY):
        rows = pl.ds(t * step, step)
        part = dot(a_ref[rows, :], b_ref[...], 1, 0).astype(BF16)
        for h in range(NY):
            out_ref[h, rows, :] = part[:, h * DH : (h + 1) * DH]


def state_kernel(packed_ref, part_ref, grad_ref, states_ref, copies_ref):
    step = packed_ref.shape[2]
    total_k = jnp.zeros((DH, DH), F32)
    total_q = jnp.zeros((DH, DH), F32)
    for b in range(NY):
        rows = pl.ds(b * step, step)
        grad = part_ref[0, rows, :].astype(F32)
        for y in range(1, NY):
            grad = grad + part_ref[y, rows, :].astype(F32)
        grad = grad.astype(BF16)
        grad_ref[rows, :] = grad
        key_state = dot(packed_ref[b, 1], packed_ref[b, 2], 0, 0)
        query_state = dot(packed_ref[b, 0], grad, 0, 0)
        states_ref[0, b] = key_state
        states_ref[1, b] = query_state
        total_k = total_k + key_state
        total_q = total_q + query_state
    for i in range(ZG):
        copies_ref[i, 0] = total_k.astype(BF16)
        copies_ref[i, 1] = total_q.astype(BF16)


def final_kernel(factor, place_ref, packed_ref, grad_ref, states_ref, near_ref, far_ref, out_ref):
    step = packed_ref.shape[2]
    inner, outer = place_ref[0], place_ref[1]
    prefix = jnp.zeros((DH, DH), F32)
    suffix = jnp.zeros((DH, DH), F32)
    for i in range(near_ref.shape[0]):
        prefix = prefix + jnp.where(i < inner, near_ref[i, 0].astype(F32), 0.0)
        suffix = suffix + jnp.where(i > inner, near_ref[i, 1].astype(F32), 0.0)
    for i in range(far_ref.shape[0]):
        other = far_ref[i].astype(F32)
        prefix = prefix + jnp.where(i < outer, other, 0.0)
        suffix = suffix + jnp.where(i > outer, other, 0.0)
    suffixes = [suffix]
    for b in range(NY - 1, 0, -1):
        suffix = suffix + states_ref[1, b]
        suffixes.append(suffix)
    suffixes = suffixes[::-1]
    row = lax.broadcasted_iota(jnp.int32, (step, step), 0)
    col = lax.broadcasted_iota(jnp.int32, (step, step), 1)
    lower = row >= col
    upper = row <= col
    for b in range(NY):
        query, key, value = packed_ref[b, 0], packed_ref[b, 1], packed_ref[b, 2]
        grad = grad_ref[b * step : (b + 1) * step, :]
        before = prefix.astype(BF16)
        after = suffixes[b].astype(BF16)
        scores_grad = jnp.where(lower, dot(grad, value, 1, 1), 0.0).astype(BF16)
        scores_grad_t = jnp.where(upper, dot(value, grad, 1, 1), 0.0).astype(BF16)
        scores_t = jnp.where(upper, dot(key, query, 1, 1), 0.0).astype(BF16)
        grad_q = dot(scores_grad, key, 1, 0) + dot(grad, before, 1, 1)
        grad_k = dot(scores_grad_t, query, 1, 0) + dot(value, after, 1, 1)
        grad_v = dot(scores_t, grad, 1, 0) + dot(key, after, 1, 0)
        out_ref[b, 0] = (factor * grad_q).astype(BF16)
        out_ref[b, 1] = (factor * grad_k).astype(BF16)
        out_ref[b, 2] = (factor * grad_v).astype(BF16)
        prefix = prefix + states_ref[0, b]


def unpack_kernel(in_ref, q_ref, k_ref, v_ref):
    for h in range(NY):
        for at, ref in enumerate((q_ref, k_ref, v_ref)):
            ref[:, h * DH : (h + 1) * DH] = in_ref[h, at]


def local(queries, keys, values, grad_out, out_weight):
    step, width = queries.shape
    ctx, tp = lax.axis_size("ctx"), lax.axis_size("tp")
    nz = ctx // NY
    tokens = NY * step
    depth = nz * out_weight.shape[0]
    factor = 1.0 / math.sqrt(step * ctx)
    y_line, z_line, z_near, z_far = groups(ctx)
    z = lax.axis_index("ctx") // NY
    place = jnp.stack([z % ZG, z // ZG]).astype(jnp.int32)

    packed = call(pack_kernel, shape((NY, 4, step, DH)), 0, 8 * step * width * 2)(queries, keys, values, grad_out)
    packed = exchange(packed, y_line)
    mine = packed[:, 3].reshape(tokens, DH)
    full_grad = lax.all_gather(mine, "tp", axis=1, tiled=True)
    weight = exchange(jnp.broadcast_to(out_weight[None], (nz,) + out_weight.shape), z_line)
    weight = weight.reshape(depth, width)
    parts = call(product_kernel, shape((NY, tokens, DH)), 2 * tokens * depth * width, 4 * 1024 * 1024)(full_grad, weight)
    parts = exchange(parts, y_line)
    grads, states, copies = call(
        state_kernel,
        [shape((tokens, DH)), shape((2, NY, DH, DH), F32), shape((ZG, 2, DH, DH))],
        4 * tokens * DH * DH,
        3 * 1024 * 1024,
    )(packed, parts)
    near = exchange(copies, z_near)
    total = jnp.sum(near.astype(F32), axis=0).astype(BF16)
    other = jnp.arange(nz // ZG, dtype=jnp.int32)[:, None, None]
    far = exchange(jnp.where(other < place[1], total[1][None], total[0][None]), z_far)
    result = call(
        lambda *refs: final_kernel(factor, *refs),
        shape((NY, 3, step, DH)),
        8 * 2 * tokens * step * DH,
        3 * 1024 * 1024,
        smem=(0,),
    )(place, packed, grads, states, near, far)
    result = exchange(result, y_line)
    out = shape((step, width))
    return tuple(call(unpack_kernel, [out, out, out], 0, 6 * step * width * 2)(result))


def solution(mesh):
    placed = P("ctx", "tp")
    return jax.shard_map(
        local,
        mesh=mesh,
        in_specs=(placed,) * 5,
        out_specs=(placed,) * 3,
        check_vma=False,
    )
```

time: 580 us -> 171 us (0.29)
  waiting for transfers between devices: 491 us -> 67.5 us
  other arithmetic: 60.7 us -> 0.86 us
  blocking collectives: 0 us -> 44.6 us
  starting transfers between devices: 0.16 us -> 31.3 us
  matrix products: 8.26 us -> 0 us
    all_gather x4 -> x1, waiting for transfers between devices: 490 us -> 0.01 us  [local(): full_grad = lax.all_gather(mine, 'tp', axis=1, tiled=True)]
    all_to_all x0 -> x3, waiting for transfers between devices: none -> 67.4 us  [exchange(): return lax.all_to_all(pieces, 'ctx', 0, 0, axis_index_groups=group)]
    add x63 -> x0, other arithmetic: 60.7 us -> none  [add_states(): return jax.tree.map(jnp.add, earlier, later)]
    all_to_all x0 -> x3, blocking collectives: none -> 44.6 us  [exchange(): return lax.all_to_all(pieces, 'ctx', 0, 0, axis_index_groups=group)]
    all_to_all x0 -> x3, starting transfers between devices: none -> 31.3 us  [exchange(): return lax.all_to_all(pieces, 'ctx', 0, 0, axis_index_groups=group)]
    dot_general x10 -> x0, matrix products: 8.26 us -> none  [the longest x1 4.06 us: local(): jnp.dot(full_grad, lax.all_gather(out_weight, 'ctx', axis=0, tiled=True),...]
  transfers between devices with their start and end apart: 4 -> 4, of which waited for: 4 -> 3; matrix products, arithmetic and copies ran while one was open for 2% -> 0% of each run, Pallas kernels for 0% -> 0%
where the time goes in v1:
time: 171 us
  waiting for transfers between devices  67.5 us (39%)
  blocking collectives  44.6 us (26%)
  starting transfers between devices  31.3 us (18%)
  between operations  14.1 us (8%)
  local copies, waits for them, and re-layouts  7.18 us (4%)
  Pallas kernels  5.27 us (3%)
    all_to_all x3, waiting for transfers between devices, exchange(): return lax.all_to_all(pieces, 'ctx', 0, 0, axis_index_groups=group)  67.4 us
    all_to_all x3, blocking collectives, exchange(): return lax.all_to_all(pieces, 'ctx', 0, 0, axis_index_groups=group)  44.6 us
    all_to_all x3, starting transfers between devices, exchange(): return lax.all_to_all(pieces, 'ctx', 0, 0, axis_index_groups=group)  31.3 us
    unnamed x12, local copies, waits for them, and re-layouts  5.39 us
    pallas_call x5, Pallas kernels, run(): pl.pallas_call(kernel, out_shape=out_shape, in_specs=specs, out_specs=out...  5.27 us
  transfers between devices with their start and end apart: 4, of which 3 were waited for; matrix products, arithmetic and copies ran while one was open for 0% of the time, Pallas kernels for 0%

profile of v1, /device:TPU:2, one launch (start us, length us, event | category | flops | bytes accessed | tf_op | source)
XLA Modules:
  0.0 170.7 jit_solution(18272460897809517894)
XLA Ops:
  7.2 0.0 copy-start.1
  7.2 0.9 copy-done.1
  8.1 0.0 copy-start.2
  8.1 0.9 copy-done.2
  9.1 0.0 copy-start.3
  9.1 0.9 copy-done.3
  10.0 0.0 copy-start.4
  10.0 0.9 copy-done.4
  11.0 0.0 copy-start.5
  11.0 0.2 shard_map.76
  11.2 19.4 %all_to_all.30.packed_ref.refs_1_ = bf16[4,4,256,128]{3,2,1,0:T(8,128)(2,1)S(1)} all-to-all(bf16[4,4,256,128]{3,2,1,0:T(8,128)(2,1)S(1)} %shard_map.76), channel_id=1, replica_groups={{0,8,16,24},{32,40,48,56},{64,72,80,88},{96,104,112,120},{128,136,144,1..., dimensions={0} | all-to-all | bytes 2097152 | tf_op jit(solution)/shard_map/all_to_all | solution.py:27
  30.5 0.0 copy-done.5
  30.5 1.1 broadcast_in_dim.35
  31.6 15.2 %all-to-all-start.1 = ((bf16[16,64,512]{2,1,0:T(8,128)(2,1)}), bf16[16,64,512]{2,1,0:T(8,128)(2,1)S(1)}, u32[]{:S(2)}, u32[]{:S(2)}) async-start(bf16[16,64,512]{2,1,0:T(8,128)(2,1)} %broadcast_in_dim.35), calls=%async_computation.1 | async-start | bytes 2097152 | tf_op jit(solution)/shard_map/all_to_all | solution.py:27
  46.8 0.0 all-gather.2.cloned.1.call-start
  46.9 0.7 slice.12
  47.6 0.0 all-gather.2.cloned.1.call-update
  47.6 47.5 %all-to-all-done.1 = bf16[16,64,512]{2,1,0:T(8,128)(2,1)S(1)} async-done(((bf16[16,64,512]{2,1,0:T(8,128)(2,1)}), bf16[16,64,512]{2,1,0:T(8,128)(2,1)S(1)}, u32[]{:S(2)}, u32[]{:S(2)}) %all-to-all-start.1) | async-done | bytes 1048608 | tf_op jit(solution)/shard_map/all_to_all | solution.py:27
  95.2 0.0 all-gather.2.cloned.1.call-done.a_ref
  95.2 0.0 copy-start
  95.2 1.6 copy-done
  96.7 1.2 shard_map.77
  98.0 13.3 %all_to_all.31.part_ref = bf16[4,1024,128]{2,1,0:T(8,128)(2,1)S(1)} all-to-all(bf16[4,1024,128]{2,1,0:T(8,128)(2,1)S(1)} %shard_map.77), channel_id=1, replica_groups={{0,8,16,24},{32,40,48,56},{64,72,80,88},{96,104,112,120},{128,136,144,1..., dimensions={0} | all-to-all | bytes 2097152 | tf_op jit(solution)/shard_map/all_to_all | solution.py:27
  111.3 1.1 shard_map.78
  112.4 6.3 %all-to-all-start.3 = ((bf16[4,2,128,128]{3,2,1,0:T(8,128)(2,1)}), bf16[4,2,128,128]{3,2,1,0:T(8,128)(2,1)S(1)}, u32[]{:S(2)}, u32[]{:S(2)}) async-start(bf16[4,2,128,128]{3,2,1,0:T(8,128)(2,1)} %get-tuple-element.8), calls=%async_computation.3 | async-start | bytes 524288 | tf_op jit(solution)/shard_map/all_to_all | solution.py:27
  118.6 6.8 %all-to-all-done.3.refs_4_ = bf16[4,2,128,128]{3,2,1,0:T(8,128)(2,1)S(1)} async-done(((bf16[4,2,128,128]{3,2,1,0:T(8,128)(2,1)}), bf16[4,2,128,128]{3,2,1,0:T(8,128)(2,1)S(1)}, u32[]{:S(2)}, u32[]{:S(2)}) %all-to-all-start.3) | async-done | bytes 262176 | tf_op jit(solution)/shard_map/all_to_all | solution.py:27
  125.5 0.7 broadcast_select_fusion
  126.2 9.8 %all-to-all-start.4 = ((bf16[4,128,128]{2,1,0:T(8,128)(2,1)}), bf16[4,128,128]{2,1,0:T(8,128)(2,1)S(1)}, u32[]{:S(2)}, u32[]{:S(2)}) async-start(bf16[4,128,128]{2,1,0:T(8,128)(2,1)} %broadcast_select_fusion), calls=%async_computation.4 | async-start | bytes 262144 | tf_op jit(solution)/shard_map/all_to_all | solution.py:27
  136.0 0.1 pad_add_fusion.refs_0_
  136.1 13.1 %all-to-all-done.4.refs_5_ = bf16[4,128,128]{2,1,0:T(8,128)(2,1)S(1)} async-done(((bf16[4,128,128]{2,1,0:T(8,128)(2,1)}), bf16[4,128,128]{2,1,0:T(8,128)(2,1)S(1)}, u32[]{:S(2)}, u32[]{:S(2)}) %all-to-all-start.4) | async-done | bytes 131104 | tf_op jit(solution)/shard_map/all_to_all | solution.py:27
  149.2 1.8 %shard_map.79 = bf16[4,3,256,128]{3,2,1,0:T(8,128)(2,1)S(1)} custom-call(s32[2]{0:T(128)S(1)} %pad_add_fusion.refs_0_, bf16[4,4,256,128]{3,2,1,0:T(8,128)(2,1)S(1)} %all_to_all.30.packed_ref.refs_1_, bf16[1024,128]{1,0:T(8,128)(2,1)S(1)} %get-tuple-element.6.refs_2_, f32[2,4,128,128]{3,2,1,0:T(8,128)S(1)} %get-tuple-element.7.refs_3_, ...), custom_call_target="tpu_custom_call" | custom-call | flops 536870912 | bytes 3145728 | tf_op jit(solution)/shard_map/pallas_call | solution.py:37
  151.0 11.9 %all_to_all.32.in_ref = bf16[4,3,256,128]{3,2,1,0:T(8,128)(2,1)S(1)} all-to-all(bf16[4,3,256,128]{3,2,1,0:T(8,128)(2,1)S(1)} %shard_map.79), channel_id=1, replica_groups={{0,8,16,24},{32,40,48,56},{64,72,80,88},{96,104,112,120},{128,136,144,1..., dimensions={0} | all-to-all | bytes 1572864 | tf_op jit(solution)/shard_map/all_to_all | solution.py:27
  162.9 1.0 shard_map.80
  (3 shorter events, 0.1 us)
Async XLA Ops:
  7.2 1.0 copy-start.1
  8.1 0.9 copy-start.2
  9.1 0.9 copy-start.3
  10.0 0.9 copy-start.4
  11.0 19.6 %copy-start.5 = (bf16[64,512]{1,0:T(8,128)(2,1)S(1)}, bf16[64,512]{1,0:T(8,128)(2,1)}, u32[]{:S(2)}) copy-start(bf16[64,512]{1,0:T(8,128)(2,1)} %param.9) | copy-start | bytes 196612
  31.6 63.5 %all-to-all-start.1 = ((bf16[16,64,512]{2,1,0:T(8,128)(2,1)}), bf16[16,64,512]{2,1,0:T(8,128)(2,1)S(1)}, u32[]{:S(2)}, u32[]{:S(2)}) async-start(bf16[16,64,512]{2,1,0:T(8,128)(2,1)} %broadcast_in_dim.35), calls=%async_computation.1 | async-start | bytes 2097152 | tf_op jit(solution)/shard_map/all_to_all | solution.py:27
  46.8 48.3 %all-gather.2.cloned.1.call-start = ((), (), s32[]{:S(2)}) async-start(), calls=%async_computation.6 | async-start | bytes 2359296 | tf_op jit(solution)/shard_map/all_gather | solution.py:157
  95.2 1.6 copy-start
  112.4 13.0 %all-to-all-start.3 = ((bf16[4,2,128,128]{3,2,1,0:T(8,128)(2,1)}), bf16[4,2,128,128]{3,2,1,0:T(8,128)(2,1)S(1)}, u32[]{:S(2)}, u32[]{:S(2)}) async-start(bf16[4,2,128,128]{3,2,1,0:T(8,128)(2,1)} %get-tuple-element.8), calls=%async_computation.3 | async-start | bytes 524288 | tf_op jit(solution)/shard_map/all_to_all | solution.py:27
  126.2 23.0 %all-to-all-start.4 = ((bf16[4,128,128]{2,1,0:T(8,128)(2,1)}), bf16[4,128,128]{2,1,0:T(8,128)(2,1)S(1)}, u32[]{:S(2)}, u32[]{:S(2)}) async-start(bf16[4,128,128]{2,1,0:T(8,128)(2,1)} %broadcast_select_fusion), calls=%async_computation.4 | async-start | bytes 262144 | tf_op jit(solution)/shard_map/all_to_all | solution.py:27
Sparse Core Ops, SparseCore 0:
  50.3 33.6 all-gather.1

commit v2 on v1

--- a/solution.py
+++ b/solution.py
@@ -27,18 +27,23 @@
     return lax.all_to_all(pieces, "ctx", 0, 0, axis_index_groups=group)
 
 
-def call(kernel, out_shape, flops, size, smem=()):
+def call(kernel, out_shape, flops, size, smem=(), hbm=(), scratch=(), out_hbm=False):
     def run(*operands):
         specs = [
-            pl.BlockSpec(memory_space=pltpu.SMEM if i in smem else pltpu.VMEM) for i in range(len(operands))
+            pl.BlockSpec(memory_space=pltpu.SMEM if i in smem else pltpu.HBM if i in hbm else pltpu.VMEM)
+            for i in range(len(operands))
+        ]
+        operands = [
+            pltpu.with_memory_space_constraint(x, pltpu.HBM) if i in hbm else x for i, x in enumerate(operands)
         ]
         many = isinstance(out_shape, (list, tuple))
-        out_specs = [pl.BlockSpec(memory_space=pltpu.VMEM)] * len(out_shape) if many else pl.BlockSpec(memory_space=pltpu.VMEM)
+        out_specs = [pl.BlockSpec(memory_space=pltpu.VMEM)] * len(out_shape) if many else pl.BlockSpec(memory_space=pltpu.HBM if out_hbm else pltpu.VMEM)
         return pl.pallas_call(
             kernel,
             out_shape=out_shape,
             in_specs=specs,
             out_specs=out_specs,
+            scratch_shapes=scratch,
             compiler_params=pltpu.CompilerParams(vmem_limit_bytes=40 * 1024 * 1024),
             cost_estimate=pl.CostEstimate(flops=flops, bytes_accessed=size, transcendentals=0),
         )(*operands)
@@ -54,22 +59,38 @@
     return lax.dot_general(a, b, (((ca,), (cb,)), ((), ())), preferred_element_type=F32)
 
 
-def pack_kernel(q_ref, k_ref, v_ref, g_ref, out_ref):
+def pack_kernel(q_ref, k_ref, v_ref, g_ref, out_ref, grad, sems):
+    load = pltpu.make_async_copy(g_ref, grad, sems.at[NY, 0])
+    load.start()
+    moves = []
     for y in range(NY):
         for at, ref in enumerate((q_ref, k_ref, v_ref)):
-            out_ref[y, at] = ref[:, y * DH : (y + 1) * DH]
-        rows = g_ref.shape[1] // (2 * NY)
-        low = g_ref[:, y * rows : (y + 1) * rows]
-        high = g_ref[:, (NY + y) * rows : (NY + y + 1) * rows]
+            move = pltpu.make_async_copy(ref.at[:, pl.ds(y * DH, DH)], out_ref.at[y, at], sems.at[y, at])
+            move.start()
+            moves.append(move)
+    load.wait()
+    rows = grad.shape[1] // (2 * NY)
+    for y in range(NY):
+        low = grad[:, y * rows : (y + 1) * rows]
+        high = grad[:, (NY + y) * rows : (NY + y + 1) * rows]
         out_ref[y, 3] = jnp.concatenate([low, high], axis=1)
-
-
-def product_kernel(a_ref, b_ref, out_ref):
-    tokens = a_ref.shape[0]
+    for move in moves:
+        move.wait()
+
+
+def product_kernel(place_ref, a0_ref, a1_ref, a2_ref, a3_ref, b_ref, out_ref):
+    tokens, depth = a0_ref.shape
     step = tokens // NY
+    held = (a0_ref, a1_ref, a2_ref, a3_ref)
+    chips = len(held)
     for t in range(NY):
         rows = pl.ds(t * step, step)
-        part = dot(a_ref[rows, :], b_ref[...], 1, 0).astype(BF16)
+        part = jnp.zeros((step, b_ref.shape[1]), F32)
+        for d, ref in enumerate(held):
+            chip = lax.rem(place_ref[2] + (chips - d), chips)
+            start = pl.multiple_of(chip * depth, depth)
+            part = part + dot(ref[rows, :], b_ref[pl.ds(start, depth), :], 1, 0)
+        part = part.astype(BF16)
         for h in range(NY):
             out_ref[h, rows, :] = part[:, h * DH : (h + 1) * DH]
 
@@ -148,16 +169,42 @@
     depth = nz * out_weight.shape[0]
     factor = 1.0 / math.sqrt(step * ctx)
     y_line, z_line, z_near, z_far = groups(ctx)
+    at = lax.axis_index("tp")
     z = lax.axis_index("ctx") // NY
-    place = jnp.stack([z % ZG, z // ZG]).astype(jnp.int32)
-
-    packed = call(pack_kernel, shape((NY, 4, step, DH)), 0, 8 * step * width * 2)(queries, keys, values, grad_out)
+    place = jnp.stack([z % ZG, z // ZG, at // 2]).astype(jnp.int32)
+    earlier = jnp.arange(nz // ZG, dtype=jnp.int32) < place[1]
+    first = at % 2 == 0
+    queries, place, earlier, first = lax.optimization_barrier((queries, place, earlier, first))
+
+    packed = call(
+        pack_kernel,
+        shape((NY, 4, step, DH)),
+        0,
+        8 * step * width * 2,
+        hbm=range(4),
+        scratch=[pltpu.VMEM((step, width), BF16), pltpu.SemaphoreType.DMA((NY + 1, 3))],
+    )(queries, keys, values, grad_out)
     packed = exchange(packed, y_line)
     mine = packed[:, 3].reshape(tokens, DH)
-    full_grad = lax.all_gather(mine, "tp", axis=1, tiled=True)
-    weight = exchange(jnp.broadcast_to(out_weight[None], (nz,) + out_weight.shape), z_line)
-    weight = weight.reshape(depth, width)
-    parts = call(product_kernel, shape((NY, tokens, DH)), 2 * tokens * depth * width, 4 * 1024 * 1024)(full_grad, weight)
+    swap = [(t, t ^ 1) for t in range(tp)]
+    other = lax.ppermute(mine, "tp", swap)
+    pair = jnp.concatenate([jnp.where(first, mine, other), jnp.where(first, other, mine)], axis=1)
+    shares = [pair]
+    for d in range(1, tp // 2):
+        shares.append(lax.ppermute(pair, "tp", [(t, (t + 2 * d) % tp) for t in range(tp)]))
+    shard = out_weight.shape[0]
+    main = shard - shard // 8
+    rest, pair_seen = lax.optimization_barrier((out_weight, pair))
+    weight = lax.all_gather(rest[:main], "ctx", axis_index_groups=z_line)
+    last = exchange(jnp.broadcast_to(rest[None, main:], (nz, shard - main, width)), z_line)
+    weight = jnp.concatenate([weight, last], axis=1).reshape(depth, width)
+    parts = call(
+        product_kernel,
+        shape((NY, tokens, DH)),
+        2 * tokens * depth * width,
+        4 * 1024 * 1024,
+        smem=(0,),
+    )(place, *shares, weight)
     parts = exchange(parts, y_line)
     grads, states, copies = call(
         state_kernel,
@@ -167,8 +214,7 @@
     )(packed, parts)
     near = exchange(copies, z_near)
     total = jnp.sum(near.astype(F32), axis=0).astype(BF16)
-    other = jnp.arange(nz // ZG, dtype=jnp.int32)[:, None, None]
-    far = exchange(jnp.where(other < place[1], total[1][None], total[0][None]), z_far)
+    far = exchange(jnp.where(earlier[:, None, None], total[1][None], total[0][None]), z_far)
     result = call(
         lambda *refs: final_kernel(factor, *refs),
         shape((NY, 3, step, DH)),

time: 171 us -> 153 us (0.89)
  blocking collectives: 44.6 us -> 114 us
  waiting for transfers between devices: 67.5 us -> 1.51 us
  between operations: 14.1 us -> 0.87 us
  local copies, waits for them, and re-layouts: 7.18 us -> 0.7 us
  starting transfers between devices: 31.3 us -> 27.6 us
    all_to_all x3 -> x1, waiting for transfers between devices: 67.4 us -> 0.01 us  [exchange(): return lax.all_to_all(pieces, 'ctx', 0, 0, axis_index_groups=group)]
    all_gather x0 -> x1, blocking collectives: none -> 37.9 us  [local(): weight = lax.all_gather(rest[:main], 'ctx', axis_index_groups=z_line)]
    all_to_all x3 -> x5, blocking collectives: 44.6 us -> 76.2 us  [exchange(): return lax.all_to_all(pieces, 'ctx', 0, 0, axis_index_groups=group)]
    all_to_all x3 -> x1, starting transfers between devices: 31.3 us -> 15.2 us  [exchange(): return lax.all_to_all(pieces, 'ctx', 0, 0, axis_index_groups=group)]
    ppermute x0 -> x4, starting transfers between devices: none -> 12.4 us  [the longest x3 10.5 us: local(): lax.ppermute(pair, 'tp', [(t, (t + 2 * d) % tp) for t in range(tp)])]
    unnamed x12 -> x0, local copies, waits for them, and re-layouts: 5.39 us -> none
  transfers between devices with their start and end apart: 4 -> 5, of which waited for: 3 -> 1; matrix products, arithmetic and copies ran while one was open for 0% -> 1% of each run, Pallas kernels for 0% -> 0%
where the time goes in v2:
time: 153 us
  blocking collectives  114 us (75%)
  starting transfers between devices  27.6 us (18%)
  Pallas kernels  6.28 us (4%)
  other arithmetic  1.6 us (1%)
    all_to_all x5, blocking collectives, exchange(): return lax.all_to_all(pieces, 'ctx', 0, 0, axis_index_groups=group)  76.2 us
    all_gather x1, blocking collectives, local(): weight = lax.all_gather(rest[:main], 'ctx', axis_index_groups=z_line)  37.9 us
    all_to_all x1, starting transfers between devices, exchange(): return lax.all_to_all(pieces, 'ctx', 0, 0, axis_index_groups=group)  15.2 us
    ppermute x3, starting transfers between devices, local(): lax.ppermute(pair, 'tp', [(t, (t + 2 * d) % tp) for t in range(tp)])  10.5 us
    pallas_call x5, Pallas kernels, run(): pl.pallas_call(kernel, out_shape=out_shape, in_specs=specs, out_specs=out...  6.28 us
  transfers between devices with their start and end apart: 5, of which 1 were waited for; matrix products, arithmetic and copies ran while one was open for 1% of the time, Pallas kernels for 0%

profile of v2, /device:TPU:2, one launch (start us, length us, event | category | flops | bytes accessed | tf_op | source)
XLA Modules:
  0.0 152.7 jit_solution(2138573726508080916)
XLA Ops:
  0.7 0.1 pad_add_fusion.place_ref.refs_0_
  0.8 1.3 shard_map.76
  2.1 19.4 %all_to_all.30.packed_ref.refs_1_ = bf16[4,4,256,128]{3,2,1,0:T(8,128)(2,1)S(1)} all-to-all(bf16[4,4,256,128]{3,2,1,0:T(8,128)(2,1)S(1)} %shard_map.76), channel_id=1, replica_groups={{0,8,16,24},{32,40,48,56},{64,72,80,88},{96,104,112,120},{128,136,144,1..., dimensions={0} | all-to-all | bytes 2097152 | tf_op jit(solution)/shard_map/all_to_all | solution.py:27
  21.5 0.0 slice-start
  21.5 1.9 %collective-permute-start = (bf16[1024,128]{1,0:T(8,128)(2,1)S(1)}, bf16[1024,128]{1,0:T(8,128)(2,1)S(1)}, u32[]{:S(2)}, u32[]{:S(2)}) collective-permute-start(bf16[1024,128]{1,0:T(8,128)(2,1)S(1)} %bitcast.14), channel_id=1, source_target_pairs={{0,1},{1,0},{2,3},{3,2},{4,5},{5,4},{6,7},{7,6},{8,9},{9,8},{10,11... | collective-permute-start | bytes 786440 | tf_op jit(solution)/shard_map/ppermute | solution.py:190
  23.5 1.5 collective-permute-done
  25.0 0.1 broadcast_select_fusion.1
  25.0 0.0 slice-start.1
  25.0 0.1 pad_maximum_fusion.1.a0_ref
  25.1 0.0 slice-done
  25.1 0.7 broadcast_in_dim.35
  25.8 15.2 %all-to-all-start.1 = ((bf16[16,8,512]{2,1,0:T(8,128)(2,1)}), bf16[16,8,512]{2,1,0:T(8,128)(2,1)S(1)}, u32[]{:S(2)}, u32[]{:S(2)}) async-start(bf16[16,8,512]{2,1,0:T(8,128)(2,1)} %broadcast_in_dim.35), calls=%async_computation.1 | async-start | bytes 262144 | tf_op jit(solution)/shard_map/all_to_all | solution.py:27
  41.0 2.4 %collective-permute-start.3 = (bf16[1024,256]{1,0:T(8,128)(2,1)S(1)}, bf16[1024,256]{1,0:T(8,128)(2,1)S(1)}, u32[]{:S(2)}, u32[]{:S(2)}) collective-permute-start(bf16[1024,256]{1,0:T(8,128)(2,1)S(1)} %pad_maximum_fusion.1.a0_ref), channel_id=1, source_target_pairs={{0,6},{1,7},{2,0},{3,1},{4,2},{5,3},{6,4},{7,5},{8,14},{9,15},{10,... | collective-permute-start | bytes 1572872 | tf_op jit(solution)/shard_map/ppermute | solution.py:194
  43.4 4.3 %collective-permute-start.2 = (bf16[1024,256]{1,0:T(8,128)(2,1)S(1)}, bf16[1024,256]{1,0:T(8,128)(2,1)S(1)}, u32[]{:S(2)}, u32[]{:S(2)}) collective-permute-start(bf16[1024,256]{1,0:T(8,128)(2,1)S(1)} %pad_maximum_fusion.1.a0_ref), channel_id=1, source_target_pairs={{0,4},{1,5},{2,6},{3,7},{4,0},{5,1},{6,2},{7,3},{8,12},{9,13},{10,... | collective-permute-start | bytes 1572872 | tf_op jit(solution)/shard_map/ppermute | solution.py:194
  47.8 3.7 %collective-permute-start.1 = (bf16[1024,256]{1,0:T(8,128)(2,1)S(1)}, bf16[1024,256]{1,0:T(8,128)(2,1)S(1)}, u32[]{:S(2)}, u32[]{:S(2)}) collective-permute-start(bf16[1024,256]{1,0:T(8,128)(2,1)S(1)} %pad_maximum_fusion.1.a0_ref), channel_id=1, source_target_pairs={{0,2},{1,3},{2,4},{3,5},{4,6},{5,7},{6,0},{7,1},{8,10},{9,11},{10,... | collective-permute-start | bytes 1572872 | tf_op jit(solution)/shard_map/ppermute | solution.py:194
  51.5 0.0 slice-done.1
  51.5 37.9 %all-gather = bf16[896,512]{1,0:T(8,128)(2,1)} all-gather(bf16[56,512]{1,0:T(8,128)(2,1)S(1)} %slice-done.1), channel_id=2, replica_groups={{0,32,64,96,128,160,192,224,256,288,320,352,384,416,448,480},{8,40,72,1..., dimensions={0}, use_global_device_ids=true | all-gather | bytes 974848 | tf_op jit(solution)/shard_map/all_gather | solution.py:198
  89.4 0.0 all-to-all-done.1
  89.4 1.3 pad_maximum_fusion
  90.7 0.0 collective-permute-done.3.a3_ref
  90.7 0.0 collective-permute-done.2.a2_ref
  90.7 0.0 collective-permute-done.1.a1_ref
  90.7 1.8 %shard_map.77 = bf16[4,1024,128]{2,1,0:T(8,128)(2,1)S(1)} custom-call(s32[3]{0:T(128)S(1)} %pad_add_fusion.place_ref.refs_0_, bf16[1024,256]{1,0:T(8,128)(2,1)S(1)} %pad_maximum_fusion.1.a0_ref, bf16[1024,256]{1,0:T(8,128)(2,1)S(1)} %collective-permute-done.1.a1_ref, bf16[1024,256]{1,0:T(8,128)(2,1)S(1)} %collective-permute-done.2.a2_ref, ...), custom_call_target="tpu_custom_call" | custom-call | flops 1073741824 | bytes 4194304 | tf_op jit(solution)/shard_map/pallas_call | solution.py:41
  92.5 13.3 %all_to_all.31.part_ref = bf16[4,1024,128]{2,1,0:T(8,128)(2,1)S(1)} all-to-all(bf16[4,1024,128]{2,1,0:T(8,128)(2,1)S(1)} %shard_map.77), channel_id=1, replica_groups={{0,8,16,24},{32,40,48,56},{64,72,80,88},{96,104,112,120},{128,136,144,1..., dimensions={0} | all-to-all | bytes 2097152 | tf_op jit(solution)/shard_map/all_to_all | solution.py:27
  105.9 0.4 shard_map.78
  106.2 9.8 %all_to_all.32.refs_4_ = bf16[4,2,128,128]{3,2,1,0:T(8,128)(2,1)S(1)} all-to-all(bf16[4,2,128,128]{3,2,1,0:T(8,128)(2,1)S(1)} %get-tuple-element.17), channel_id=1, replica_groups={{0,32,64,96},{8,40,72,104},{16,48,80,112},{24,56,88,120},{128,160,192,2..., dimensions={0} | all-to-all | bytes 524288 | tf_op jit(solution)/shard_map/all_to_all | solution.py:27
  116.1 0.1 broadcast_select_fusion.2
  116.2 21.8 %all_to_all.33.refs_5_ = bf16[4,128,128]{2,1,0:T(8,128)(2,1)S(1)} all-to-all(bf16[4,128,128]{2,1,0:T(8,128)(2,1)S(1)} %broadcast_select_fusion.2), channel_id=1, replica_groups={{0,128,256,384},{8,136,264,392},{16,144,272,400},{24,152,280,408},{32,1..., dimensions={0} | all-to-all | bytes 262144 | tf_op jit(solution)/shard_map/all_to_all | solution.py:27
  138.0 1.8 %shard_map.79 = bf16[4,3,256,128]{3,2,1,0:T(8,128)(2,1)S(1)} custom-call(s32[3]{0:T(128)S(1)} %pad_add_fusion.place_ref.refs_0_, bf16[4,4,256,128]{3,2,1,0:T(8,128)(2,1)S(1)} %all_to_all.30.packed_ref.refs_1_, bf16[1024,128]{1,0:T(8,128)(2,1)S(1)} %get-tuple-element.15.refs_2_, f32[2,4,128,128]{3,2,1,0:T(8,128)S(1)} %get-tuple-element.16.refs_3_, ...), custom_call_target="tpu_custom_call" | custom-call | flops 536870912 | bytes 3145728 | tf_op jit(solution)/shard_map/pallas_call | solution.py:41
  139.7 11.9 %all_to_all.34.in_ref = bf16[4,3,256,128]{3,2,1,0:T(8,128)(2,1)S(1)} all-to-all(bf16[4,3,256,128]{3,2,1,0:T(8,128)(2,1)S(1)} %shard_map.79), channel_id=1, replica_groups={{0,8,16,24},{32,40,48,56},{64,72,80,88},{96,104,112,120},{128,136,144,1..., dimensions={0} | all-to-all | bytes 1572864 | tf_op jit(solution)/shard_map/all_to_all | solution.py:27
  151.6 1.0 shard_map.80
  (4 shorter events, 0.1 us)
Async XLA Ops:
  21.5 3.6 %slice-start = ((bf16[64,512]{1,0:T(8,128)(2,1)}), bf16[8,512]{1,0:T(8,128)(2,1)S(1)}, s32[]{:S(2)}) async-start(bf16[64,512]{1,0:T(8,128)(2,1)} %param.9), calls=%async_computation.6 | async-start | bytes 16384 | tf_op jit(solution)/shard_map/slice | solution.py:199
  21.5 3.4 %collective-permute-start = (bf16[1024,128]{1,0:T(8,128)(2,1)S(1)}, bf16[1024,128]{1,0:T(8,128)(2,1)S(1)}, u32[]{:S(2)}, u32[]{:S(2)}) collective-permute-start(bf16[1024,128]{1,0:T(8,128)(2,1)S(1)} %bitcast.14), channel_id=1, source_target_pairs={{0,1},{1,0},{2,3},{3,2},{4,5},{5,4},{6,7},{7,6},{8,9},{9,8},{10,11... | collective-permute-start | bytes 786440 | tf_op jit(solution)/shard_map/ppermute | solution.py:190
  25.0 26.5 %slice-start.1 = ((bf16[64,512]{1,0:T(8,128)(2,1)}), bf16[56,512]{1,0:T(8,128)(2,1)S(1)}, s32[]{:S(2)}) async-start(bf16[64,512]{1,0:T(8,128)(2,1)} %param.9), calls=%async_computation.7 | async-start | bytes 114688 | tf_op jit(solution)/shard_map/slice | solution.py:198
  25.8 63.6 %all-to-all-start.1 = ((bf16[16,8,512]{2,1,0:T(8,128)(2,1)}), bf16[16,8,512]{2,1,0:T(8,128)(2,1)S(1)}, u32[]{:S(2)}, u32[]{:S(2)}) async-start(bf16[16,8,512]{2,1,0:T(8,128)(2,1)} %broadcast_in_dim.35), calls=%async_computation.1 | async-start | bytes 262144 | tf_op jit(solution)/shard_map/all_to_all | solution.py:27
  41.0 49.7 %collective-permute-start.3 = (bf16[1024,256]{1,0:T(8,128)(2,1)S(1)}, bf16[1024,256]{1,0:T(8,128)(2,1)S(1)}, u32[]{:S(2)}, u32[]{:S(2)}) collective-permute-start(bf16[1024,256]{1,0:T(8,128)(2,1)S(1)} %pad_maximum_fusion.1.a0_ref), channel_id=1, source_target_pairs={{0,6},{1,7},{2,0},{3,1},{4,2},{5,3},{6,4},{7,5},{8,14},{9,15},{10,... | collective-permute-start | bytes 1572872 | tf_op jit(solution)/shard_map/ppermute | solution.py:194
  43.4 47.3 %collective-permute-start.2 = (bf16[1024,256]{1,0:T(8,128)(2,1)S(1)}, bf16[1024,256]{1,0:T(8,128)(2,1)S(1)}, u32[]{:S(2)}, u32[]{:S(2)}) collective-permute-start(bf16[1024,256]{1,0:T(8,128)(2,1)S(1)} %pad_maximum_fusion.1.a0_ref), channel_id=1, source_target_pairs={{0,4},{1,5},{2,6},{3,7},{4,0},{5,1},{6,2},{7,3},{8,12},{9,13},{10,... | collective-permute-start | bytes 1572872 | tf_op jit(solution)/shard_map/ppermute | solution.py:194
  47.8 43.0 %collective-permute-start.1 = (bf16[1024,256]{1,0:T(8,128)(2,1)S(1)}, bf16[1024,256]{1,0:T(8,128)(2,1)S(1)}, u32[]{:S(2)}, u32[]{:S(2)}) collective-permute-start(bf16[1024,256]{1,0:T(8,128)(2,1)S(1)} %pad_maximum_fusion.1.a0_ref), channel_id=1, source_target_pairs={{0,2},{1,3},{2,4},{3,5},{4,6},{5,7},{6,0},{7,1},{8,10},{9,11},{10,... | collective-permute-start | bytes 1572872 | tf_op jit(solution)/shard_map/ppermute | solution.py:194

commit v3 on v2

v3 whole, which is shorter than its diff:
```python
import math

import jax
import jax.numpy as jnp
from jax import lax
from jax.experimental import pallas as pl
from jax.experimental.pallas import tpu as pltpu
from jax.sharding import PartitionSpec as P

DH = 128
NY = 4
ZG = 4
F32 = jnp.float32
BF16 = jnp.bfloat16


def groups(ctx):
    nz = ctx // NY
    y_line = [[z * NY + y for y in range(NY)] for z in range(nz)]
    z_line = [[z * NY + y for z in range(nz)] for y in range(NY)]
    z_near = [[(g * ZG + i) * NY + y for i in range(ZG)] for g in range(nz // ZG) for y in range(NY)]
    z_far = [[(g * ZG + i) * NY + y for g in range(nz // ZG)] for i in range(ZG) for y in range(NY)]
    return y_line, z_line, z_near, z_far


def exchange(pieces, group):
    return lax.all_to_all(pieces, "ctx", 0, 0, axis_index_groups=group)


def call(kernel, out_shape, flops, size, smem=(), hbm=(), scratch=(), out_hbm=False):
    def run(*operands):
        specs = [
            pl.BlockSpec(memory_space=pltpu.SMEM if i in smem else pltpu.HBM if i in hbm else pltpu.VMEM)
            for i in range(len(operands))
        ]
        operands = [
            pltpu.with_memory_space_constraint(x, pltpu.HBM) if i in hbm else x for i, x in enumerate(operands)
        ]
        many = isinstance(out_shape, (list, tuple))
        out_specs = [pl.BlockSpec(memory_space=pltpu.VMEM)] * len(out_shape) if many else pl.BlockSpec(memory_space=pltpu.HBM if out_hbm else pltpu.VMEM)
        return pl.pallas_call(
            kernel,
            out_shape=out_shape,
            in_specs=specs,
            out_specs=out_specs,
            scratch_shapes=scratch,
            compiler_params=pltpu.CompilerParams(vmem_limit_bytes=40 * 1024 * 1024),
            cost_estimate=pl.CostEstimate(flops=flops, bytes_accessed=size, transcendentals=0),
        )(*operands)

    return run


def shape(dims, dtype=BF16):
    return jax.ShapeDtypeStruct(dims, dtype)


def dot(a, b, ca, cb):
    return lax.dot_general(a, b, (((ca,), (cb,)), ((), ())), preferred_element_type=F32)


def block_of(place_ref, d):
    return lax.rem(place_ref[2] + (NY - d), NY)


def pack_kernel(place_ref, q_ref, k_ref, v_ref, g_ref, *rest):
    outs, (grad, pieces, sems) = rest[:NY], rest[NY:]
    load = pltpu.make_async_copy(g_ref, grad, sems.at[NY, 0])
    load.start()
    moves = []
    for d, out_ref in enumerate(outs):
        start = pl.multiple_of(lax.rem(place_ref[2] + d, NY) * DH, DH)
        for at, ref in enumerate((q_ref, k_ref, v_ref)):
            move = pltpu.make_async_copy(ref.at[:, pl.ds(start, DH)], out_ref.at[at], sems.at[d, at])
            move.start()
            moves.append(move)
    load.wait()
    rows = grad.shape[1] // (2 * NY)
    for y in range(NY):
        low = grad[:, y * rows : (y + 1) * rows]
        high = grad[:, (NY + y) * rows : (NY + y + 1) * rows]
        pieces[y] = jnp.concatenate([low, high], axis=1)
    for d, out_ref in enumerate(outs):
        out_ref[3] = pieces[lax.rem(place_ref[2] + d, NY)]
    for move in moves:
        move.wait()


def mine_kernel(*refs):
    step = refs[0].shape[1]
    for d in range(NY):
        refs[NY][d * step : (d + 1) * step, :] = refs[d][3]


def pair_kernel(place_ref, mine_ref, other_ref, out_ref):
    first = place_ref[4] == 0
    mine, other = mine_ref[...], other_ref[...]
    out_ref[:, :DH] = jnp.where(first, mine, other)
    out_ref[:, DH:] = jnp.where(first, other, mine)


def product_kernel(place_ref, a0_ref, a1_ref, a2_ref, a3_ref, main_ref, last_ref, out_ref, weight):
    tokens, depth = a0_ref.shape
    step = tokens // NY
    held = (a0_ref, a1_ref, a2_ref, a3_ref)
    chips = len(held)
    main, last = main_ref.shape[1], last_ref.shape[1]
    for z in range(main_ref.shape[0]):
        low = z * (main + last)
        weight[low : low + main, :] = main_ref[z]
        weight[low + main : low + main + last, :] = last_ref[z]
    for t in range(NY):
        part = jnp.zeros((step, weight.shape[1]), F32)
        for d, ref in enumerate(held):
            chip = lax.rem(place_ref[3] + (chips - d), chips)
            start = pl.multiple_of(chip * depth, depth)
            part = part + dot(ref[t * step : (t + 1) * step, :], weight[pl.ds(start, depth), :], 1, 0)
        part = part.astype(BF16)
        rows = pl.ds(pl.multiple_of(block_of(place_ref, t) * step, step), step)
        for h in range(NY):
            out_ref[h, rows, :] = part[:, h * DH : (h + 1) * DH]


def state_kernel(place_ref, p0_ref, p1_ref, p2_ref, p3_ref, part_ref, grad_ref, states_ref, copies_ref):
    step = p0_ref.shape[1]
    total_k = jnp.zeros((DH, DH), F32)
    total_q = jnp.zeros((DH, DH), F32)
    for d, ref in enumerate((p0_ref, p1_ref, p2_ref, p3_ref)):
        rows = pl.ds(pl.multiple_of(block_of(place_ref, d) * step, step), step)
        grad = part_ref[0, rows, :].astype(F32)
        for y in range(1, NY):
            grad = grad + part_ref[y, rows, :].astype(F32)
        grad = grad.astype(BF16)
        grad_ref[d] = grad
        key_state = dot(ref[1], ref[2], 0, 0)
        query_state = dot(ref[0], grad, 0, 0)
        states_ref[0, d] = key_state
        states_ref[1, d] = query_state
        total_k = total_k + key_state
        total_q = total_q + query_state
    for i in range(ZG):
        copies_ref[i, 0] = total_k.astype(BF16)
        copies_ref[i, 1] = total_q.astype(BF16)


def final_kernel(factor, place_ref, p0_ref, p1_ref, p2_ref, p3_ref, grad_ref, states_ref, near_ref, far_ref, out_ref):
    step = p0_ref.shape[1]
    inner, outer = place_ref[0], place_ref[1]
    prefix = jnp.zeros((DH, DH), F32)
    suffix = jnp.zeros((DH, DH), F32)
    for i in range(near_ref.shape[0]):
        prefix = prefix + jnp.where(i < inner, near_ref[i, 0].astype(F32), 0.0)
        suffix = suffix + jnp.where(i > inner, near_ref[i, 1].astype(F32), 0.0)
    for i in range(far_ref.shape[0]):
        other = far_ref[i].astype(F32)
        prefix = prefix + jnp.where(i < outer, other, 0.0)
        suffix = suffix + jnp.where(i > outer, other, 0.0)
    row = lax.broadcasted_iota(jnp.int32, (step, step), 0)
    col = lax.broadcasted_iota(jnp.int32, (step, step), 1)
    lower = row >= col
    upper = row <= col
    for d, ref in enumerate((p0_ref, p1_ref, p2_ref, p3_ref)):
        block = block_of(place_ref, d)
        query, key, value = ref[0], ref[1], ref[2]
        grad = grad_ref[d]
        before, after = prefix, suffix
        for e in range(NY):
            if e != d:
                other = block_of(place_ref, e)
                before = before + jnp.where(other < block, states_ref[0, e], 0.0)
                after = after + jnp.where(other > block, states_ref[1, e], 0.0)
        before = before.astype(BF16)
        after = after.astype(BF16)
        scores_grad = jnp.where(lower, dot(grad, value, 1, 1), 0.0).astype(BF16)
        scores_grad_t = jnp.where(upper, dot(value, grad, 1, 1), 0.0).astype(BF16)
        scores_t = jnp.where(upper, dot(key, query, 1, 1), 0.0).astype(BF16)
        grad_q = dot(scores_grad, key, 1, 0) + dot(grad, before, 1, 1)
        grad_k = dot(scores_grad_t, query, 1, 0) + dot(value, after, 1, 1)
        grad_v = dot(scores_t, grad, 1, 0) + dot(key, after, 1, 0)
        out_ref[block, 0] = (factor * grad_q).astype(BF16)
        out_ref[block, 1] = (factor * grad_k).astype(BF16)
        out_ref[block, 2] = (factor * grad_v).astype(BF16)


def unpack_kernel(in_ref, q_ref, k_ref, v_ref):
    for h in range(NY):
        for at, ref in enumerate((q_ref, k_ref, v_ref)):
            ref[:, h * DH : (h + 1) * DH] = in_ref[h, at]


def local(queries, keys, values, grad_out, out_weight):
    step, width = queries.shape
    ctx, tp = lax.axis_size("ctx"), lax.axis_size("tp")
    nz = ctx // NY
    tokens = NY * step
    depth = nz * out_weight.shape[0]
    factor = 1.0 / math.sqrt(step * ctx)
    y_line, z_line, z_near, z_far = groups(ctx)
    at = lax.axis_index("tp")
    here = lax.axis_index("ctx")
    z = here // NY
    place = jnp.stack([z % ZG, z // ZG, here % NY, at // 2, at % 2]).astype(jnp.int32)
    earlier = jnp.arange(nz // ZG, dtype=jnp.int32) < place[1]
    queries, place, earlier = lax.optimization_barrier((queries, place, earlier))

    packed = call(
        pack_kernel,
        [shape((4, step, DH))] * NY,
        0,
        8 * step * width * 2,
        smem=(0,),
        hbm=range(1, 5),
        scratch=[
            pltpu.VMEM((step, width), BF16),
            pltpu.VMEM((NY, step, DH), BF16),
            pltpu.SemaphoreType.DMA((NY + 1, 3)),
        ],
    )(place, queries, keys, values, grad_out)
    packed = list(packed)
    for d in (1, 3, 2):
        turn = [(i, i // NY * NY + (i + d) % NY) for i in range(ctx)]
        packed[d] = lax.ppermute(packed[d], "ctx", turn)
    mine = call(mine_kernel, shape((tokens, DH)), 0, 4 * tokens * DH)(*packed)
    other = lax.ppermute(mine, "tp", [(t, t ^ 1) for t in range(tp)])
    pair = call(pair_kernel, shape((tokens, 2 * DH)), 0, 8 * tokens * DH, smem=(0,))(place, mine, other)
    shares = [pair]
    for d in range(1, tp // 2):
        shares.append(lax.ppermute(pair, "tp", [(t, (t + 2 * d) % tp) for t in range(tp)]))
    shard = out_weight.shape[0]
    main = shard - shard // 4
    kept, pair_seen = lax.optimization_barrier((out_weight, pair))
    weight = lax.all_gather(kept[:main], "ctx", axis_index_groups=z_line)
    last = exchange(jnp.broadcast_to(out_weight[None, main:], (nz, shard - main, width)), z_line)
    parts = call(
        product_kernel,
        shape((NY, tokens, DH)),
        2 * tokens * depth * width,
        4 * 1024 * 1024,
        smem=(0,),
        scratch=[pltpu.VMEM((depth, width), BF16)],
    )(place, *shares, weight, last)
    parts = exchange(parts, y_line)
    grads, states, copies = call(
        state_kernel,
        [shape((NY, step, DH)), shape((2, NY, DH, DH), F32), shape((ZG, 2, DH, DH))],
        4 * tokens * DH * DH,
        3 * 1024 * 1024,
        smem=(0,),
    )(place, *packed, parts)
    near = exchange(copies, z_near)
    total = jnp.sum(near.astype(F32), axis=0).astype(BF16)
    far = exchange(jnp.where(earlier[:, None, None], total[1][None], total[0][None]), z_far)
    result = call(
        lambda *refs: final_kernel(factor, *refs),
        shape((NY, 3, step, DH)),
        8 * 2 * tokens * step * DH,
        3 * 1024 * 1024,
        smem=(0,),
    )(place, *packed, grads, states, near, far)
    result = exchange(result, y_line)
    out = shape((step, width))
    return tuple(call(unpack_kernel, [out, out, out], 0, 6 * step * width * 2)(result))


def solution(mesh):
    placed = P("ctx", "tp")
    return jax.shard_map(
        local,
        mesh=mesh,
        in_specs=(placed,) * 5,
        out_specs=(placed,) * 3,
        check_vma=False,
    )
```

time: 153 us -> 143 us (0.935)
  blocking collectives: 114 us -> 91.4 us
  starting transfers between devices: 27.6 us -> 39.3 us
  Pallas kernels: 6.28 us -> 8.76 us
    all_to_all x5 -> x4, blocking collectives: 76.2 us -> 56.9 us  [exchange(): return lax.all_to_all(pieces, 'ctx', 0, 0, axis_index_groups=group)]
    ppermute x1 -> x4, starting transfers between devices: 1.92 us -> 13.5 us  [the longest x3 11.6 us: local(): packed[d] = lax.ppermute(packed[d], 'ctx', turn)]
    all_gather x1, blocking collectives: 37.9 us -> 34.4 us  [local(): weight = lax.all_gather(kept[:main], 'ctx', axis_index_groups=z_line)]
    pallas_call x5 -> x7, Pallas kernels: 6.28 us -> 8.76 us  [run(): pl.pallas_call(kernel, out_shape=out_shape, in_specs=specs, out_specs=out...]
  transfers between devices with their start and end apart: 5 -> 8, of which waited for: 1 -> 1; matrix products, arithmetic and copies ran while one was open for 1% -> 1% of each run, Pallas kernels for 0% -> 0%
where the time goes in v3:
time: 143 us
  blocking collectives  91.4 us (64%)
  starting transfers between devices  39.3 us (27%)
  Pallas kernels  8.76 us (6%)
  waiting for transfers between devices  1.52 us (1%)
    all_to_all x4, blocking collectives, exchange(): return lax.all_to_all(pieces, 'ctx', 0, 0, axis_index_groups=group)  56.9 us
    all_gather x1, blocking collectives, local(): weight = lax.all_gather(kept[:main], 'ctx', axis_index_groups=z_line)  34.4 us
    all_to_all x1, starting transfers between devices, exchange(): return lax.all_to_all(pieces, 'ctx', 0, 0, axis_index_groups=group)  15.2 us
    ppermute x3, starting transfers between devices, local(): packed[d] = lax.ppermute(packed[d], 'ctx', turn)  11.6 us
    ppermute x3, starting transfers between devices, local(): lax.ppermute(pair, 'tp', [(t, (t + 2 * d) % tp) for t in range(tp)])  10.6 us
    pallas_call x7, Pallas kernels, run(): pl.pallas_call(kernel, out_shape=out_shape, in_specs=specs, out_specs=out...  8.76 us
  transfers between devices with their start and end apart: 8, of which 1 were waited for; matrix products, arithmetic and copies ran while one was open for 1% of the time, Pallas kernels for 0%

profile of v3, /device:TPU:2, one launch (start us, length us, event | category | flops | bytes accessed | tf_op | source)
XLA Modules:
  0.0 142.8 jit_solution(7367544112375213397)
XLA Ops:
  0.7 0.1 stack.23.place_ref.refs_0_
  0.8 1.9 %shard_map.76 = (bf16[4,256,128]{2,1,0:T(8,128)(2,1)S(1)}, bf16[4,256,128]{2,1,0:T(8,128)(2,1)S(1)}, bf16[4,256,128]{2,1,0:T(8,128)(2,1)S(1)}, bf16[4,256,128]{2,1,0:T(8,128)(2,1)S(1)}) custom-call(s32[5]{0:T(128)S(1)} %stack.23.place_ref.refs_0_, bf16[256,512]{1,0:T(8,128)(2,1)} %q_ref, bf16[256,512]{1,0:T(8,128)(2,1)} %k_ref.1, bf16[256,512]{1,0:T(8,128)(2,1)} %v_ref.1, ...), custom_call_target="tpu_custom_call" | custom-call | bytes 2097152 | tf_op jit(solution)/shard_map/pallas_call | solution.py:41
  2.7 3.5 %collective-permute-start = (bf16[4,256,128]{2,1,0:T(8,128)(2,1)S(1)}, bf16[4,256,128]{2,1,0:T(8,128)(2,1)S(1)}, u32[]{:S(2)}, u32[]{:S(2)}) collective-permute-start(bf16[4,256,128]{2,1,0:T(8,128)(2,1)S(1)} %get-tuple-element.17), channel_id=1, source_target_pairs={{0,8},{8,16},{16,24},{24,0},{32,40},{40,48},{48,56},{56,32},{64,72... | collective-permute-start | bytes 786440 | tf_op jit(solution)/shard_map/ppermute | solution.py:222
  6.2 4.8 %collective-permute-start.1 = (bf16[4,256,128]{2,1,0:T(8,128)(2,1)S(1)}, bf16[4,256,128]{2,1,0:T(8,128)(2,1)S(1)}, u32[]{:S(2)}, u32[]{:S(2)}) collective-permute-start(bf16[4,256,128]{2,1,0:T(8,128)(2,1)S(1)} %get-tuple-element.18), channel_id=1, source_target_pairs={{0,16},{8,24},{16,0},{24,8},{32,48},{40,56},{48,32},{56,40},{64,80... | collective-permute-start | bytes 786440 | tf_op jit(solution)/shard_map/ppermute | solution.py:222
  11.0 0.0 slice-start
  11.0 3.3 %collective-permute-start.2 = (bf16[4,256,128]{2,1,0:T(8,128)(2,1)S(1)}, bf16[4,256,128]{2,1,0:T(8,128)(2,1)S(1)}, u32[]{:S(2)}, u32[]{:S(2)}) collective-permute-start(bf16[4,256,128]{2,1,0:T(8,128)(2,1)S(1)} %get-tuple-element.19), channel_id=1, source_target_pairs={{0,24},{8,0},{16,8},{24,16},{32,56},{40,32},{48,40},{56,48},{64,88... | collective-permute-start | bytes 786440 | tf_op jit(solution)/shard_map/ppermute | solution.py:222
  14.3 0.0 slice-done
  14.3 0.7 broadcast_in_dim.35
  15.0 15.2 %all-to-all-start = ((bf16[16,16,512]{2,1,0:T(8,128)(2,1)}), bf16[16,16,512]{2,1,0:T(8,128)(2,1)S(1)}, u32[]{:S(2)}, u32[]{:S(2)}) async-start(bf16[16,16,512]{2,1,0:T(8,128)(2,1)} %broadcast_in_dim.35), calls=%async_computation | async-start | bytes 524288 | tf_op jit(solution)/shard_map/all_to_all | solution.py:27
  30.2 0.0 collective-permute-done.refs_1_.p1_ref.refs_2_
  30.2 0.0 collective-permute-done.1.refs_2_.p2_ref.refs_3_
  30.2 0.0 collective-permute-done.2.refs_3_.p3_ref.refs_4_
  30.3 1.9 %collective-permute-start.3 = (bf16[1024,128]{1,0:T(8,128)(2,1)S(1)}, bf16[1024,128]{1,0:T(8,128)(2,1)S(1)}, u32[]{:S(2)}, u32[]{:S(2)}) collective-permute-start(bf16[1024,128]{1,0:T(8,128)(2,1)S(1)} %shard_map.77.mine_ref), channel_id=1, source_target_pairs={{0,1},{1,0},{2,3},{3,2},{4,5},{5,4},{6,7},{7,6},{8,9},{9,8},{10,11... | collective-permute-start | bytes 786440 | tf_op jit(solution)/shard_map/ppermute | solution.py:224
  32.2 1.5 %collective-permute-done.3.other_ref = bf16[1024,128]{1,0:T(8,128)(2,1)S(1)} collective-permute-done((bf16[1024,128]{1,0:T(8,128)(2,1)S(1)}, bf16[1024,128]{1,0:T(8,128)(2,1)S(1)}, u32[]{:S(2)}, u32[]{:S(2)}) %collective-permute-start.3) | collective-permute-done | bytes 262176 | tf_op jit(solution)/shard_map/ppermute | solution.py:224
  33.7 0.6 shard_map.78.a0_ref
  34.4 0.0 slice-start.1
  34.4 2.6 %collective-permute-start.6 = (bf16[1024,256]{1,0:T(8,128)(2,1)S(1)}, bf16[1024,256]{1,0:T(8,128)(2,1)S(1)}, u32[]{:S(2)}, u32[]{:S(2)}) collective-permute-start(bf16[1024,256]{1,0:T(8,128)(2,1)S(1)} %shard_map.78.a0_ref), channel_id=1, source_target_pairs={{0,6},{1,7},{2,0},{3,1},{4,2},{5,3},{6,4},{7,5},{8,14},{9,15},{10,... | collective-permute-start | bytes 1572872 | tf_op jit(solution)/shard_map/ppermute | solution.py:228
  37.0 4.3 %collective-permute-start.5 = (bf16[1024,256]{1,0:T(8,128)(2,1)S(1)}, bf16[1024,256]{1,0:T(8,128)(2,1)}, u32[]{:S(2)}, u32[]{:S(2)}) collective-permute-start(bf16[1024,256]{1,0:T(8,128)(2,1)S(1)} %shard_map.78.a0_ref), channel_id=1, source_target_pairs={{0,4},{1,5},{2,6},{3,7},{4,0},{5,1},{6,2},{7,3},{8,12},{9,13},{10,... | collective-permute-start | bytes 1572872 | tf_op jit(solution)/shard_map/ppermute | solution.py:228
  41.3 3.7 %collective-permute-start.4 = (bf16[1024,256]{1,0:T(8,128)(2,1)S(1)}, bf16[1024,256]{1,0:T(8,128)(2,1)}, u32[]{:S(2)}, u32[]{:S(2)}) collective-permute-start(bf16[1024,256]{1,0:T(8,128)(2,1)S(1)} %shard_map.78.a0_ref), channel_id=1, source_target_pairs={{0,2},{1,3},{2,4},{3,5},{4,6},{5,7},{6,0},{7,1},{8,10},{9,11},{10,... | collective-permute-start | bytes 1572872 | tf_op jit(solution)/shard_map/ppermute | solution.py:228
  45.0 0.0 slice-done.1
  45.0 34.4 %all-gather = bf16[768,512]{1,0:T(8,128)(2,1)S(1)} all-gather(bf16[48,512]{1,0:T(8,128)(2,1)S(1)} %slice-done.1), channel_id=2, replica_groups={{0,32,64,96,128,160,192,224,256,288,320,352,384,416,448,480},{8,40,72,1..., dimensions={0}, use_global_device_ids=true | all-gather | bytes 835584 | tf_op jit(solution)/shard_map/all_gather | solution.py:232
  79.5 0.0 all-to-all-done.last_ref
  79.5 0.0 collective-permute-done.6.a3_ref
  79.5 0.0 collective-permute-done.5.a2_ref
  79.5 0.0 collective-permute-done.4.a1_ref
  79.5 2.5 %shard_map.79 = bf16[4,1024,128]{2,1,0:T(8,128)(2,1)S(1)} custom-call(s32[5]{0:T(128)S(1)} %stack.23.place_ref.refs_0_, bf16[1024,256]{1,0:T(8,128)(2,1)S(1)} %shard_map.78.a0_ref, bf16[1024,256]{1,0:T(8,128)(2,1)} %collective-permute-done.4.a1_ref, bf16[1024,256]{1,0:T(8,128)(2,1)} %collective-permute-done.5.a2_ref, ...), custom_call_target="tpu_custom_call" | custom-call | flops 1073741824 | bytes 4194304 | tf_op jit(solution)/shard_map/pallas_call | solution.py:41
  82.0 13.3 %all_to_all.25.part_ref = bf16[4,1024,128]{2,1,0:T(8,128)(2,1)S(1)} all-to-all(bf16[4,1024,128]{2,1,0:T(8,128)(2,1)S(1)} %shard_map.79), channel_id=1, replica_groups={{0,8,16,24},{32,40,48,56},{64,72,80,88},{96,104,112,120},{128,136,144,1..., dimensions={0} | all-to-all | bytes 2097152 | tf_op jit(solution)/shard_map/all_to_all | solution.py:27
  95.4 0.9 shard_map.80
  96.3 10.2 %all_to_all.26.refs_7_ = bf16[4,2,128,128]{3,2,1,0:T(8,128)(2,1)S(1)} all-to-all(bf16[4,2,128,128]{3,2,1,0:T(8,128)(2,1)S(1)} %get-tuple-element.23), channel_id=1, replica_groups={{0,32,64,96},{8,40,72,104},{16,48,80,112},{24,56,88,120},{128,160,192,2..., dimensions={0} | all-to-all | bytes 524288 | tf_op jit(solution)/shard_map/all_to_all | solution.py:27
  106.5 0.1 broadcast_select_fusion
  106.6 21.5 %all_to_all.27.refs_8_ = bf16[4,128,128]{2,1,0:T(8,128)(2,1)S(1)} all-to-all(bf16[4,128,128]{2,1,0:T(8,128)(2,1)S(1)} %broadcast_select_fusion), channel_id=1, replica_groups={{0,128,256,384},{8,136,264,392},{16,144,272,400},{24,152,280,408},{32,1..., dimensions={0} | all-to-all | bytes 262144 | tf_op jit(solution)/shard_map/all_to_all | solution.py:27
  128.1 1.8 %shard_map.81 = bf16[4,3,256,128]{3,2,1,0:T(8,128)(2,1)S(1)} custom-call(s32[5]{0:T(128)S(1)} %stack.23.place_ref.refs_0_, bf16[4,256,128]{2,1,0:T(8,128)(2,1)S(1)} %get-tuple-element.16.refs_0_.p0_ref.refs_1_, bf16[4,256,128]{2,1,0:T(8,128)(2,1)S(1)} %collective-permute-done.refs_1_.p1_ref.refs_2_, ...), custom_call_target="tpu_custom_call" | custom-call | flops 536870912 | bytes 3145728 | tf_op jit(solution)/shard_map/pallas_call | solution.py:41
  129.9 11.9 %all_to_all.28.in_ref = bf16[4,3,256,128]{3,2,1,0:T(8,128)(2,1)S(1)} all-to-all(bf16[4,3,256,128]{3,2,1,0:T(8,128)(2,1)S(1)} %shard_map.81), channel_id=1, replica_groups={{0,8,16,24},{32,40,48,56},{64,72,80,88},{96,104,112,120},{128,136,144,1..., dimensions={0} | all-to-all | bytes 1572864 | tf_op jit(solution)/shard_map/all_to_all | solution.py:27
  141.8 1.0 shard_map.82
  (4 shorter events, 0.1 us)
Async XLA Ops:
  2.7 27.5 %collective-permute-start = (bf16[4,256,128]{2,1,0:T(8,128)(2,1)S(1)}, bf16[4,256,128]{2,1,0:T(8,128)(2,1)S(1)}, u32[]{:S(2)}, u32[]{:S(2)}) collective-permute-start(bf16[4,256,128]{2,1,0:T(8,128)(2,1)S(1)} %get-tuple-element.17), channel_id=1, source_target_pairs={{0,8},{8,16},{16,24},{24,0},{32,40},{40,48},{48,56},{56,32},{64,72... | collective-permute-start | bytes 786440 | tf_op jit(solution)/shard_map/ppermute | solution.py:222
  6.2 24.1 %collective-permute-start.1 = (bf16[4,256,128]{2,1,0:T(8,128)(2,1)S(1)}, bf16[4,256,128]{2,1,0:T(8,128)(2,1)S(1)}, u32[]{:S(2)}, u32[]{:S(2)}) collective-permute-start(bf16[4,256,128]{2,1,0:T(8,128)(2,1)S(1)} %get-tuple-element.18), channel_id=1, source_target_pairs={{0,16},{8,24},{16,0},{24,8},{32,48},{40,56},{48,32},{56,40},{64,80... | collective-permute-start | bytes 786440 | tf_op jit(solution)/shard_map/ppermute | solution.py:222
  11.0 3.3 %slice-start = ((bf16[64,512]{1,0:T(8,128)(2,1)}), bf16[16,512]{1,0:T(8,128)(2,1)S(1)}, s32[]{:S(2)}) async-start(bf16[64,512]{1,0:T(8,128)(2,1)} %param.9), calls=%async_computation.5 | async-start | bytes 32768 | tf_op jit(solution)/shard_map/slice | solution.py:233
  11.0 19.2 %collective-permute-start.2 = (bf16[4,256,128]{2,1,0:T(8,128)(2,1)S(1)}, bf16[4,256,128]{2,1,0:T(8,128)(2,1)S(1)}, u32[]{:S(2)}, u32[]{:S(2)}) collective-permute-start(bf16[4,256,128]{2,1,0:T(8,128)(2,1)S(1)} %get-tuple-element.19), channel_id=1, source_target_pairs={{0,24},{8,0},{16,8},{24,16},{32,56},{40,32},{48,40},{56,48},{64,88... | collective-permute-start | bytes 786440 | tf_op jit(solution)/shard_map/ppermute | solution.py:222
  15.0 64.4 %all-to-all-start = ((bf16[16,16,512]{2,1,0:T(8,128)(2,1)}), bf16[16,16,512]{2,1,0:T(8,128)(2,1)S(1)}, u32[]{:S(2)}, u32[]{:S(2)}) async-start(bf16[16,16,512]{2,1,0:T(8,128)(2,1)} %broadcast_in_dim.35), calls=%async_computation | async-start | bytes 524288 | tf_op jit(solution)/shard_map/all_to_all | solution.py:27
  30.3 3.4 %collective-permute-start.3 = (bf16[1024,128]{1,0:T(8,128)(2,1)S(1)}, bf16[1024,128]{1,0:T(8,128)(2,1)S(1)}, u32[]{:S(2)}, u32[]{:S(2)}) collective-permute-start(bf16[1024,128]{1,0:T(8,128)(2,1)S(1)} %shard_map.77.mine_ref), channel_id=1, source_target_pairs={{0,1},{1,0},{2,3},{3,2},{4,5},{5,4},{6,7},{7,6},{8,9},{9,8},{10,11... | collective-permute-start | bytes 786440 | tf_op jit(solution)/shard_map/ppermute | solution.py:224
  34.4 10.7 %slice-start.1 = ((bf16[64,512]{1,0:T(8,128)(2,1)}), bf16[48,512]{1,0:T(8,128)(2,1)S(1)}, s32[]{:S(2)}) async-start(bf16[64,512]{1,0:T(8,128)(2,1)} %param.9), calls=%async_computation.6 | async-start | bytes 98304 | tf_op jit(solution)/shard_map/slice | solution.py:232
  34.4 45.1 %collective-permute-start.6 = (bf16[1024,256]{1,0:T(8,128)(2,1)S(1)}, bf16[1024,256]{1,0:T(8,128)(2,1)S(1)}, u32[]{:S(2)}, u32[]{:S(2)}) collective-permute-start(bf16[1024,256]{1,0:T(8,128)(2,1)S(1)} %shard_map.78.a0_ref), channel_id=1, source_target_pairs={{0,6},{1,7},{2,0},{3,1},{4,2},{5,3},{6,4},{7,5},{8,14},{9,15},{10,... | collective-permute-start | bytes 1572872 | tf_op jit(solution)/shard_map/ppermute | solution.py:228
  37.0 42.5 %collective-permute-start.5 = (bf16[1024,256]{1,0:T(8,128)(2,1)S(1)}, bf16[1024,256]{1,0:T(8,128)(2,1)}, u32[]{:S(2)}, u32[]{:S(2)}) collective-permute-start(bf16[1024,256]{1,0:T(8,128)(2,1)S(1)} %shard_map.78.a0_ref), channel_id=1, source_target_pairs={{0,4},{1,5},{2,6},{3,7},{4,0},{5,1},{6,2},{7,3},{8,12},{9,13},{10,... | collective-permute-start | bytes 1572872 | tf_op jit(solution)/shard_map/ppermute | solution.py:228
  41.3 38.2 %collective-permute-start.4 = (bf16[1024,256]{1,0:T(8,128)(2,1)S(1)}, bf16[1024,256]{1,0:T(8,128)(2,1)}, u32[]{:S(2)}, u32[]{:S(2)}) collective-permute-start(bf16[1024,256]{1,0:T(8,128)(2,1)S(1)} %shard_map.78.a0_ref), channel_id=1, source_target_pairs={{0,2},{1,3},{2,4},{3,5},{4,6},{5,7},{6,0},{7,1},{8,10},{9,11},{10,... | collective-permute-start | bytes 1572872 | tf_op jit(solution)/shard_map/ppermute | solution.py:228

commit v4 on v3

--- a/solution.py
+++ b/solution.py
@@ -9,6 +9,7 @@
 
 DH = 128
 NY = 4
+NX = 4
 ZG = 4
 F32 = jnp.float32
 BF16 = jnp.bfloat16
@@ -27,10 +28,10 @@
     return lax.all_to_all(pieces, "ctx", 0, 0, axis_index_groups=group)
 
 
-def call(kernel, out_shape, flops, size, smem=(), hbm=(), scratch=(), out_hbm=False):
+def call(kernel, out_shape, flops, size, smem=(), hbm=(), anywhere=(), scratch=(), out_hbm=False):
     def run(*operands):
         specs = [
-            pl.BlockSpec(memory_space=pltpu.SMEM if i in smem else pltpu.HBM if i in hbm else pltpu.VMEM)
+            pl.BlockSpec(memory_space=pltpu.SMEM if i in smem else pltpu.HBM if i in hbm else pl.ANY if i in anywhere else pltpu.VMEM)
             for i in range(len(operands))
         ]
         operands = [
@@ -44,7 +45,7 @@
             in_specs=specs,
             out_specs=out_specs,
             scratch_shapes=scratch,
-            compiler_params=pltpu.CompilerParams(vmem_limit_bytes=40 * 1024 * 1024),
+            compiler_params=pltpu.CompilerParams(vmem_limit_bytes=16 * 1024 * 1024),
             cost_estimate=pl.CostEstimate(flops=flops, bytes_accessed=size, transcendentals=0),
         )(*operands)
 
@@ -92,36 +93,58 @@
         refs[NY][d * step : (d + 1) * step, :] = refs[d][3]
 
 
-def pair_kernel(place_ref, mine_ref, other_ref, out_ref):
-    first = place_ref[4] == 0
-    mine, other = mine_ref[...], other_ref[...]
-    out_ref[:, :DH] = jnp.where(first, mine, other)
-    out_ref[:, DH:] = jnp.where(first, other, mine)
-
-
-def product_kernel(place_ref, a0_ref, a1_ref, a2_ref, a3_ref, main_ref, last_ref, out_ref, weight):
-    tokens, depth = a0_ref.shape
+def copies_kernel(w_ref, out_ref, held, sem, sems):
+    load = pltpu.make_async_copy(w_ref, held, sem)
+    load.start()
+    load.wait()
+    moves = []
+    for z in range(out_ref.shape[0]):
+        move = pltpu.make_async_copy(held, out_ref.at[z], sems.at[z])
+        move.start()
+        moves.append(move)
+    for move in moves:
+        move.wait()
+
+
+def product_kernel(place_ref, *refs):
+    weight, early_ref, out_ref, held, sems = refs[2 * NX :]
+    tokens, depth = refs[0].shape
     step = tokens // NY
-    held = (a0_ref, a1_ref, a2_ref, a3_ref)
-    chips = len(held)
-    main, last = main_ref.shape[1], last_ref.shape[1]
-    for z in range(main_ref.shape[0]):
-        low = z * (main + last)
-        weight[low : low + main, :] = main_ref[z]
-        weight[low + main : low + main + last, :] = last_ref[z]
+    core = place_ref[4]
+    loads = []
+    for t in range(NY):
+        tile = pl.ds(t * step, step)
+        for i in range(2 * NX):
+            lanes = pl.ds(i // NX * depth, depth)
+            load = pltpu.make_async_copy(refs[i].at[tile, :], held.at[i % NX, tile, lanes], sems.at[t, i])
+            load.start()
+            loads.append(load)
     for t in range(NY):
         part = jnp.zeros((step, weight.shape[1]), F32)
-        for d, ref in enumerate(held):
-            chip = lax.rem(place_ref[3] + (chips - d), chips)
-            start = pl.multiple_of(chip * depth, depth)
-            part = part + dot(ref[t * step : (t + 1) * step, :], weight[pl.ds(start, depth), :], 1, 0)
+        for load in loads[t * 2 * NX : (t + 1) * 2 * NX]:
+            load.wait()
+        for d in range(NX):
+            chip = lax.rem(place_ref[3] + (NX - d), NX)
+            own = pl.multiple_of((chip * 2 + core) * depth, depth)
+            far = pl.multiple_of((chip * 2 + 1 - core) * depth, depth)
+            rows = jnp.concatenate([weight[pl.ds(own, depth), :], weight[pl.ds(far, depth), :]], axis=0)
+            part = part + dot(held[d, t * step : (t + 1) * step, :], rows, 1, 0)
         part = part.astype(BF16)
         rows = pl.ds(pl.multiple_of(block_of(place_ref, t) * step, step), step)
         for h in range(NY):
             out_ref[h, rows, :] = part[:, h * DH : (h + 1) * DH]
 
 
-def state_kernel(place_ref, p0_ref, p1_ref, p2_ref, p3_ref, part_ref, grad_ref, states_ref, copies_ref):
+def key_kernel(p0_ref, p1_ref, p2_ref, p3_ref, states_ref, scores_ref):
+    step = p0_ref.shape[1]
+    row = lax.broadcasted_iota(jnp.int32, (step, step), 0)
+    col = lax.broadcasted_iota(jnp.int32, (step, step), 1)
+    for d, ref in enumerate((p0_ref, p1_ref, p2_ref, p3_ref)):
+        states_ref[d] = dot(ref[1], ref[2], 0, 0)
+        scores_ref[d] = jnp.where(row <= col, dot(ref[1], ref[0], 1, 1), 0.0).astype(BF16)
+
+
+def state_kernel(place_ref, p0_ref, p1_ref, p2_ref, p3_ref, part_ref, key_ref, grad_ref, query_ref, copies_ref):
     step = p0_ref.shape[1]
     total_k = jnp.zeros((DH, DH), F32)
     total_q = jnp.zeros((DH, DH), F32)
@@ -132,18 +155,16 @@
             grad = grad + part_ref[y, rows, :].astype(F32)
         grad = grad.astype(BF16)
         grad_ref[d] = grad
-        key_state = dot(ref[1], ref[2], 0, 0)
         query_state = dot(ref[0], grad, 0, 0)
-        states_ref[0, d] = key_state
-        states_ref[1, d] = query_state
-        total_k = total_k + key_state
+        query_ref[d] = query_state
+        total_k = total_k + key_ref[d]
         total_q = total_q + query_state
     for i in range(ZG):
         copies_ref[i, 0] = total_k.astype(BF16)
         copies_ref[i, 1] = total_q.astype(BF16)
 
 
-def final_kernel(factor, place_ref, p0_ref, p1_ref, p2_ref, p3_ref, grad_ref, states_ref, near_ref, far_ref, out_ref):
+def final_kernel(factor, place_ref, p0_ref, p1_ref, p2_ref, p3_ref, grad_ref, key_ref, query_ref, scores_ref, near_ref, far_ref, out_ref):
     step = p0_ref.shape[1]
     inner, outer = place_ref[0], place_ref[1]
     prefix = jnp.zeros((DH, DH), F32)
@@ -167,13 +188,13 @@
         for e in range(NY):
             if e != d:
                 other = block_of(place_ref, e)
-                before = before + jnp.where(other < block, states_ref[0, e], 0.0)
-                after = after + jnp.where(other > block, states_ref[1, e], 0.0)
+                before = before + jnp.where(other < block, key_ref[e], 0.0)
+                after = after + jnp.where(other > block, query_ref[e], 0.0)
         before = before.astype(BF16)
         after = after.astype(BF16)
         scores_grad = jnp.where(lower, dot(grad, value, 1, 1), 0.0).astype(BF16)
         scores_grad_t = jnp.where(upper, dot(value, grad, 1, 1), 0.0).astype(BF16)
-        scores_t = jnp.where(upper, dot(key, query, 1, 1), 0.0).astype(BF16)
+        scores_t = scores_ref[d]
         grad_q = dot(scores_grad, key, 1, 0) + dot(grad, before, 1, 1)
         grad_k = dot(scores_grad_t, query, 1, 0) + dot(value, after, 1, 1)
         grad_v = dot(scores_t, grad, 1, 0) + dot(key, after, 1, 0)
@@ -201,8 +222,20 @@
     z = here // NY
     place = jnp.stack([z % ZG, z // ZG, here % NY, at // 2, at % 2]).astype(jnp.int32)
     earlier = jnp.arange(nz // ZG, dtype=jnp.int32) < place[1]
-    queries, place, earlier = lax.optimization_barrier((queries, place, earlier))
-
+    grad_out, place, earlier = lax.optimization_barrier((grad_out, place, earlier))
+
+    copies = call(
+        copies_kernel,
+        pltpu.HBM((nz,) + out_weight.shape, BF16),
+        0,
+        2 * depth * width,
+        hbm=(0,),
+        out_hbm=True,
+        scratch=[pltpu.VMEM(out_weight.shape, BF16), pltpu.SemaphoreType.DMA, pltpu.SemaphoreType.DMA((nz,))],
+    )(out_weight)
+    weight = exchange(copies, z_line).reshape(depth, width)
+    grad_out, copies = lax.optimization_barrier((grad_out, copies))
+    turns = {d: [(i, i // NY * NY + (i + d) % NY) for i in range(ctx)] for d in (1, 3, 2)}
     packed = call(
         pack_kernel,
         [shape((4, step, DH))] * NY,
@@ -217,36 +250,38 @@
         ],
     )(place, queries, keys, values, grad_out)
     packed = list(packed)
-    for d in (1, 3, 2):
-        turn = [(i, i // NY * NY + (i + d) % NY) for i in range(ctx)]
+    for d, turn in turns.items():
         packed[d] = lax.ppermute(packed[d], "ctx", turn)
     mine = call(mine_kernel, shape((tokens, DH)), 0, 4 * tokens * DH)(*packed)
-    other = lax.ppermute(mine, "tp", [(t, t ^ 1) for t in range(tp)])
-    pair = call(pair_kernel, shape((tokens, 2 * DH)), 0, 8 * tokens * DH, smem=(0,))(place, mine, other)
-    shares = [pair]
-    for d in range(1, tp // 2):
-        shares.append(lax.ppermute(pair, "tp", [(t, (t + 2 * d) % tp) for t in range(tp)]))
-    shard = out_weight.shape[0]
-    main = shard - shard // 4
-    kept, pair_seen = lax.optimization_barrier((out_weight, pair))
-    weight = lax.all_gather(kept[:main], "ctx", axis_index_groups=z_line)
-    last = exchange(jnp.broadcast_to(out_weight[None, main:], (nz, shard - main, width)), z_line)
+    shares = [mine]
+    for d in range(1, NX):
+        shares.append(lax.ppermute(mine, "tp", [(t, (t + 2 * d) % tp) for t in range(tp)]))
+    swap = [(t, t ^ 1) for t in range(tp)]
+    shares = shares + [lax.ppermute(share, "tp", swap) for share in shares]
+    key_states, scores = call(
+        key_kernel,
+        [shape((NY, DH, DH), F32), shape((NY, step, step))],
+        4 * tokens * DH * (DH + step),
+        2 * 1024 * 1024,
+    )(*packed)
     parts = call(
         product_kernel,
         shape((NY, tokens, DH)),
         2 * tokens * depth * width,
         4 * 1024 * 1024,
         smem=(0,),
-        scratch=[pltpu.VMEM((depth, width), BF16)],
-    )(place, *shares, weight, last)
+        hbm=range(1, 2 * NX + 1),
+        anywhere=(2 * NX + 2,),
+        scratch=[pltpu.VMEM((NX, tokens, 2 * DH), BF16), pltpu.SemaphoreType.DMA((NY, 2 * NX))],
+    )(place, *shares, weight, scores)
     parts = exchange(parts, y_line)
-    grads, states, copies = call(
+    grads, query_states, copies = call(
         state_kernel,
-        [shape((NY, step, DH)), shape((2, NY, DH, DH), F32), shape((ZG, 2, DH, DH))],
+        [shape((NY, step, DH)), shape((NY, DH, DH), F32), shape((ZG, 2, DH, DH))],
         4 * tokens * DH * DH,
         3 * 1024 * 1024,
         smem=(0,),
-    )(place, *packed, parts)
+    )(place, *packed, parts, key_states)
     near = exchange(copies, z_near)
     total = jnp.sum(near.astype(F32), axis=0).astype(BF16)
     far = exchange(jnp.where(earlier[:, None, None], total[1][None], total[0][None]), z_far)
@@ -256,7 +291,7 @@
         8 * 2 * tokens * step * DH,
         3 * 1024 * 1024,
         smem=(0,),
-    )(place, *packed, grads, states, near, far)
+    )(place, *packed, grads, key_states, query_states, scores, near, far)
     result = exchange(result, y_line)
     out = shape((step, width))
     return tuple(call(unpack_kernel, [out, out, out], 0, 6 * step * width * 2)(result))

time: 143 us -> 139 us (0.972)
  the two profiles are of different devices: /device:TPU:2 before, /device:TPU:8 now
where the time goes in v4:
time: 139 us; the launch traced here: 138 us
  blocking collectives  62.9 us (45%)
  starting transfers between devices  44.2 us (32%)
  waiting for transfers between devices  16.9 us (12%)
  Pallas kernels  11.5 us (8%)
  local copies, waits for them, and re-layouts  1.58 us (1%)
    all_to_all x4, blocking collectives, exchange(): return lax.all_to_all(pieces, 'ctx', 0, 0, axis_index_groups=group)  62.9 us
    all_to_all x1, starting transfers between devices, exchange(): return lax.all_to_all(pieces, 'ctx', 0, 0, axis_index_groups=group)  15.2 us
    pallas_call x8, Pallas kernels, run(): pl.pallas_call(kernel, out_shape=out_shape, in_specs=specs, out_specs=out...  11.5 us
    ppermute x3, starting transfers between devices, local(): packed[d] = lax.ppermute(packed[d], 'ctx', turn)  10.7 us
    ppermute x3, starting transfers between devices, local(): lax.ppermute(mine, 'tp', [(t, (t + 2 * d) % tp) for t in range(tp)])  10.2 us
    ppermute x3, waiting for transfers between devices, local(): packed[d] = lax.ppermute(packed[d], 'ctx', turn)  9.31 us
    ppermute x4, starting transfers between devices, local(): shares = shares + [lax.ppermute(share, 'tp', swap) for share in shares]  8.15 us
    ppermute x3, waiting for transfers between devices, local(): lax.ppermute(mine, 'tp', [(t, (t + 2 * d) % tp) for t in range(tp)])  5.16 us
  transfers between devices with their start and end apart: 11, of which 5 were waited for; matrix products, arithmetic and copies ran while one was open for 0% of the time, Pallas kernels for 2%

profile of v4, /device:TPU:8, one launch (start us, length us, event | category | flops | bytes accessed | tf_op | source)
XLA Modules:
  0.0 138.2 jit_solution(6833094891220181129)
XLA Ops:
  0.6 2.0 %shard_map.76 = bf16[16,64,512]{2,1,0:T(8,128)(2,1)} custom-call(bf16[64,512]{1,0:T(8,128)(2,1)} %w_ref.1), custom_call_target="tpu_custom_call" | custom-call | bytes 1048576 | tf_op jit(solution)/shard_map/pallas_call | solution.py:42
  2.6 15.2 %all-to-all-start = ((bf16[16,64,512]{2,1,0:T(8,128)(2,1)}), bf16[16,64,512]{2,1,0:T(8,128)(2,1)S(1)}, u32[]{:S(2)}, u32[]{:S(2)}) async-start(bf16[16,64,512]{2,1,0:T(8,128)(2,1)} %shard_map.76), calls=%async_computation | async-start | bytes 2097152 | tf_op jit(solution)/shard_map/all_to_all | solution.py:28
  17.9 0.1 stack.23.place_ref.refs_0_
  18.0 1.9 %shard_map.77 = (bf16[4,256,128]{2,1,0:T(8,128)(2,1)S(1)}, bf16[4,256,128]{2,1,0:T(8,128)(2,1)S(1)}, bf16[4,256,128]{2,1,0:T(8,128)(2,1)S(1)}, bf16[4,256,128]{2,1,0:T(8,128)(2,1)S(1)}) custom-call(s32[5]{0:T(128)S(1)} %stack.23.place_ref.refs_0_, bf16[256,512]{1,0:T(8,128)(2,1)} %q_ref.1, bf16[256,512]{1,0:T(8,128)(2,1)} %k_ref.1, bf16[256,512]{1,0:T(8,128)(2,1)} %v_ref.1, ...), custom_call_target="tpu_custom_call" | custom-call | bytes 2097152 | tf_op jit(solution)/shard_map/pallas_call | solution.py:42
  19.9 3.5 %collective-permute-start = (bf16[4,256,128]{2,1,0:T(8,128)(2,1)S(1)}, bf16[4,256,128]{2,1,0:T(8,128)(2,1)S(1)}, u32[]{:S(2)}, u32[]{:S(2)}) collective-permute-start(bf16[4,256,128]{2,1,0:T(8,128)(2,1)S(1)} %get-tuple-element.20), channel_id=1, source_target_pairs={{0,8},{8,16},{16,24},{24,0},{32,40},{40,48},{48,56},{56,32},{64,72... | collective-permute-start | bytes 786440 | tf_op jit(solution)/shard_map/ppermute | solution.py:254
  23.4 2.8 %collective-permute-start.1 = (bf16[4,256,128]{2,1,0:T(8,128)(2,1)S(1)}, bf16[4,256,128]{2,1,0:T(8,128)(2,1)S(1)}, u32[]{:S(2)}, u32[]{:S(2)}) collective-permute-start(bf16[4,256,128]{2,1,0:T(8,128)(2,1)S(1)} %get-tuple-element.21), channel_id=1, source_target_pairs={{0,16},{8,24},{16,0},{24,8},{32,48},{40,56},{48,32},{56,40},{64,80... | collective-permute-start | bytes 786440 | tf_op jit(solution)/shard_map/ppermute | solution.py:254
  26.2 4.3 %collective-permute-start.2 = (bf16[4,256,128]{2,1,0:T(8,128)(2,1)S(1)}, bf16[4,256,128]{2,1,0:T(8,128)(2,1)S(1)}, u32[]{:S(2)}, u32[]{:S(2)}) collective-permute-start(bf16[4,256,128]{2,1,0:T(8,128)(2,1)S(1)} %get-tuple-element.22), channel_id=1, source_target_pairs={{0,24},{8,0},{16,8},{24,16},{32,56},{40,32},{48,40},{56,48},{64,88... | collective-permute-start | bytes 786440 | tf_op jit(solution)/shard_map/ppermute | solution.py:254
  30.5 0.0 collective-permute-done.refs_1_.p1_ref.refs_2_
  30.6 5.5 %collective-permute-done.1.refs_2_.p2_ref.refs_3_ = bf16[4,256,128]{2,1,0:T(8,128)(2,1)S(1)} collective-permute-done((bf16[4,256,128]{2,1,0:T(8,128)(2,1)S(1)}, bf16[4,256,128]{2,1,0:T(8,128)(2,1)S(1)}, u32[]{:S(2)}, u32[]{:S(2)}) %collective-permute-start.1) | collective-permute-done | bytes 262176 | tf_op jit(solution)/shard_map/ppermute | solution.py:254
  36.1 3.8 %collective-permute-done.2.refs_3_.p3_ref.refs_4_ = bf16[4,256,128]{2,1,0:T(8,128)(2,1)S(1)} collective-permute-done((bf16[4,256,128]{2,1,0:T(8,128)(2,1)S(1)}, bf16[4,256,128]{2,1,0:T(8,128)(2,1)S(1)}, u32[]{:S(2)}, u32[]{:S(2)}) %collective-permute-start.2) | collective-permute-done | bytes 262176 | tf_op jit(solution)/shard_map/ppermute | solution.py:254
  39.9 0.0 copy-start
  39.9 4.7 %collective-permute-start.5 = (bf16[1024,128]{1,0:T(8,128)(2,1)S(1)}, bf16[1024,128]{1,0:T(8,128)(2,1)S(1)}, u32[]{:S(2)}, u32[]{:S(2)}) collective-permute-start(bf16[1024,128]{1,0:T(8,128)(2,1)S(1)} %shard_map.78.refs_0_), channel_id=1, source_target_pairs={{0,6},{1,7},{2,0},{3,1},{4,2},{5,3},{6,4},{7,5},{8,14},{9,15},{10,... | collective-permute-start | bytes 786440 | tf_op jit(solution)/shard_map/ppermute | solution.py:258
  44.6 2.7 %collective-permute-start.4 = (bf16[1024,128]{1,0:T(8,128)(2,1)S(1)}, bf16[1024,128]{1,0:T(8,128)(2,1)S(1)}, u32[]{:S(2)}, u32[]{:S(2)}) collective-permute-start(bf16[1024,128]{1,0:T(8,128)(2,1)S(1)} %shard_map.78.refs_0_), channel_id=1, source_target_pairs={{0,4},{1,5},{2,6},{3,7},{4,0},{5,1},{6,2},{7,3},{8,12},{9,13},{10,... | collective-permute-start | bytes 786440 | tf_op jit(solution)/shard_map/ppermute | solution.py:258
  47.3 2.8 %collective-permute-start.3 = (bf16[1024,128]{1,0:T(8,128)(2,1)S(1)}, bf16[1024,128]{1,0:T(8,128)(2,1)S(1)}, u32[]{:S(2)}, u32[]{:S(2)}) collective-permute-start(bf16[1024,128]{1,0:T(8,128)(2,1)S(1)} %shard_map.78.refs_0_), channel_id=1, source_target_pairs={{0,2},{1,3},{2,4},{3,5},{4,6},{5,7},{6,0},{7,1},{8,10},{9,11},{10,... | collective-permute-start | bytes 786440 | tf_op jit(solution)/shard_map/ppermute | solution.py:258
  50.1 1.9 %collective-permute-start.6 = (bf16[1024,128]{1,0:T(8,128)(2,1)S(1)}, bf16[1024,128]{1,0:T(8,128)(2,1)S(1)}, u32[]{:S(2)}, u32[]{:S(2)}) collective-permute-start(bf16[1024,128]{1,0:T(8,128)(2,1)S(1)} %shard_map.78.refs_0_), channel_id=1, source_target_pairs={{0,1},{1,0},{2,3},{3,2},{4,5},{5,4},{6,7},{7,6},{8,9},{9,8},{10,11... | collective-permute-start | bytes 786440 | tf_op jit(solution)/shard_map/ppermute | solution.py:260
  52.0 3.9 %collective-permute-done.5.refs_3_ = bf16[1024,128]{1,0:T(8,128)(2,1)S(1)} collective-permute-done((bf16[1024,128]{1,0:T(8,128)(2,1)S(1)}, bf16[1024,128]{1,0:T(8,128)(2,1)S(1)}, u32[]{:S(2)}, u32[]{:S(2)}) %collective-permute-start.5) | collective-permute-done | bytes 262176 | tf_op jit(solution)/shard_map/ppermute | solution.py:258
  55.9 0.0 copy-start.1
  56.0 1.9 %collective-permute-start.9 = (bf16[1024,128]{1,0:T(8,128)(2,1)S(1)}, bf16[1024,128]{1,0:T(8,128)(2,1)S(1)}, u32[]{:S(2)}, u32[]{:S(2)}) collective-permute-start(bf16[1024,128]{1,0:T(8,128)(2,1)S(1)} %collective-permute-done.5.refs_3_), channel_id=1, source_target_pairs={{0,1},{1,0},{2,3},{3,2},{4,5},{5,4},{6,7},{7,6},{8,9},{9,8},{10,11... | collective-permute-start | bytes 786440 | tf_op jit(solution)/shard_map/ppermute | solution.py:260
  57.9 0.0 collective-permute-done.4.refs_2_
  57.9 0.0 copy-start.2
  57.9 2.4 %collective-permute-start.8 = (bf16[1024,128]{1,0:T(8,128)(2,1)S(1)}, bf16[1024,128]{1,0:T(8,128)(2,1)S(1)}, u32[]{:S(2)}, u32[]{:S(2)}) collective-permute-start(bf16[1024,128]{1,0:T(8,128)(2,1)S(1)} %collective-permute-done.4.refs_2_), channel_id=1, source_target_pairs={{0,1},{1,0},{2,3},{3,2},{4,5},{5,4},{6,7},{7,6},{8,9},{9,8},{10,11... | collective-permute-start | bytes 786440 | tf_op jit(solution)/shard_map/ppermute | solution.py:260
  60.3 1.2 collective-permute-done.3.refs_1_
  61.5 0.0 copy-start.3
  61.5 1.9 %collective-permute-start.7 = (bf16[1024,128]{1,0:T(8,128)(2,1)S(1)}, bf16[1024,128]{1,0:T(8,128)(2,1)}, u32[]{:S(2)}, u32[]{:S(2)}) collective-permute-start(bf16[1024,128]{1,0:T(8,128)(2,1)S(1)} %collective-permute-done.3.refs_1_), channel_id=1, source_target_pairs={{0,1},{1,0},{2,3},{3,2},{4,5},{5,4},{6,7},{7,6},{8,9},{9,8},{10,11... | collective-permute-start | bytes 786440 | tf_op jit(solution)/shard_map/ppermute | solution.py:260
  63.5 0.4 shard_map.79
  63.9 0.0 copy-done
  63.9 0.0 copy-done.1
  63.9 0.0 copy-done.2
  63.9 0.0 copy-done.3
  63.9 0.0 collective-permute-done.6.refs_4_
  63.9 0.0 copy-start.4
  63.9 0.0 collective-permute-done.9.refs_7_
  63.9 0.0 copy-start.5
  64.0 0.0 collective-permute-done.8.refs_6_
  64.0 0.7 copy-done.4
  64.6 0.1 copy-done.5
  64.7 0.0 copy-start.6
  64.7 0.7 copy-done.6
  65.4 0.0 collective-permute-done.7.refs_5_
  65.4 2.4 %all-to-all-done = bf16[16,64,512]{2,1,0:T(8,128)(2,1)S(1)} async-done(((bf16[16,64,512]{2,1,0:T(8,128)(2,1)}), bf16[16,64,512]{2,1,0:T(8,128)(2,1)S(1)}, u32[]{:S(2)}, u32[]{:S(2)}) %all-to-all-start) | async-done | bytes 1048608 | tf_op jit(solution)/shard_map/all_to_all | solution.py:28
  67.8 3.7 %shard_map.80 = bf16[4,1024,128]{2,1,0:T(8,128)(2,1)S(1)} custom-call(s32[5]{0:T(128)S(1)} %stack.23.place_ref.refs_0_, bf16[1024,128]{1,0:T(8,128)(2,1)} %copy-done, bf16[1024,128]{1,0:T(8,128)(2,1)} %copy-done.3, bf16[1024,128]{1,0:T(8,128)(2,1)} %copy-done.2, bf16[1024,128]{1,0:T(8,128)(2,1)} %copy-done.1, bf16[1024,128]{1,0:T(8,128)(2,1)} %copy-done.4, ...), custom_call_target="tpu_custom_call" | custom-call | flops 1073741824 | bytes 4194304 | tf_op jit(solution)/shard_map/pallas_call | solution.py:42
  71.5 15.0 %all_to_all.25.part_ref = bf16[4,1024,128]{2,1,0:T(8,128)(2,1)S(1)} all-to-all(bf16[4,1024,128]{2,1,0:T(8,128)(2,1)S(1)} %shard_map.80), channel_id=1, replica_groups={{0,8,16,24},{32,40,48,56},{64,72,80,88},{96,104,112,120},{128,136,144,1..., dimensions={0} | all-to-all | bytes 2097152 | tf_op jit(solution)/shard_map/all_to_all | solution.py:28
  86.5 0.8 shard_map.81
  87.4 11.6 %all_to_all.26.refs_9_ = bf16[4,2,128,128]{3,2,1,0:T(8,128)(2,1)S(1)} all-to-all(bf16[4,2,128,128]{3,2,1,0:T(8,128)(2,1)S(1)} %get-tuple-element.27), channel_id=1, replica_groups={{0,32,64,96},{8,40,72,104},{16,48,80,112},{24,56,88,120},{128,160,192,2..., dimensions={0} | all-to-all | bytes 524288 | tf_op jit(solution)/shard_map/all_to_all | solution.py:28
  99.0 0.1 broadcast_select_fusion
  99.1 24.4 %all_to_all.27.refs_10_ = bf16[4,128,128]{2,1,0:T(8,128)(2,1)S(1)} all-to-all(bf16[4,128,128]{2,1,0:T(8,128)(2,1)S(1)} %broadcast_select_fusion), channel_id=1, replica_groups={{0,128,256,384},{8,136,264,392},{16,144,272,400},{24,152,280,408},{32,1..., dimensions={0} | all-to-all | bytes 262144 | tf_op jit(solution)/shard_map/all_to_all | solution.py:28
  123.5 1.7 %shard_map.82 = bf16[4,3,256,128]{3,2,1,0:T(8,128)(2,1)S(1)} custom-call(s32[5]{0:T(128)S(1)} %stack.23.place_ref.refs_0_, bf16[4,256,128]{2,1,0:T(8,128)(2,1)S(1)} %get-tuple-element.19.refs_0_.p0_ref.refs_1_, bf16[4,256,128]{2,1,0:T(8,128)(2,1)S(1)} %collective-permute-done.refs_1_.p1_ref.refs_2_, ...), custom_call_target="tpu_custom_call" | custom-call | flops 536870912 | bytes 3145728 | tf_op jit(solution)/shard_map/pallas_call | solution.py:42
  125.3 11.9 %all_to_all.28.in_ref = bf16[4,3,256,128]{3,2,1,0:T(8,128)(2,1)S(1)} all-to-all(bf16[4,3,256,128]{3,2,1,0:T(8,128)(2,1)S(1)} %shard_map.82), channel_id=1, replica_groups={{0,8,16,24},{32,40,48,56},{64,72,80,88},{96,104,112,120},{128,136,144,1..., dimensions={0} | all-to-all | bytes 1572864 | tf_op jit(solution)/shard_map/all_to_all | solution.py:28
  137.2 1.0 shard_map.83
  (4 shorter events, 0.1 us)
Async XLA Ops:
  2.6 65.2 %all-to-all-start = ((bf16[16,64,512]{2,1,0:T(8,128)(2,1)}), bf16[16,64,512]{2,1,0:T(8,128)(2,1)S(1)}, u32[]{:S(2)}, u32[]{:S(2)}) async-start(bf16[16,64,512]{2,1,0:T(8,128)(2,1)} %shard_map.76), calls=%async_computation | async-start | bytes 2097152 | tf_op jit(solution)/shard_map/all_to_all | solution.py:28
  19.9 10.7 %collective-permute-start = (bf16[4,256,128]{2,1,0:T(8,128)(2,1)S(1)}, bf16[4,256,128]{2,1,0:T(8,128)(2,1)S(1)}, u32[]{:S(2)}, u32[]{:S(2)}) collective-permute-start(bf16[4,256,128]{2,1,0:T(8,128)(2,1)S(1)} %get-tuple-element.20), channel_id=1, source_target_pairs={{0,8},{8,16},{16,24},{24,0},{32,40},{40,48},{48,56},{56,32},{64,72... | collective-permute-start | bytes 786440 | tf_op jit(solution)/shard_map/ppermute | solution.py:254
  23.4 12.7 %collective-permute-start.1 = (bf16[4,256,128]{2,1,0:T(8,128)(2,1)S(1)}, bf16[4,256,128]{2,1,0:T(8,128)(2,1)S(1)}, u32[]{:S(2)}, u32[]{:S(2)}) collective-permute-start(bf16[4,256,128]{2,1,0:T(8,128)(2,1)S(1)} %get-tuple-element.21), channel_id=1, source_target_pairs={{0,16},{8,24},{16,0},{24,8},{32,48},{40,56},{48,32},{56,40},{64,80... | collective-permute-start | bytes 786440 | tf_op jit(solution)/shard_map/ppermute | solution.py:254
  26.2 13.6 %collective-permute-start.2 = (bf16[4,256,128]{2,1,0:T(8,128)(2,1)S(1)}, bf16[4,256,128]{2,1,0:T(8,128)(2,1)S(1)}, u32[]{:S(2)}, u32[]{:S(2)}) collective-permute-start(bf16[4,256,128]{2,1,0:T(8,128)(2,1)S(1)} %get-tuple-element.22), channel_id=1, source_target_pairs={{0,24},{8,0},{16,8},{24,16},{32,56},{40,32},{48,40},{56,48},{64,88... | collective-permute-start | bytes 786440 | tf_op jit(solution)/shard_map/ppermute | solution.py:254
  39.9 24.0 %copy-start = (bf16[1024,128]{1,0:T(8,128)(2,1)}, bf16[1024,128]{1,0:T(8,128)(2,1)S(1)}, u32[]{:S(2)}) copy-start(bf16[1024,128]{1,0:T(8,128)(2,1)S(1)} %shard_map.78.refs_0_) | copy-start | bytes 786436
  39.9 16.0 %collective-permute-start.5 = (bf16[1024,128]{1,0:T(8,128)(2,1)S(1)}, bf16[1024,128]{1,0:T(8,128)(2,1)S(1)}, u32[]{:S(2)}, u32[]{:S(2)}) collective-permute-start(bf16[1024,128]{1,0:T(8,128)(2,1)S(1)} %shard_map.78.refs_0_), channel_id=1, source_target_pairs={{0,6},{1,7},{2,0},{3,1},{4,2},{5,3},{6,4},{7,5},{8,14},{9,15},{10,... | collective-permute-start | bytes 786440 | tf_op jit(solution)/shard_map/ppermute | solution.py:258
  44.6 13.3 %collective-permute-start.4 = (bf16[1024,128]{1,0:T(8,128)(2,1)S(1)}, bf16[1024,128]{1,0:T(8,128)(2,1)S(1)}, u32[]{:S(2)}, u32[]{:S(2)}) collective-permute-start(bf16[1024,128]{1,0:T(8,128)(2,1)S(1)} %shard_map.78.refs_0_), channel_id=1, source_target_pairs={{0,4},{1,5},{2,6},{3,7},{4,0},{5,1},{6,2},{7,3},{8,12},{9,13},{10,... | collective-permute-start | bytes 786440 | tf_op jit(solution)/shard_map/ppermute | solution.py:258
  47.3 14.2 %collective-permute-start.3 = (bf16[1024,128]{1,0:T(8,128)(2,1)S(1)}, bf16[1024,128]{1,0:T(8,128)(2,1)S(1)}, u32[]{:S(2)}, u32[]{:S(2)}) collective-permute-start(bf16[1024,128]{1,0:T(8,128)(2,1)S(1)} %shard_map.78.refs_0_), channel_id=1, source_target_pairs={{0,2},{1,3},{2,4},{3,5},{4,6},{5,7},{6,0},{7,1},{8,10},{9,11},{10,... | collective-permute-start | bytes 786440 | tf_op jit(solution)/shard_map/ppermute | solution.py:258
  50.1 13.8 %collective-permute-start.6 = (bf16[1024,128]{1,0:T(8,128)(2,1)S(1)}, bf16[1024,128]{1,0:T(8,128)(2,1)S(1)}, u32[]{:S(2)}, u32[]{:S(2)}) collective-permute-start(bf16[1024,128]{1,0:T(8,128)(2,1)S(1)} %shard_map.78.refs_0_), channel_id=1, source_target_pairs={{0,1},{1,0},{2,3},{3,2},{4,5},{5,4},{6,7},{7,6},{8,9},{9,8},{10,11... | collective-permute-start | bytes 786440 | tf_op jit(solution)/shard_map/ppermute | solution.py:260
  55.9 7.9 %copy-start.1 = (bf16[1024,128]{1,0:T(8,128)(2,1)}, bf16[1024,128]{1,0:T(8,128)(2,1)S(1)}, u32[]{:S(2)}) copy-start(bf16[1024,128]{1,0:T(8,128)(2,1)S(1)} %collective-permute-done.5.refs_3_) | copy-start | bytes 786436
  56.0 8.0 %collective-permute-start.9 = (bf16[1024,128]{1,0:T(8,128)(2,1)S(1)}, bf16[1024,128]{1,0:T(8,128)(2,1)S(1)}, u32[]{:S(2)}, u32[]{:S(2)}) collective-permute-start(bf16[1024,128]{1,0:T(8,128)(2,1)S(1)} %collective-permute-done.5.refs_3_), channel_id=1, source_target_pairs={{0,1},{1,0},{2,3},{3,2},{4,5},{5,4},{6,7},{7,6},{8,9},{9,8},{10,11... | collective-permute-start | bytes 786440 | tf_op jit(solution)/shard_map/ppermute | solution.py:260
  57.9 6.0 %copy-start.2 = (bf16[1024,128]{1,0:T(8,128)(2,1)}, bf16[1024,128]{1,0:T(8,128)(2,1)S(1)}, u32[]{:S(2)}) copy-start(bf16[1024,128]{1,0:T(8,128)(2,1)S(1)} %collective-permute-done.4.refs_2_) | copy-start | bytes 786436
  57.9 6.1 %collective-permute-start.8 = (bf16[1024,128]{1,0:T(8,128)(2,1)S(1)}, bf16[1024,128]{1,0:T(8,128)(2,1)S(1)}, u32[]{:S(2)}, u32[]{:S(2)}) collective-permute-start(bf16[1024,128]{1,0:T(8,128)(2,1)S(1)} %collective-permute-done.4.refs_2_), channel_id=1, source_target_pairs={{0,1},{1,0},{2,3},{3,2},{4,5},{5,4},{6,7},{7,6},{8,9},{9,8},{10,11... | collective-permute-start | bytes 786440 | tf_op jit(solution)/shard_map/ppermute | solution.py:260
  61.5 2.4 %copy-start.3 = (bf16[1024,128]{1,0:T(8,128)(2,1)}, bf16[1024,128]{1,0:T(8,128)(2,1)S(1)}, u32[]{:S(2)}) copy-start(bf16[1024,128]{1,0:T(8,128)(2,1)S(1)} %collective-permute-done.3.refs_1_) | copy-start | bytes 786436
  61.5 3.9 %collective-permute-start.7 = (bf16[1024,128]{1,0:T(8,128)(2,1)S(1)}, bf16[1024,128]{1,0:T(8,128)(2,1)}, u32[]{:S(2)}, u32[]{:S(2)}) collective-permute-start(bf16[1024,128]{1,0:T(8,128)(2,1)S(1)} %collective-permute-done.3.refs_1_), channel_id=1, source_target_pairs={{0,1},{1,0},{2,3},{3,2},{4,5},{5,4},{6,7},{7,6},{8,9},{9,8},{10,11... | collective-permute-start | bytes 786440 | tf_op jit(solution)/shard_map/ppermute | solution.py:260
  63.9 0.7 copy-start.4
  63.9 0.8 copy-start.5
  64.7 0.7 copy-start.6

commit v5 on v4

--- a/solution.py
+++ b/solution.py
@@ -11,16 +11,19 @@
 NY = 4
 NX = 4
 ZG = 4
+LINE = (2, 1, 3, 0)
+NEAR = (2, 1, 3, 0)
+FAR = (2, 1, 3, 0)
 F32 = jnp.float32
 BF16 = jnp.bfloat16
 
 
 def groups(ctx):
     nz = ctx // NY
-    y_line = [[z * NY + y for y in range(NY)] for z in range(nz)]
+    y_line = [[z * NY + y for y in LINE] for z in range(nz)]
     z_line = [[z * NY + y for z in range(nz)] for y in range(NY)]
-    z_near = [[(g * ZG + i) * NY + y for i in range(ZG)] for g in range(nz // ZG) for y in range(NY)]
-    z_far = [[(g * ZG + i) * NY + y for g in range(nz // ZG)] for i in range(ZG) for y in range(NY)]
+    z_near = [[(g * ZG + i) * NY + y for i in NEAR] for g in range(nz // ZG) for y in range(NY)]
+    z_far = [[(g * ZG + i) * NY + y for g in FAR] for i in range(ZG) for y in range(NY)]
     return y_line, z_line, z_near, z_far
 
 
@@ -116,9 +119,9 @@
         tile = pl.ds(t * step, step)
         for i in range(2 * NX):
             lanes = pl.ds(i // NX * depth, depth)
-            load = pltpu.make_async_copy(refs[i].at[tile, :], held.at[i % NX, tile, lanes], sems.at[t, i])
-            load.start()
-            loads.append(load)
+            loads.append(pltpu.make_async_copy(refs[i].at[tile, :], held.at[i % NX, tile, lanes], sems.at[t, i]))
+    for load in loads:
+        load.start()
     for t in range(NY):
         part = jnp.zeros((step, weight.shape[1]), F32)
         for load in loads[t * 2 * NX : (t + 1) * 2 * NX]:
@@ -131,8 +134,8 @@
             part = part + dot(held[d, t * step : (t + 1) * step, :], rows, 1, 0)
         part = part.astype(BF16)
         rows = pl.ds(pl.multiple_of(block_of(place_ref, t) * step, step), step)
-        for h in range(NY):
-            out_ref[h, rows, :] = part[:, h * DH : (h + 1) * DH]
+        for i, h in enumerate(LINE):
+            out_ref[i, rows, :] = part[:, h * DH : (h + 1) * DH]
 
 
 def key_kernel(p0_ref, p1_ref, p2_ref, p3_ref, states_ref, scores_ref):
@@ -170,12 +173,12 @@
     prefix = jnp.zeros((DH, DH), F32)
     suffix = jnp.zeros((DH, DH), F32)
     for i in range(near_ref.shape[0]):
-        prefix = prefix + jnp.where(i < inner, near_ref[i, 0].astype(F32), 0.0)
-        suffix = suffix + jnp.where(i > inner, near_ref[i, 1].astype(F32), 0.0)
+        prefix = prefix + jnp.where(NEAR[i] < inner, near_ref[i, 0].astype(F32), 0.0)
+        suffix = suffix + jnp.where(NEAR[i] > inner, near_ref[i, 1].astype(F32), 0.0)
     for i in range(far_ref.shape[0]):
         other = far_ref[i].astype(F32)
-        prefix = prefix + jnp.where(i < outer, other, 0.0)
-        suffix = suffix + jnp.where(i > outer, other, 0.0)
+        prefix = prefix + jnp.where(FAR[i] < outer, other, 0.0)
+        suffix = suffix + jnp.where(FAR[i] > outer, other, 0.0)
     row = lax.broadcasted_iota(jnp.int32, (step, step), 0)
     col = lax.broadcasted_iota(jnp.int32, (step, step), 1)
     lower = row >= col
@@ -198,15 +201,16 @@
         grad_q = dot(scores_grad, key, 1, 0) + dot(grad, before, 1, 1)
         grad_k = dot(scores_grad_t, query, 1, 0) + dot(value, after, 1, 1)
         grad_v = dot(scores_t, grad, 1, 0) + dot(key, after, 1, 0)
-        out_ref[block, 0] = (factor * grad_q).astype(BF16)
-        out_ref[block, 1] = (factor * grad_k).astype(BF16)
-        out_ref[block, 2] = (factor * grad_v).astype(BF16)
+        to = sum(jnp.where(block == h, i, 0) for i, h in enumerate(LINE))
+        out_ref[to, 0] = (factor * grad_q).astype(BF16)
+        out_ref[to, 1] = (factor * grad_k).astype(BF16)
+        out_ref[to, 2] = (factor * grad_v).astype(BF16)
 
 
 def unpack_kernel(in_ref, q_ref, k_ref, v_ref):
-    for h in range(NY):
+    for i, h in enumerate(LINE):
         for at, ref in enumerate((q_ref, k_ref, v_ref)):
-            ref[:, h * DH : (h + 1) * DH] = in_ref[h, at]
+            ref[:, h * DH : (h + 1) * DH] = in_ref[i, at]
 
 
 def local(queries, keys, values, grad_out, out_weight):
@@ -221,7 +225,7 @@
     here = lax.axis_index("ctx")
     z = here // NY
     place = jnp.stack([z % ZG, z // ZG, here % NY, at // 2, at % 2]).astype(jnp.int32)
-    earlier = jnp.arange(nz // ZG, dtype=jnp.int32) < place[1]
+    earlier = jnp.array(FAR, jnp.int32) < place[1]
     grad_out, place, earlier = lax.optimization_barrier((grad_out, place, earlier))
 
     copies = call(

time: 139 us -> 130 us (0.935)
  the two profiles are of different devices: /device:TPU:8 before, /device:TPU:42 now
where the time goes in v5:
time: 130 us
  blocking collectives  55.1 us (42%)
  starting transfers between devices  44.5 us (34%)
  waiting for transfers between devices  15.3 us (12%)
  Pallas kernels  11.5 us (9%)
  local copies, waits for them, and re-layouts  2.13 us (2%)
    all_to_all x4, blocking collectives, exchange(): return lax.all_to_all(pieces, 'ctx', 0, 0, axis_index_groups=group)  55.1 us
    all_to_all x1, starting transfers between devices, exchange(): return lax.all_to_all(pieces, 'ctx', 0, 0, axis_index_groups=group)  15.2 us
    pallas_call x8, Pallas kernels, run(): pl.pallas_call(kernel, out_shape=out_shape, in_specs=specs, out_specs=out...  11.5 us
    ppermute x3, starting transfers between devices, local(): packed[d] = lax.ppermute(packed[d], 'ctx', turn)  10.7 us
    ppermute x3, starting transfers between devices, local(): lax.ppermute(mine, 'tp', [(t, (t + 2 * d) % tp) for t in range(tp)])  10.5 us
    ppermute x3, waiting for transfers between devices, local(): packed[d] = lax.ppermute(packed[d], 'ctx', turn)  9.03 us
    ppermute x4, starting transfers between devices, local(): shares = shares + [lax.ppermute(share, 'tp', swap) for share in shares]  8.15 us
    all_to_all x1, waiting for transfers between devices, exchange(): return lax.all_to_all(pieces, 'ctx', 0, 0, axis_index_groups=group)  3.62 us
  transfers between devices with their start and end apart: 11, of which 5 were waited for; matrix products, arithmetic and copies ran while one was open for 0% of the time, Pallas kernels for 2%

profile of v5, /device:TPU:42, one launch (start us, length us, event | category | flops | bytes accessed | tf_op | source)
XLA Modules:
  0.0 129.6 jit_solution(7490667600921545328)
XLA Ops:
  0.6 2.0 %shard_map.85 = bf16[16,64,512]{2,1,0:T(8,128)(2,1)} custom-call(bf16[64,512]{1,0:T(8,128)(2,1)} %w_ref.1), custom_call_target="tpu_custom_call" | custom-call | bytes 1048576 | tf_op jit(solution)/shard_map/pallas_call | solution.py:45
  2.6 15.2 %all-to-all-start = ((bf16[16,64,512]{2,1,0:T(8,128)(2,1)}), bf16[16,64,512]{2,1,0:T(8,128)(2,1)S(1)}, u32[]{:S(2)}, u32[]{:S(2)}) async-start(bf16[16,64,512]{2,1,0:T(8,128)(2,1)} %shard_map.85), calls=%async_computation | async-start | bytes 2097152 | tf_op jit(solution)/shard_map/all_to_all | solution.py:31
  17.8 0.0 copy-start.7
  17.8 0.1 stack.23.place_ref.refs_0_
  17.9 0.6 copy-done.7
  18.5 1.9 %shard_map.86 = (bf16[4,256,128]{2,1,0:T(8,128)(2,1)S(1)}, bf16[4,256,128]{2,1,0:T(8,128)(2,1)S(1)}, bf16[4,256,128]{2,1,0:T(8,128)(2,1)S(1)}, bf16[4,256,128]{2,1,0:T(8,128)(2,1)S(1)}) custom-call(s32[5]{0:T(128)S(1)} %stack.23.place_ref.refs_0_, bf16[256,512]{1,0:T(8,128)(2,1)} %q_ref.1, bf16[256,512]{1,0:T(8,128)(2,1)} %k_ref.1, bf16[256,512]{1,0:T(8,128)(2,1)} %v_ref.1, ...), custom_call_target="tpu_custom_call" | custom-call | bytes 2097152 | tf_op jit(solution)/shard_map/pallas_call | solution.py:45
  20.4 3.5 %collective-permute-start = (bf16[4,256,128]{2,1,0:T(8,128)(2,1)S(1)}, bf16[4,256,128]{2,1,0:T(8,128)(2,1)S(1)}, u32[]{:S(2)}, u32[]{:S(2)}) collective-permute-start(bf16[4,256,128]{2,1,0:T(8,128)(2,1)S(1)} %get-tuple-element.20), channel_id=1, source_target_pairs={{0,8},{8,16},{16,24},{24,0},{32,40},{40,48},{48,56},{56,32},{64,72... | collective-permute-start | bytes 786440 | tf_op jit(solution)/shard_map/ppermute | solution.py:258
  23.9 2.8 %collective-permute-start.1 = (bf16[4,256,128]{2,1,0:T(8,128)(2,1)S(1)}, bf16[4,256,128]{2,1,0:T(8,128)(2,1)S(1)}, u32[]{:S(2)}, u32[]{:S(2)}) collective-permute-start(bf16[4,256,128]{2,1,0:T(8,128)(2,1)S(1)} %get-tuple-element.21), channel_id=1, source_target_pairs={{0,16},{8,24},{16,0},{24,8},{32,48},{40,56},{48,32},{56,40},{64,80... | collective-permute-start | bytes 786440 | tf_op jit(solution)/shard_map/ppermute | solution.py:258
  26.7 4.3 %collective-permute-start.2 = (bf16[4,256,128]{2,1,0:T(8,128)(2,1)S(1)}, bf16[4,256,128]{2,1,0:T(8,128)(2,1)S(1)}, u32[]{:S(2)}, u32[]{:S(2)}) collective-permute-start(bf16[4,256,128]{2,1,0:T(8,128)(2,1)S(1)} %get-tuple-element.22), channel_id=1, source_target_pairs={{0,24},{8,0},{16,8},{24,16},{32,56},{40,32},{48,40},{56,48},{64,88... | collective-permute-start | bytes 786440 | tf_op jit(solution)/shard_map/ppermute | solution.py:258
  31.1 0.0 collective-permute-done.refs_1_.p1_ref.refs_2_
  31.1 5.5 %collective-permute-done.1.refs_2_.p2_ref.refs_3_ = bf16[4,256,128]{2,1,0:T(8,128)(2,1)S(1)} collective-permute-done((bf16[4,256,128]{2,1,0:T(8,128)(2,1)S(1)}, bf16[4,256,128]{2,1,0:T(8,128)(2,1)S(1)}, u32[]{:S(2)}, u32[]{:S(2)}) %collective-permute-start.1) | collective-permute-done | bytes 262176 | tf_op jit(solution)/shard_map/ppermute | solution.py:258
  36.6 3.5 %collective-permute-done.2.refs_3_.p3_ref.refs_4_ = bf16[4,256,128]{2,1,0:T(8,128)(2,1)S(1)} collective-permute-done((bf16[4,256,128]{2,1,0:T(8,128)(2,1)S(1)}, bf16[4,256,128]{2,1,0:T(8,128)(2,1)S(1)}, u32[]{:S(2)}, u32[]{:S(2)}) %collective-permute-start.2) | collective-permute-done | bytes 262176 | tf_op jit(solution)/shard_map/ppermute | solution.py:258
  40.1 0.0 copy-start
  40.1 2.4 %collective-permute-start.5 = (bf16[1024,128]{1,0:T(8,128)(2,1)S(1)}, bf16[1024,128]{1,0:T(8,128)(2,1)S(1)}, u32[]{:S(2)}, u32[]{:S(2)}) collective-permute-start(bf16[1024,128]{1,0:T(8,128)(2,1)S(1)} %shard_map.87.refs_0_), channel_id=1, source_target_pairs={{0,6},{1,7},{2,0},{3,1},{4,2},{5,3},{6,4},{7,5},{8,14},{9,15},{10,... | collective-permute-start | bytes 786440 | tf_op jit(solution)/shard_map/ppermute | solution.py:262
  42.6 4.3 %collective-permute-start.4 = (bf16[1024,128]{1,0:T(8,128)(2,1)S(1)}, bf16[1024,128]{1,0:T(8,128)(2,1)S(1)}, u32[]{:S(2)}, u32[]{:S(2)}) collective-permute-start(bf16[1024,128]{1,0:T(8,128)(2,1)S(1)} %shard_map.87.refs_0_), channel_id=1, source_target_pairs={{0,4},{1,5},{2,6},{3,7},{4,0},{5,1},{6,2},{7,3},{8,12},{9,13},{10,... | collective-permute-start | bytes 786440 | tf_op jit(solution)/shard_map/ppermute | solution.py:262
  46.9 3.7 %collective-permute-start.3 = (bf16[1024,128]{1,0:T(8,128)(2,1)S(1)}, bf16[1024,128]{1,0:T(8,128)(2,1)S(1)}, u32[]{:S(2)}, u32[]{:S(2)}) collective-permute-start(bf16[1024,128]{1,0:T(8,128)(2,1)S(1)} %shard_map.87.refs_0_), channel_id=1, source_target_pairs={{0,2},{1,3},{2,4},{3,5},{4,6},{5,7},{6,0},{7,1},{8,10},{9,11},{10,... | collective-permute-start | bytes 786440 | tf_op jit(solution)/shard_map/ppermute | solution.py:262
  50.6 1.9 %collective-permute-start.6 = (bf16[1024,128]{1,0:T(8,128)(2,1)S(1)}, bf16[1024,128]{1,0:T(8,128)(2,1)S(1)}, u32[]{:S(2)}, u32[]{:S(2)}) collective-permute-start(bf16[1024,128]{1,0:T(8,128)(2,1)S(1)} %shard_map.87.refs_0_), channel_id=1, source_target_pairs={{0,1},{1,0},{2,3},{3,2},{4,5},{5,4},{6,7},{7,6},{8,9},{9,8},{10,11... | collective-permute-start | bytes 786440 | tf_op jit(solution)/shard_map/ppermute | solution.py:264
  52.6 0.0 collective-permute-done.5.refs_3_
  52.6 0.0 copy-start.1
  52.6 2.4 %collective-permute-start.9 = (bf16[1024,128]{1,0:T(8,128)(2,1)S(1)}, bf16[1024,128]{1,0:T(8,128)(2,1)S(1)}, u32[]{:S(2)}, u32[]{:S(2)}) collective-permute-start(bf16[1024,128]{1,0:T(8,128)(2,1)S(1)} %collective-permute-done.5.refs_3_), channel_id=1, source_target_pairs={{0,1},{1,0},{2,3},{3,2},{4,5},{5,4},{6,7},{7,6},{8,9},{9,8},{10,11... | collective-permute-start | bytes 786440 | tf_op jit(solution)/shard_map/ppermute | solution.py:264
  55.0 1.8 %collective-permute-done.4.refs_2_ = bf16[1024,128]{1,0:T(8,128)(2,1)S(1)} collective-permute-done((bf16[1024,128]{1,0:T(8,128)(2,1)S(1)}, bf16[1024,128]{1,0:T(8,128)(2,1)S(1)}, u32[]{:S(2)}, u32[]{:S(2)}) %collective-permute-start.4) | collective-permute-done | bytes 262176 | tf_op jit(solution)/shard_map/ppermute | solution.py:262
  56.8 0.0 copy-start.2
  56.8 1.9 %collective-permute-start.8 = (bf16[1024,128]{1,0:T(8,128)(2,1)S(1)}, bf16[1024,128]{1,0:T(8,128)(2,1)S(1)}, u32[]{:S(2)}, u32[]{:S(2)}) collective-permute-start(bf16[1024,128]{1,0:T(8,128)(2,1)S(1)} %collective-permute-done.4.refs_2_), channel_id=1, source_target_pairs={{0,1},{1,0},{2,3},{3,2},{4,5},{5,4},{6,7},{7,6},{8,9},{9,8},{10,11... | collective-permute-start | bytes 786440 | tf_op jit(solution)/shard_map/ppermute | solution.py:264
  58.7 0.9 collective-permute-done.3.refs_1_
  59.6 0.0 copy-start.3
  59.6 1.9 %collective-permute-start.7 = (bf16[1024,128]{1,0:T(8,128)(2,1)S(1)}, bf16[1024,128]{1,0:T(8,128)(2,1)}, u32[]{:S(2)}, u32[]{:S(2)}) collective-permute-start(bf16[1024,128]{1,0:T(8,128)(2,1)S(1)} %collective-permute-done.3.refs_1_), channel_id=1, source_target_pairs={{0,1},{1,0},{2,3},{3,2},{4,5},{5,4},{6,7},{7,6},{8,9},{9,8},{10,11... | collective-permute-start | bytes 786440 | tf_op jit(solution)/shard_map/ppermute | solution.py:264
  61.5 0.4 shard_map.88
  61.9 0.0 copy-done
  61.9 0.0 copy-done.1
  61.9 0.0 copy-done.2
  61.9 0.0 copy-done.3
  61.9 0.0 collective-permute-done.6.refs_4_
  62.0 0.0 copy-start.4
  62.0 0.0 collective-permute-done.9.refs_7_
  62.0 0.0 copy-start.5
  62.0 0.0 collective-permute-done.8.refs_6_
  62.0 0.7 copy-done.4
  62.7 0.1 copy-done.5
  62.7 0.0 copy-start.6
  62.7 0.7 copy-done.6
  63.5 0.0 collective-permute-done.7.refs_5_
  63.5 3.6 %all-to-all-done = bf16[16,64,512]{2,1,0:T(8,128)(2,1)S(1)} async-done(((bf16[16,64,512]{2,1,0:T(8,128)(2,1)}), bf16[16,64,512]{2,1,0:T(8,128)(2,1)S(1)}, u32[]{:S(2)}, u32[]{:S(2)}) %all-to-all-start) | async-done | bytes 1048608 | tf_op jit(solution)/shard_map/all_to_all | solution.py:31
  67.1 3.7 %shard_map.89 = bf16[4,1024,128]{2,1,0:T(8,128)(2,1)S(1)} custom-call(s32[5]{0:T(128)S(1)} %stack.23.place_ref.refs_0_, bf16[1024,128]{1,0:T(8,128)(2,1)} %copy-done, bf16[1024,128]{1,0:T(8,128)(2,1)} %copy-done.3, bf16[1024,128]{1,0:T(8,128)(2,1)} %copy-done.2, bf16[1024,128]{1,0:T(8,128)(2,1)} %copy-done.1, bf16[1024,128]{1,0:T(8,128)(2,1)} %copy-done.4, ...), custom_call_target="tpu_custom_call" | custom-call | flops 1073741824 | bytes 4194304 | tf_op jit(solution)/shard_map/pallas_call | solution.py:45
  70.8 13.8 %all_to_all.25.part_ref = bf16[4,1024,128]{2,1,0:T(8,128)(2,1)S(1)} all-to-all(bf16[4,1024,128]{2,1,0:T(8,128)(2,1)S(1)} %shard_map.89), channel_id=1, replica_groups={{16,8,24,0},{48,40,56,32},{80,72,88,64},{112,104,120,96},{144,136,152,1..., dimensions={0} | all-to-all | bytes 2097152 | tf_op jit(solution)/shard_map/all_to_all | solution.py:31
  84.5 0.8 shard_map.90
  85.4 10.4 %all_to_all.26.refs_9_ = bf16[4,2,128,128]{3,2,1,0:T(8,128)(2,1)S(1)} all-to-all(bf16[4,2,128,128]{3,2,1,0:T(8,128)(2,1)S(1)} %get-tuple-element.27), channel_id=1, replica_groups={{64,32,96,0},{72,40,104,8},{80,48,112,16},{88,56,120,24},{192,160,224,1..., dimensions={0} | all-to-all | bytes 524288 | tf_op jit(solution)/shard_map/all_to_all | solution.py:31
  95.9 0.1 broadcast_select_fusion
  95.9 18.4 %all_to_all.27.refs_10_ = bf16[4,128,128]{2,1,0:T(8,128)(2,1)S(1)} all-to-all(bf16[4,128,128]{2,1,0:T(8,128)(2,1)S(1)} %broadcast_select_fusion), channel_id=1, replica_groups={{256,128,384,0},{264,136,392,8},{272,144,400,16},{280,152,408,24},{288,..., dimensions={0} | all-to-all | bytes 262144 | tf_op jit(solution)/shard_map/all_to_all | solution.py:31
  114.4 1.7 %shard_map.91 = bf16[4,3,256,128]{3,2,1,0:T(8,128)(2,1)S(1)} custom-call(s32[5]{0:T(128)S(1)} %stack.23.place_ref.refs_0_, bf16[4,256,128]{2,1,0:T(8,128)(2,1)S(1)} %get-tuple-element.19.refs_0_.p0_ref.refs_1_, bf16[4,256,128]{2,1,0:T(8,128)(2,1)S(1)} %collective-permute-done.refs_1_.p1_ref.refs_2_, ...), custom_call_target="tpu_custom_call" | custom-call | flops 536870912 | bytes 3145728 | tf_op jit(solution)/shard_map/pallas_call | solution.py:45
  116.1 12.5 %all_to_all.28.in_ref = bf16[4,3,256,128]{3,2,1,0:T(8,128)(2,1)S(1)} all-to-all(bf16[4,3,256,128]{3,2,1,0:T(8,128)(2,1)S(1)} %shard_map.91), channel_id=1, replica_groups={{16,8,24,0},{48,40,56,32},{80,72,88,64},{112,104,120,96},{144,136,152,1..., dimensions={0} | all-to-all | bytes 1572864 | tf_op jit(solution)/shard_map/all_to_all | solution.py:31
  128.6 1.0 shard_map.92
  (4 shorter events, 0.1 us)
Async XLA Ops:
  2.6 64.5 %all-to-all-start = ((bf16[16,64,512]{2,1,0:T(8,128)(2,1)}), bf16[16,64,512]{2,1,0:T(8,128)(2,1)S(1)}, u32[]{:S(2)}, u32[]{:S(2)}) async-start(bf16[16,64,512]{2,1,0:T(8,128)(2,1)} %shard_map.85), calls=%async_computation | async-start | bytes 2097152 | tf_op jit(solution)/shard_map/all_to_all | solution.py:31
  17.8 0.7 copy-start.7
  20.4 10.7 %collective-permute-start = (bf16[4,256,128]{2,1,0:T(8,128)(2,1)S(1)}, bf16[4,256,128]{2,1,0:T(8,128)(2,1)S(1)}, u32[]{:S(2)}, u32[]{:S(2)}) collective-permute-start(bf16[4,256,128]{2,1,0:T(8,128)(2,1)S(1)} %get-tuple-element.20), channel_id=1, source_target_pairs={{0,8},{8,16},{16,24},{24,0},{32,40},{40,48},{48,56},{56,32},{64,72... | collective-permute-start | bytes 786440 | tf_op jit(solution)/shard_map/ppermute | solution.py:258
  23.9 12.7 %collective-permute-start.1 = (bf16[4,256,128]{2,1,0:T(8,128)(2,1)S(1)}, bf16[4,256,128]{2,1,0:T(8,128)(2,1)S(1)}, u32[]{:S(2)}, u32[]{:S(2)}) collective-permute-start(bf16[4,256,128]{2,1,0:T(8,128)(2,1)S(1)} %get-tuple-element.21), channel_id=1, source_target_pairs={{0,16},{8,24},{16,0},{24,8},{32,48},{40,56},{48,32},{56,40},{64,80... | collective-permute-start | bytes 786440 | tf_op jit(solution)/shard_map/ppermute | solution.py:258
  26.7 13.4 %collective-permute-start.2 = (bf16[4,256,128]{2,1,0:T(8,128)(2,1)S(1)}, bf16[4,256,128]{2,1,0:T(8,128)(2,1)S(1)}, u32[]{:S(2)}, u32[]{:S(2)}) collective-permute-start(bf16[4,256,128]{2,1,0:T(8,128)(2,1)S(1)} %get-tuple-element.22), channel_id=1, source_target_pairs={{0,24},{8,0},{16,8},{24,16},{32,56},{40,32},{48,40},{56,48},{64,88... | collective-permute-start | bytes 786440 | tf_op jit(solution)/shard_map/ppermute | solution.py:258
  40.1 21.8 %copy-start = (bf16[1024,128]{1,0:T(8,128)(2,1)}, bf16[1024,128]{1,0:T(8,128)(2,1)S(1)}, u32[]{:S(2)}) copy-start(bf16[1024,128]{1,0:T(8,128)(2,1)S(1)} %shard_map.87.refs_0_) | copy-start | bytes 786436
  40.1 12.4 %collective-permute-start.5 = (bf16[1024,128]{1,0:T(8,128)(2,1)S(1)}, bf16[1024,128]{1,0:T(8,128)(2,1)S(1)}, u32[]{:S(2)}, u32[]{:S(2)}) collective-permute-start(bf16[1024,128]{1,0:T(8,128)(2,1)S(1)} %shard_map.87.refs_0_), channel_id=1, source_target_pairs={{0,6},{1,7},{2,0},{3,1},{4,2},{5,3},{6,4},{7,5},{8,14},{9,15},{10,... | collective-permute-start | bytes 786440 | tf_op jit(solution)/shard_map/ppermute | solution.py:262
  42.6 14.2 %collective-permute-start.4 = (bf16[1024,128]{1,0:T(8,128)(2,1)S(1)}, bf16[1024,128]{1,0:T(8,128)(2,1)S(1)}, u32[]{:S(2)}, u32[]{:S(2)}) collective-permute-start(bf16[1024,128]{1,0:T(8,128)(2,1)S(1)} %shard_map.87.refs_0_), channel_id=1, source_target_pairs={{0,4},{1,5},{2,6},{3,7},{4,0},{5,1},{6,2},{7,3},{8,12},{9,13},{10,... | collective-permute-start | bytes 786440 | tf_op jit(solution)/shard_map/ppermute | solution.py:262
  46.9 12.7 %collective-permute-start.3 = (bf16[1024,128]{1,0:T(8,128)(2,1)S(1)}, bf16[1024,128]{1,0:T(8,128)(2,1)S(1)}, u32[]{:S(2)}, u32[]{:S(2)}) collective-permute-start(bf16[1024,128]{1,0:T(8,128)(2,1)S(1)} %shard_map.87.refs_0_), channel_id=1, source_target_pairs={{0,2},{1,3},{2,4},{3,5},{4,6},{5,7},{6,0},{7,1},{8,10},{9,11},{10,... | collective-permute-start | bytes 786440 | tf_op jit(solution)/shard_map/ppermute | solution.py:262
  50.6 11.3 %collective-permute-start.6 = (bf16[1024,128]{1,0:T(8,128)(2,1)S(1)}, bf16[1024,128]{1,0:T(8,128)(2,1)S(1)}, u32[]{:S(2)}, u32[]{:S(2)}) collective-permute-start(bf16[1024,128]{1,0:T(8,128)(2,1)S(1)} %shard_map.87.refs_0_), channel_id=1, source_target_pairs={{0,1},{1,0},{2,3},{3,2},{4,5},{5,4},{6,7},{7,6},{8,9},{9,8},{10,11... | collective-permute-start | bytes 786440 | tf_op jit(solution)/shard_map/ppermute | solution.py:264
  52.6 9.3 %copy-start.1 = (bf16[1024,128]{1,0:T(8,128)(2,1)}, bf16[1024,128]{1,0:T(8,128)(2,1)S(1)}, u32[]{:S(2)}) copy-start(bf16[1024,128]{1,0:T(8,128)(2,1)S(1)} %collective-permute-done.5.refs_3_) | copy-start | bytes 786436
  52.6 9.4 %collective-permute-start.9 = (bf16[1024,128]{1,0:T(8,128)(2,1)S(1)}, bf16[1024,128]{1,0:T(8,128)(2,1)S(1)}, u32[]{:S(2)}, u32[]{:S(2)}) collective-permute-start(bf16[1024,128]{1,0:T(8,128)(2,1)S(1)} %collective-permute-done.5.refs_3_), channel_id=1, source_target_pairs={{0,1},{1,0},{2,3},{3,2},{4,5},{5,4},{6,7},{7,6},{8,9},{9,8},{10,11... | collective-permute-start | bytes 786440 | tf_op jit(solution)/shard_map/ppermute | solution.py:264
  56.8 5.1 %copy-start.2 = (bf16[1024,128]{1,0:T(8,128)(2,1)}, bf16[1024,128]{1,0:T(8,128)(2,1)S(1)}, u32[]{:S(2)}) copy-start(bf16[1024,128]{1,0:T(8,128)(2,1)S(1)} %collective-permute-done.4.refs_2_) | copy-start | bytes 786436
  56.8 5.2 %collective-permute-start.8 = (bf16[1024,128]{1,0:T(8,128)(2,1)S(1)}, bf16[1024,128]{1,0:T(8,128)(2,1)S(1)}, u32[]{:S(2)}, u32[]{:S(2)}) collective-permute-start(bf16[1024,128]{1,0:T(8,128)(2,1)S(1)} %collective-permute-done.4.refs_2_), channel_id=1, source_target_pairs={{0,1},{1,0},{2,3},{3,2},{4,5},{5,4},{6,7},{7,6},{8,9},{9,8},{10,11... | collective-permute-start | bytes 786440 | tf_op jit(solution)/shard_map/ppermute | solution.py:264
  59.6 2.4 %copy-start.3 = (bf16[1024,128]{1,0:T(8,128)(2,1)}, bf16[1024,128]{1,0:T(8,128)(2,1)S(1)}, u32[]{:S(2)}) copy-start(bf16[1024,128]{1,0:T(8,128)(2,1)S(1)} %collective-permute-done.3.refs_1_) | copy-start | bytes 786436
  59.6 3.9 %collective-permute-start.7 = (bf16[1024,128]{1,0:T(8,128)(2,1)S(1)}, bf16[1024,128]{1,0:T(8,128)(2,1)}, u32[]{:S(2)}, u32[]{:S(2)}) collective-permute-start(bf16[1024,128]{1,0:T(8,128)(2,1)S(1)} %collective-permute-done.3.refs_1_), channel_id=1, source_target_pairs={{0,1},{1,0},{2,3},{3,2},{4,5},{5,4},{6,7},{7,6},{8,9},{9,8},{10,11... | collective-permute-start | bytes 786440 | tf_op jit(solution)/shard_map/ppermute | solution.py:264
  62.0 0.7 copy-start.4
  62.0 0.8 copy-start.5
  62.7 0.7 copy-start.6

commit v6 on v5

--- a/solution.py
+++ b/solution.py
@@ -110,41 +110,37 @@
 
 
 def product_kernel(place_ref, *refs):
-    weight, early_ref, out_ref, held, sems = refs[2 * NX :]
+    weight_ref, early_ref, out_ref, weight, sems = refs[2 * NX :]
     tokens, depth = refs[0].shape
     step = tokens // NY
     core = place_ref[4]
     loads = []
+    for d in range(NX):
+        chip = lax.rem(place_ref[3] + (NX - d), NX)
+        start = pl.multiple_of(chip * 2 * depth, 2 * depth)
+        load = pltpu.make_async_copy(weight_ref.at[pl.ds(start, 2 * depth), :], weight.at[d], sems.at[d])
+        load.start()
+        loads.append(load)
+    own = pl.multiple_of(core * depth, depth)
+    far = pl.multiple_of((1 - core) * depth, depth)
     for t in range(NY):
-        tile = pl.ds(t * step, step)
-        for i in range(2 * NX):
-            lanes = pl.ds(i // NX * depth, depth)
-            loads.append(pltpu.make_async_copy(refs[i].at[tile, :], held.at[i % NX, tile, lanes], sems.at[t, i]))
-    for load in loads:
-        load.start()
-    for t in range(NY):
-        part = jnp.zeros((step, weight.shape[1]), F32)
-        for load in loads[t * 2 * NX : (t + 1) * 2 * NX]:
-            load.wait()
+        part = jnp.zeros((step, weight.shape[2]), F32)
+        tile = slice(t * step, (t + 1) * step)
         for d in range(NX):
-            chip = lax.rem(place_ref[3] + (NX - d), NX)
-            own = pl.multiple_of((chip * 2 + core) * depth, depth)
-            far = pl.multiple_of((chip * 2 + 1 - core) * depth, depth)
-            rows = jnp.concatenate([weight[pl.ds(own, depth), :], weight[pl.ds(far, depth), :]], axis=0)
-            part = part + dot(held[d, t * step : (t + 1) * step, :], rows, 1, 0)
+            if t == 0:
+                loads[d].wait()
+            held = jnp.concatenate([refs[d][tile, :], refs[NX + d][tile, :]], axis=1)
+            rows = jnp.concatenate([weight[d, pl.ds(own, depth), :], weight[d, pl.ds(far, depth), :]], axis=0)
+            part = part + dot(held, rows, 1, 0)
         part = part.astype(BF16)
         rows = pl.ds(pl.multiple_of(block_of(place_ref, t) * step, step), step)
         for i, h in enumerate(LINE):
             out_ref[i, rows, :] = part[:, h * DH : (h + 1) * DH]
 
 
-def key_kernel(p0_ref, p1_ref, p2_ref, p3_ref, states_ref, scores_ref):
-    step = p0_ref.shape[1]
-    row = lax.broadcasted_iota(jnp.int32, (step, step), 0)
-    col = lax.broadcasted_iota(jnp.int32, (step, step), 1)
+def key_kernel(p0_ref, p1_ref, p2_ref, p3_ref, states_ref):
     for d, ref in enumerate((p0_ref, p1_ref, p2_ref, p3_ref)):
         states_ref[d] = dot(ref[1], ref[2], 0, 0)
-        scores_ref[d] = jnp.where(row <= col, dot(ref[1], ref[0], 1, 1), 0.0).astype(BF16)
 
 
 def state_kernel(place_ref, p0_ref, p1_ref, p2_ref, p3_ref, part_ref, key_ref, grad_ref, query_ref, copies_ref):
@@ -167,7 +163,7 @@
         copies_ref[i, 1] = total_q.astype(BF16)
 
 
-def final_kernel(factor, place_ref, p0_ref, p1_ref, p2_ref, p3_ref, grad_ref, key_ref, query_ref, scores_ref, near_ref, far_ref, out_ref):
+def final_kernel(factor, place_ref, p0_ref, p1_ref, p2_ref, p3_ref, grad_ref, key_ref, query_ref, near_ref, far_ref, out_ref):
     step = p0_ref.shape[1]
     inner, outer = place_ref[0], place_ref[1]
     prefix = jnp.zeros((DH, DH), F32)
@@ -197,7 +193,7 @@
         after = after.astype(BF16)
         scores_grad = jnp.where(lower, dot(grad, value, 1, 1), 0.0).astype(BF16)
         scores_grad_t = jnp.where(upper, dot(value, grad, 1, 1), 0.0).astype(BF16)
-        scores_t = scores_ref[d]
+        scores_t = jnp.where(upper, dot(key, query, 1, 1), 0.0).astype(BF16)
         grad_q = dot(scores_grad, key, 1, 0) + dot(grad, before, 1, 1)
         grad_k = dot(scores_grad_t, query, 1, 0) + dot(value, after, 1, 1)
         grad_v = dot(scores_t, grad, 1, 0) + dot(key, after, 1, 0)
@@ -225,7 +221,8 @@
     here = lax.axis_index("ctx")
     z = here // NY
     place = jnp.stack([z % ZG, z // ZG, here % NY, at // 2, at % 2]).astype(jnp.int32)
-    earlier = jnp.array(FAR, jnp.int32) < place[1]
+    slot = jnp.arange(nz // ZG, dtype=jnp.int32)
+    earlier = sum(jnp.where(slot == i, g, 0) for i, g in enumerate(FAR)) < place[1]
     grad_out, place, earlier = lax.optimization_barrier((grad_out, place, earlier))
 
     copies = call(
@@ -262,9 +259,9 @@
         shares.append(lax.ppermute(mine, "tp", [(t, (t + 2 * d) % tp) for t in range(tp)]))
     swap = [(t, t ^ 1) for t in range(tp)]
     shares = shares + [lax.ppermute(share, "tp", swap) for share in shares]
-    key_states, scores = call(
+    key_states = call(
         key_kernel,
-        [shape((NY, DH, DH), F32), shape((NY, step, step))],
+        shape((NY, DH, DH), F32),
         4 * tokens * DH * (DH + step),
         2 * 1024 * 1024,
     )(*packed)
@@ -274,10 +271,10 @@
         2 * tokens * depth * width,
         4 * 1024 * 1024,
         smem=(0,),
-        hbm=range(1, 2 * NX + 1),
+        hbm=(2 * NX + 1,),
         anywhere=(2 * NX + 2,),
-        scratch=[pltpu.VMEM((NX, tokens, 2 * DH), BF16), pltpu.SemaphoreType.DMA((NY, 2 * NX))],
-    )(place, *shares, weight, scores)
+        scratch=[pltpu.VMEM((NX, depth // NX, width), BF16), pltpu.SemaphoreType.DMA((NX,))],
+    )(place, *shares, weight, key_states)
     parts = exchange(parts, y_line)
     grads, query_states, copies = call(
         state_kernel,
@@ -295,7 +292,7 @@
         8 * 2 * tokens * step * DH,
         3 * 1024 * 1024,
         smem=(0,),
-    )(place, *packed, grads, key_states, query_states, scores, near, far)
+    )(place, *packed, grads, key_states, query_states, near, far)
     result = exchange(result, y_line)
     out = shape((step, width))
     return tuple(call(unpack_kernel, [out, out, out], 0, 6 * step * width * 2)(result))

time: 130 us -> 130 us (level)
  the two profiles are of different devices: /device:TPU:42 before, /device:TPU:44 now
where the time goes in v6:
time: 130 us; the launch traced here: 129 us
  blocking collectives  55.1 us (42%)
  starting transfers between devices  43 us (33%)
  waiting for transfers between devices  19.1 us (15%)
  Pallas kernels  10.8 us (8%)
    all_to_all x4, blocking collectives, exchange(): return lax.all_to_all(pieces, 'ctx', 0, 0, axis_index_groups=group)  55.1 us
    all_to_all x1, starting transfers between devices, exchange(): return lax.all_to_all(pieces, 'ctx', 0, 0, axis_index_groups=group)  15.2 us
    pallas_call x8, Pallas kernels, run(): pl.pallas_call(kernel, out_shape=out_shape, in_specs=specs, out_specs=out...  10.8 us
    ppermute x3, starting transfers between devices, local(): packed[d] = lax.ppermute(packed[d], 'ctx', turn)  10.7 us
    ppermute x3, waiting for transfers between devices, local(): packed[d] = lax.ppermute(packed[d], 'ctx', turn)  9.03 us
    ppermute x3, starting transfers between devices, local(): lax.ppermute(mine, 'tp', [(t, (t + 2 * d) % tp) for t in range(tp)])  9 us
    ppermute x4, starting transfers between devices, local(): shares = shares + [lax.ppermute(share, 'tp', swap) for share in shares]  8.17 us
    all_to_all x1, waiting for transfers between devices, exchange(): return lax.all_to_all(pieces, 'ctx', 0, 0, axis_index_groups=group)  4.69 us
  transfers between devices with their start and end apart: 11, of which 7 were waited for; matrix products, arithmetic and copies ran while one was open for 0% of the time, Pallas kernels for 2%

profile of v6, /device:TPU:44, one launch (start us, length us, event | category | flops | bytes accessed | tf_op | source)
XLA Modules:
  0.0 129.0 jit_solution(13910144764385525754)
XLA Ops:
  0.6 2.0 %shard_map.76 = bf16[16,64,512]{2,1,0:T(8,128)(2,1)} custom-call(bf16[64,512]{1,0:T(8,128)(2,1)} %w_ref.1), custom_call_target="tpu_custom_call" | custom-call | bytes 1048576 | tf_op jit(solution)/shard_map/pallas_call | solution.py:45
  2.6 15.2 %all-to-all-start = ((bf16[16,64,512]{2,1,0:T(8,128)(2,1)}), bf16[16,64,512]{2,1,0:T(8,128)(2,1)}, u32[]{:S(2)}, u32[]{:S(2)}) async-start(bf16[16,64,512]{2,1,0:T(8,128)(2,1)} %shard_map.76), calls=%async_computation | async-start | bytes 2097152 | tf_op jit(solution)/shard_map/all_to_all | solution.py:31
  17.9 0.1 stack.23.place_ref.refs_0_
  17.9 1.9 %shard_map.77 = (bf16[4,256,128]{2,1,0:T(8,128)(2,1)S(1)}, bf16[4,256,128]{2,1,0:T(8,128)(2,1)S(1)}, bf16[4,256,128]{2,1,0:T(8,128)(2,1)S(1)}, bf16[4,256,128]{2,1,0:T(8,128)(2,1)S(1)}) custom-call(s32[5]{0:T(128)S(1)} %stack.23.place_ref.refs_0_, bf16[256,512]{1,0:T(8,128)(2,1)} %q_ref.1, bf16[256,512]{1,0:T(8,128)(2,1)} %k_ref.1, bf16[256,512]{1,0:T(8,128)(2,1)} %v_ref.1, ...), custom_call_target="tpu_custom_call" | custom-call | bytes 2097152 | tf_op jit(solution)/shard_map/pallas_call | solution.py:45
  19.8 3.5 %collective-permute-start = (bf16[4,256,128]{2,1,0:T(8,128)(2,1)S(1)}, bf16[4,256,128]{2,1,0:T(8,128)(2,1)S(1)}, u32[]{:S(2)}, u32[]{:S(2)}) collective-permute-start(bf16[4,256,128]{2,1,0:T(8,128)(2,1)S(1)} %get-tuple-element.18), channel_id=1, source_target_pairs={{0,8},{8,16},{16,24},{24,0},{32,40},{40,48},{48,56},{56,32},{64,72... | collective-permute-start | bytes 786440 | tf_op jit(solution)/shard_map/ppermute | solution.py:255
  23.3 2.8 %collective-permute-start.1 = (bf16[4,256,128]{2,1,0:T(8,128)(2,1)S(1)}, bf16[4,256,128]{2,1,0:T(8,128)(2,1)S(1)}, u32[]{:S(2)}, u32[]{:S(2)}) collective-permute-start(bf16[4,256,128]{2,1,0:T(8,128)(2,1)S(1)} %get-tuple-element.19), channel_id=1, source_target_pairs={{0,16},{8,24},{16,0},{24,8},{32,48},{40,56},{48,32},{56,40},{64,80... | collective-permute-start | bytes 786440 | tf_op jit(solution)/shard_map/ppermute | solution.py:255
  26.2 4.3 %collective-permute-start.2 = (bf16[4,256,128]{2,1,0:T(8,128)(2,1)S(1)}, bf16[4,256,128]{2,1,0:T(8,128)(2,1)S(1)}, u32[]{:S(2)}, u32[]{:S(2)}) collective-permute-start(bf16[4,256,128]{2,1,0:T(8,128)(2,1)S(1)} %get-tuple-element.20), channel_id=1, source_target_pairs={{0,24},{8,0},{16,8},{24,16},{32,56},{40,32},{48,40},{56,48},{64,88... | collective-permute-start | bytes 786440 | tf_op jit(solution)/shard_map/ppermute | solution.py:255
  30.5 0.0 collective-permute-done.refs_1_.p1_ref.refs_2_
  30.5 5.5 %collective-permute-done.1.refs_2_.p2_ref.refs_3_ = bf16[4,256,128]{2,1,0:T(8,128)(2,1)S(1)} collective-permute-done((bf16[4,256,128]{2,1,0:T(8,128)(2,1)S(1)}, bf16[4,256,128]{2,1,0:T(8,128)(2,1)S(1)}, u32[]{:S(2)}, u32[]{:S(2)}) %collective-permute-start.1) | collective-permute-done | bytes 262176 | tf_op jit(solution)/shard_map/ppermute | solution.py:255
  36.0 3.5 %collective-permute-done.2.refs_3_.p3_ref.refs_4_ = bf16[4,256,128]{2,1,0:T(8,128)(2,1)S(1)} collective-permute-done((bf16[4,256,128]{2,1,0:T(8,128)(2,1)S(1)}, bf16[4,256,128]{2,1,0:T(8,128)(2,1)S(1)}, u32[]{:S(2)}, u32[]{:S(2)}) %collective-permute-start.2) | collective-permute-done | bytes 262176 | tf_op jit(solution)/shard_map/ppermute | solution.py:255
  39.6 2.4 %collective-permute-start.5 = (bf16[1024,128]{1,0:T(8,128)(2,1)S(1)}, bf16[1024,128]{1,0:T(8,128)(2,1)S(1)}, u32[]{:S(2)}, u32[]{:S(2)}) collective-permute-start(bf16[1024,128]{1,0:T(8,128)(2,1)S(1)} %shard_map.78.refs_0_), channel_id=1, source_target_pairs={{0,6},{1,7},{2,0},{3,1},{4,2},{5,3},{6,4},{7,5},{8,14},{9,15},{10,... | collective-permute-start | bytes 786440 | tf_op jit(solution)/shard_map/ppermute | solution.py:259
  42.0 4.6 %collective-permute-start.4 = (bf16[1024,128]{1,0:T(8,128)(2,1)S(1)}, bf16[1024,128]{1,0:T(8,128)(2,1)S(1)}, u32[]{:S(2)}, u32[]{:S(2)}) collective-permute-start(bf16[1024,128]{1,0:T(8,128)(2,1)S(1)} %shard_map.78.refs_0_), channel_id=1, source_target_pairs={{0,4},{1,5},{2,6},{3,7},{4,0},{5,1},{6,2},{7,3},{8,12},{9,13},{10,... | collective-permute-start | bytes 786440 | tf_op jit(solution)/shard_map/ppermute | solution.py:259
  46.7 1.9 %collective-permute-start.3 = (bf16[1024,128]{1,0:T(8,128)(2,1)S(1)}, bf16[1024,128]{1,0:T(8,128)(2,1)S(1)}, u32[]{:S(2)}, u32[]{:S(2)}) collective-permute-start(bf16[1024,128]{1,0:T(8,128)(2,1)S(1)} %shard_map.78.refs_0_), channel_id=1, source_target_pairs={{0,2},{1,3},{2,4},{3,5},{4,6},{5,7},{6,0},{7,1},{8,10},{9,11},{10,... | collective-permute-start | bytes 786440 | tf_op jit(solution)/shard_map/ppermute | solution.py:259
  48.6 1.9 %collective-permute-start.6 = (bf16[1024,128]{1,0:T(8,128)(2,1)S(1)}, bf16[1024,128]{1,0:T(8,128)(2,1)S(1)}, u32[]{:S(2)}, u32[]{:S(2)}) collective-permute-start(bf16[1024,128]{1,0:T(8,128)(2,1)S(1)} %shard_map.78.refs_0_), channel_id=1, source_target_pairs={{0,1},{1,0},{2,3},{3,2},{4,5},{5,4},{6,7},{7,6},{8,9},{9,8},{10,11... | collective-permute-start | bytes 786440 | tf_op jit(solution)/shard_map/ppermute | solution.py:261
  50.5 0.1 collective-permute-done.5.refs_3_
  50.6 2.3 %collective-permute-start.9 = (bf16[1024,128]{1,0:T(8,128)(2,1)S(1)}, bf16[1024,128]{1,0:T(8,128)(2,1)S(1)}, u32[]{:S(2)}, u32[]{:S(2)}) collective-permute-start(bf16[1024,128]{1,0:T(8,128)(2,1)S(1)} %collective-permute-done.5.refs_3_), channel_id=1, source_target_pairs={{0,1},{1,0},{2,3},{3,2},{4,5},{5,4},{6,7},{7,6},{8,9},{9,8},{10,11... | collective-permute-start | bytes 786440 | tf_op jit(solution)/shard_map/ppermute | solution.py:261
  52.9 1.7 %collective-permute-done.4.refs_2_ = bf16[1024,128]{1,0:T(8,128)(2,1)S(1)} collective-permute-done((bf16[1024,128]{1,0:T(8,128)(2,1)S(1)}, bf16[1024,128]{1,0:T(8,128)(2,1)S(1)}, u32[]{:S(2)}, u32[]{:S(2)}) %collective-permute-start.4) | collective-permute-done | bytes 262176 | tf_op jit(solution)/shard_map/ppermute | solution.py:259
  54.6 1.9 %collective-permute-start.8 = (bf16[1024,128]{1,0:T(8,128)(2,1)S(1)}, bf16[1024,128]{1,0:T(8,128)(2,1)S(1)}, u32[]{:S(2)}, u32[]{:S(2)}) collective-permute-start(bf16[1024,128]{1,0:T(8,128)(2,1)S(1)} %collective-permute-done.4.refs_2_), channel_id=1, source_target_pairs={{0,1},{1,0},{2,3},{3,2},{4,5},{5,4},{6,7},{7,6},{8,9},{9,8},{10,11... | collective-permute-start | bytes 786440 | tf_op jit(solution)/shard_map/ppermute | solution.py:261
  56.5 2.5 %collective-permute-done.3.refs_1_ = bf16[1024,128]{1,0:T(8,128)(2,1)S(1)} collective-permute-done((bf16[1024,128]{1,0:T(8,128)(2,1)S(1)}, bf16[1024,128]{1,0:T(8,128)(2,1)S(1)}, u32[]{:S(2)}, u32[]{:S(2)}) %collective-permute-start.3) | collective-permute-done | bytes 262176 | tf_op jit(solution)/shard_map/ppermute | solution.py:259
  59.1 2.0 %collective-permute-start.7 = (bf16[1024,128]{1,0:T(8,128)(2,1)S(1)}, bf16[1024,128]{1,0:T(8,128)(2,1)S(1)}, u32[]{:S(2)}, u32[]{:S(2)}) collective-permute-start(bf16[1024,128]{1,0:T(8,128)(2,1)S(1)} %collective-permute-done.3.refs_1_), channel_id=1, source_target_pairs={{0,1},{1,0},{2,3},{3,2},{4,5},{5,4},{6,7},{7,6},{8,9},{9,8},{10,11... | collective-permute-start | bytes 786440 | tf_op jit(solution)/shard_map/ppermute | solution.py:261
  61.1 0.3 shard_map.79.refs_9_.key_ref.refs_6_
  61.4 0.0 collective-permute-done.6.refs_4_
  61.4 0.0 collective-permute-done.9.refs_7_
  61.4 0.0 collective-permute-done.8.refs_6_
  61.4 1.1 collective-permute-done.7.refs_5_
  62.5 4.7 %all-to-all-done = bf16[16,64,512]{2,1,0:T(8,128)(2,1)} async-done(((bf16[16,64,512]{2,1,0:T(8,128)(2,1)}), bf16[16,64,512]{2,1,0:T(8,128)(2,1)}, u32[]{:S(2)}, u32[]{:S(2)}) %all-to-all-start) | async-done | bytes 1048608 | tf_op jit(solution)/shard_map/all_to_all | solution.py:31
  67.2 3.0 %shard_map.80 = bf16[4,1024,128]{2,1,0:T(8,128)(2,1)S(1)} custom-call(s32[5]{0:T(128)S(1)} %stack.23.place_ref.refs_0_, bf16[1024,128]{1,0:T(8,128)(2,1)S(1)} %shard_map.78.refs_0_, bf16[1024,128]{1,0:T(8,128)(2,1)S(1)} %collective-permute-done.3.refs_1_, bf16[1024,128]{1,0:T(8,128)(2,1)S(1)} %collective-permute-done.4.refs_2_, ...), custom_call_target="tpu_custom_call" | custom-call | flops 1073741824 | bytes 4194304 | tf_op jit(solution)/shard_map/pallas_call | solution.py:45
  70.2 13.4 %all_to_all.25.part_ref = bf16[4,1024,128]{2,1,0:T(8,128)(2,1)S(1)} all-to-all(bf16[4,1024,128]{2,1,0:T(8,128)(2,1)S(1)} %shard_map.80), channel_id=1, replica_groups={{16,8,24,0},{48,40,56,32},{80,72,88,64},{112,104,120,96},{144,136,152,1..., dimensions={0} | all-to-all | bytes 2097152 | tf_op jit(solution)/shard_map/all_to_all | solution.py:31
  83.6 0.8 shard_map.81
  84.5 10.7 %all_to_all.26.refs_8_ = bf16[4,2,128,128]{3,2,1,0:T(8,128)(2,1)S(1)} all-to-all(bf16[4,2,128,128]{3,2,1,0:T(8,128)(2,1)S(1)} %get-tuple-element.23), channel_id=1, replica_groups={{64,32,96,0},{72,40,104,8},{80,48,112,16},{88,56,120,24},{192,160,224,1..., dimensions={0} | all-to-all | bytes 524288 | tf_op jit(solution)/shard_map/all_to_all | solution.py:31
  95.3 0.1 broadcast_select_fusion
  95.4 18.4 %all_to_all.27.refs_9_ = bf16[4,128,128]{2,1,0:T(8,128)(2,1)S(1)} all-to-all(bf16[4,128,128]{2,1,0:T(8,128)(2,1)S(1)} %broadcast_select_fusion), channel_id=1, replica_groups={{256,128,384,0},{264,136,392,8},{272,144,400,16},{280,152,408,24},{288,..., dimensions={0} | all-to-all | bytes 262144 | tf_op jit(solution)/shard_map/all_to_all | solution.py:31
  113.8 1.8 %shard_map.82 = bf16[4,3,256,128]{3,2,1,0:T(8,128)(2,1)S(1)} custom-call(s32[5]{0:T(128)S(1)} %stack.23.place_ref.refs_0_, bf16[4,256,128]{2,1,0:T(8,128)(2,1)S(1)} %get-tuple-element.17.refs_0_.p0_ref.refs_1_, bf16[4,256,128]{2,1,0:T(8,128)(2,1)S(1)} %collective-permute-done.refs_1_.p1_ref.refs_2_, ...), custom_call_target="tpu_custom_call" | custom-call | flops 536870912 | bytes 3145728 | tf_op jit(solution)/shard_map/pallas_call | solution.py:45
  115.6 12.5 %all_to_all.28.in_ref = bf16[4,3,256,128]{3,2,1,0:T(8,128)(2,1)S(1)} all-to-all(bf16[4,3,256,128]{3,2,1,0:T(8,128)(2,1)S(1)} %shard_map.82), channel_id=1, replica_groups={{16,8,24,0},{48,40,56,32},{80,72,88,64},{112,104,120,96},{144,136,152,1..., dimensions={0} | all-to-all | bytes 1572864 | tf_op jit(solution)/shard_map/all_to_all | solution.py:31
  128.0 1.0 shard_map.83
  (4 shorter events, 0.1 us)
Async XLA Ops:
  2.6 64.6 %all-to-all-start = ((bf16[16,64,512]{2,1,0:T(8,128)(2,1)}), bf16[16,64,512]{2,1,0:T(8,128)(2,1)}, u32[]{:S(2)}, u32[]{:S(2)}) async-start(bf16[16,64,512]{2,1,0:T(8,128)(2,1)} %shard_map.76), calls=%async_computation | async-start | bytes 2097152 | tf_op jit(solution)/shard_map/all_to_all | solution.py:31
  19.8 10.7 %collective-permute-start = (bf16[4,256,128]{2,1,0:T(8,128)(2,1)S(1)}, bf16[4,256,128]{2,1,0:T(8,128)(2,1)S(1)}, u32[]{:S(2)}, u32[]{:S(2)}) collective-permute-start(bf16[4,256,128]{2,1,0:T(8,128)(2,1)S(1)} %get-tuple-element.18), channel_id=1, source_target_pairs={{0,8},{8,16},{16,24},{24,0},{32,40},{40,48},{48,56},{56,32},{64,72... | collective-permute-start | bytes 786440 | tf_op jit(solution)/shard_map/ppermute | solution.py:255
  23.3 12.7 %collective-permute-start.1 = (bf16[4,256,128]{2,1,0:T(8,128)(2,1)S(1)}, bf16[4,256,128]{2,1,0:T(8,128)(2,1)S(1)}, u32[]{:S(2)}, u32[]{:S(2)}) collective-permute-start(bf16[4,256,128]{2,1,0:T(8,128)(2,1)S(1)} %get-tuple-element.19), channel_id=1, source_target_pairs={{0,16},{8,24},{16,0},{24,8},{32,48},{40,56},{48,32},{56,40},{64,80... | collective-permute-start | bytes 786440 | tf_op jit(solution)/shard_map/ppermute | solution.py:255
  26.2 13.4 %collective-permute-start.2 = (bf16[4,256,128]{2,1,0:T(8,128)(2,1)S(1)}, bf16[4,256,128]{2,1,0:T(8,128)(2,1)S(1)}, u32[]{:S(2)}, u32[]{:S(2)}) collective-permute-start(bf16[4,256,128]{2,1,0:T(8,128)(2,1)S(1)} %get-tuple-element.20), channel_id=1, source_target_pairs={{0,24},{8,0},{16,8},{24,16},{32,56},{40,32},{48,40},{56,48},{64,88... | collective-permute-start | bytes 786440 | tf_op jit(solution)/shard_map/ppermute | solution.py:255
  39.6 11.0 %collective-permute-start.5 = (bf16[1024,128]{1,0:T(8,128)(2,1)S(1)}, bf16[1024,128]{1,0:T(8,128)(2,1)S(1)}, u32[]{:S(2)}, u32[]{:S(2)}) collective-permute-start(bf16[1024,128]{1,0:T(8,128)(2,1)S(1)} %shard_map.78.refs_0_), channel_id=1, source_target_pairs={{0,6},{1,7},{2,0},{3,1},{4,2},{5,3},{6,4},{7,5},{8,14},{9,15},{10,... | collective-permute-start | bytes 786440 | tf_op jit(solution)/shard_map/ppermute | solution.py:259
  42.0 12.6 %collective-permute-start.4 = (bf16[1024,128]{1,0:T(8,128)(2,1)S(1)}, bf16[1024,128]{1,0:T(8,128)(2,1)S(1)}, u32[]{:S(2)}, u32[]{:S(2)}) collective-permute-start(bf16[1024,128]{1,0:T(8,128)(2,1)S(1)} %shard_map.78.refs_0_), channel_id=1, source_target_pairs={{0,4},{1,5},{2,6},{3,7},{4,0},{5,1},{6,2},{7,3},{8,12},{9,13},{10,... | collective-permute-start | bytes 786440 | tf_op jit(solution)/shard_map/ppermute | solution.py:259
  46.7 12.4 %collective-permute-start.3 = (bf16[1024,128]{1,0:T(8,128)(2,1)S(1)}, bf16[1024,128]{1,0:T(8,128)(2,1)S(1)}, u32[]{:S(2)}, u32[]{:S(2)}) collective-permute-start(bf16[1024,128]{1,0:T(8,128)(2,1)S(1)} %shard_map.78.refs_0_), channel_id=1, source_target_pairs={{0,2},{1,3},{2,4},{3,5},{4,6},{5,7},{6,0},{7,1},{8,10},{9,11},{10,... | collective-permute-start | bytes 786440 | tf_op jit(solution)/shard_map/ppermute | solution.py:259
  48.6 12.8 %collective-permute-start.6 = (bf16[1024,128]{1,0:T(8,128)(2,1)S(1)}, bf16[1024,128]{1,0:T(8,128)(2,1)S(1)}, u32[]{:S(2)}, u32[]{:S(2)}) collective-permute-start(bf16[1024,128]{1,0:T(8,128)(2,1)S(1)} %shard_map.78.refs_0_), channel_id=1, source_target_pairs={{0,1},{1,0},{2,3},{3,2},{4,5},{5,4},{6,7},{7,6},{8,9},{9,8},{10,11... | collective-permute-start | bytes 786440 | tf_op jit(solution)/shard_map/ppermute | solution.py:261
  50.6 10.8 %collective-permute-start.9 = (bf16[1024,128]{1,0:T(8,128)(2,1)S(1)}, bf16[1024,128]{1,0:T(8,128)(2,1)S(1)}, u32[]{:S(2)}, u32[]{:S(2)}) collective-permute-start(bf16[1024,128]{1,0:T(8,128)(2,1)S(1)} %collective-permute-done.5.refs_3_), channel_id=1, source_target_pairs={{0,1},{1,0},{2,3},{3,2},{4,5},{5,4},{6,7},{7,6},{8,9},{9,8},{10,11... | collective-permute-start | bytes 786440 | tf_op jit(solution)/shard_map/ppermute | solution.py:261
  54.6 6.8 %collective-permute-start.8 = (bf16[1024,128]{1,0:T(8,128)(2,1)S(1)}, bf16[1024,128]{1,0:T(8,128)(2,1)S(1)}, u32[]{:S(2)}, u32[]{:S(2)}) collective-permute-start(bf16[1024,128]{1,0:T(8,128)(2,1)S(1)} %collective-permute-done.4.refs_2_), channel_id=1, source_target_pairs={{0,1},{1,0},{2,3},{3,2},{4,5},{5,4},{6,7},{7,6},{8,9},{9,8},{10,11... | collective-permute-start | bytes 786440 | tf_op jit(solution)/shard_map/ppermute | solution.py:261
  59.1 3.4 %collective-permute-start.7 = (bf16[1024,128]{1,0:T(8,128)(2,1)S(1)}, bf16[1024,128]{1,0:T(8,128)(2,1)S(1)}, u32[]{:S(2)}, u32[]{:S(2)}) collective-permute-start(bf16[1024,128]{1,0:T(8,128)(2,1)S(1)} %collective-permute-done.3.refs_1_), channel_id=1, source_target_pairs={{0,1},{1,0},{2,3},{3,2},{4,5},{5,4},{6,7},{7,6},{8,9},{9,8},{10,11... | collective-permute-start | bytes 786440 | tf_op jit(solution)/shard_map/ppermute | solution.py:261

commit v7 on v6

--- a/solution.py
+++ b/solution.py
@@ -21,7 +21,7 @@
 def groups(ctx):
     nz = ctx // NY
     y_line = [[z * NY + y for y in LINE] for z in range(nz)]
-    z_line = [[z * NY + y for z in range(nz)] for y in range(NY)]
+    z_line = [[z * NY + y for z in range(p, nz, 2)] for p in range(2) for y in range(NY)]
     z_near = [[(g * ZG + i) * NY + y for i in NEAR] for g in range(nz // ZG) for y in range(NY)]
     z_far = [[(g * ZG + i) * NY + y for g in FAR] for i in range(ZG) for y in range(NY)]
     return y_line, z_line, z_near, z_far
@@ -110,17 +110,23 @@
 
 
 def product_kernel(place_ref, *refs):
-    weight_ref, early_ref, out_ref, weight, sems = refs[2 * NX :]
+    same_ref, next_ref, early_ref, out_ref, weight, sems = refs[2 * NX :]
     tokens, depth = refs[0].shape
     step = tokens // NY
     core = place_ref[4]
+    odd = lax.rem(place_ref[0], 2)
+    half = depth // 2
     loads = []
     for d in range(NX):
         chip = lax.rem(place_ref[3] + (NX - d), NX)
-        start = pl.multiple_of(chip * 2 * depth, 2 * depth)
-        load = pltpu.make_async_copy(weight_ref.at[pl.ds(start, 2 * depth), :], weight.at[d], sems.at[d])
-        load.start()
-        loads.append(load)
+        slab = []
+        for c in range(2):
+            for i, (ref, at) in enumerate(((same_ref, odd), (next_ref, 1 - odd))):
+                rows = pl.ds(pl.multiple_of(c * depth + at * half, half), half)
+                slab.append(pltpu.make_async_copy(ref.at[chip * 2 + c], weight.at[d, rows, :], sems.at[d, c, i]))
+        for load in slab:
+            load.start()
+        loads.append(slab)
     own = pl.multiple_of(core * depth, depth)
     far = pl.multiple_of((1 - core) * depth, depth)
     for t in range(NY):
@@ -128,7 +134,8 @@
         tile = slice(t * step, (t + 1) * step)
         for d in range(NX):
             if t == 0:
-                loads[d].wait()
+                for load in loads[d]:
+                    load.wait()
             held = jnp.concatenate([refs[d][tile, :], refs[NX + d][tile, :]], axis=1)
             rows = jnp.concatenate([weight[d, pl.ds(own, depth), :], weight[d, pl.ds(far, depth), :]], axis=0)
             part = part + dot(held, rows, 1, 0)
@@ -227,14 +234,15 @@
 
     copies = call(
         copies_kernel,
-        pltpu.HBM((nz,) + out_weight.shape, BF16),
+        pltpu.HBM((nz // 2,) + out_weight.shape, BF16),
         0,
         2 * depth * width,
         hbm=(0,),
         out_hbm=True,
-        scratch=[pltpu.VMEM(out_weight.shape, BF16), pltpu.SemaphoreType.DMA, pltpu.SemaphoreType.DMA((nz,))],
+        scratch=[pltpu.VMEM(out_weight.shape, BF16), pltpu.SemaphoreType.DMA, pltpu.SemaphoreType.DMA((nz // 2,))],
     )(out_weight)
-    weight = exchange(copies, z_line).reshape(depth, width)
+    weight = exchange(copies, z_line)
+    beside = lax.ppermute(weight, "ctx", [(i, (i // NY ^ 1) * NY + i % NY) for i in range(ctx)])
     grad_out, copies = lax.optimization_barrier((grad_out, copies))
     turns = {d: [(i, i // NY * NY + (i + d) % NY) for i in range(ctx)] for d in (1, 3, 2)}
     packed = call(
@@ -271,10 +279,10 @@
         2 * tokens * depth * width,
         4 * 1024 * 1024,
         smem=(0,),
-        hbm=(2 * NX + 1,),
-        anywhere=(2 * NX + 2,),
-        scratch=[pltpu.VMEM((NX, depth // NX, width), BF16), pltpu.SemaphoreType.DMA((NX,))],
-    )(place, *shares, weight, key_states)
+        hbm=(2 * NX + 1, 2 * NX + 2),
+        anywhere=(2 * NX + 3,),
+        scratch=[pltpu.VMEM((NX, depth // NX, width), BF16), pltpu.SemaphoreType.DMA((NX, 2, 2))],
+    )(place, *shares, weight, beside, key_states)
     parts = exchange(parts, y_line)
     grads, query_states, copies = call(
         state_kernel,

time: 130 us -> 130 us (level)
  the two profiles are of different devices: /device:TPU:44 before, /device:TPU:14 now
where the time goes in v7:
time: 130 us; the launch traced here: 129 us
  blocking collectives  56.8 us (44%)
  starting transfers between devices  46.6 us (36%)
  waiting for transfers between devices  12.8 us (10%)
  Pallas kernels  10.6 us (8%)
    all_to_all x4, blocking collectives, exchange(): return lax.all_to_all(pieces, 'ctx', 0, 0, axis_index_groups=group)  56.8 us
    all_to_all x1, starting transfers between devices, exchange(): return lax.all_to_all(pieces, 'ctx', 0, 0, axis_index_groups=group)  15.1 us
    ppermute x3, starting transfers between devices, local(): packed[d] = lax.ppermute(packed[d], 'ctx', turn)  10.7 us
    pallas_call x8, Pallas kernels, run(): pl.pallas_call(kernel, out_shape=out_shape, in_specs=specs, out_specs=out...  10.6 us
    ppermute x3, starting transfers between devices, local(): lax.ppermute(mine, 'tp', [(t, (t + 2 * d) % tp) for t in range(tp)])  9.76 us
    ppermute x3, waiting for transfers between devices, local(): packed[d] = lax.ppermute(packed[d], 'ctx', turn)  9.31 us
    ppermute x4, starting transfers between devices, local(): shares = shares + [lax.ppermute(share, 'tp', swap) for share in shares]  8.16 us
    ppermute x1, starting transfers between devices, local(): lax.ppermute(weight, 'ctx', [(i, (i // NY ^ 1) * NY + i % NY) for i in ra...  2.93 us
  transfers between devices with their start and end apart: 12, of which 4 were waited for; matrix products, arithmetic and copies ran while one was open for 0% of the time, Pallas kernels for 2%

profile of v7, /device:TPU:14, one launch (start us, length us, event | category | flops | bytes accessed | tf_op | source)
XLA Modules:
  0.0 128.7 jit_solution(4702303935364483644)
XLA Ops:
  0.6 1.7 %shard_map.76 = bf16[8,64,512]{2,1,0:T(8,128)(2,1)} custom-call(bf16[64,512]{1,0:T(8,128)(2,1)} %w_ref.1), custom_call_target="tpu_custom_call" | custom-call | bytes 1048576 | tf_op jit(solution)/shard_map/pallas_call | solution.py:45
  2.3 15.1 %all-to-all-start = ((bf16[8,64,512]{2,1,0:T(8,128)(2,1)}), bf16[8,64,512]{2,1,0:T(8,128)(2,1)S(1)}, u32[]{:S(2)}, u32[]{:S(2)}) async-start(bf16[8,64,512]{2,1,0:T(8,128)(2,1)} %shard_map.76), calls=%async_computation | async-start | bytes 1048576 | tf_op jit(solution)/shard_map/all_to_all | solution.py:31
  17.4 0.1 stack.23.place_ref.refs_0_
  17.5 1.9 %shard_map.77 = (bf16[4,256,128]{2,1,0:T(8,128)(2,1)S(1)}, bf16[4,256,128]{2,1,0:T(8,128)(2,1)S(1)}, bf16[4,256,128]{2,1,0:T(8,128)(2,1)S(1)}, bf16[4,256,128]{2,1,0:T(8,128)(2,1)S(1)}) custom-call(s32[5]{0:T(128)S(1)} %stack.23.place_ref.refs_0_, bf16[256,512]{1,0:T(8,128)(2,1)} %q_ref.1, bf16[256,512]{1,0:T(8,128)(2,1)} %k_ref.1, bf16[256,512]{1,0:T(8,128)(2,1)} %v_ref.1, ...), custom_call_target="tpu_custom_call" | custom-call | bytes 2097152 | tf_op jit(solution)/shard_map/pallas_call | solution.py:45
  19.4 3.5 %collective-permute-start = (bf16[4,256,128]{2,1,0:T(8,128)(2,1)S(1)}, bf16[4,256,128]{2,1,0:T(8,128)(2,1)S(1)}, u32[]{:S(2)}, u32[]{:S(2)}) collective-permute-start(bf16[4,256,128]{2,1,0:T(8,128)(2,1)S(1)} %get-tuple-element.18), channel_id=1, source_target_pairs={{0,8},{8,16},{16,24},{24,0},{32,40},{40,48},{48,56},{56,32},{64,72... | collective-permute-start | bytes 786440 | tf_op jit(solution)/shard_map/ppermute | solution.py:263
  22.9 2.8 %collective-permute-start.1 = (bf16[4,256,128]{2,1,0:T(8,128)(2,1)S(1)}, bf16[4,256,128]{2,1,0:T(8,128)(2,1)S(1)}, u32[]{:S(2)}, u32[]{:S(2)}) collective-permute-start(bf16[4,256,128]{2,1,0:T(8,128)(2,1)S(1)} %get-tuple-element.19), channel_id=1, source_target_pairs={{0,16},{8,24},{16,0},{24,8},{32,48},{40,56},{48,32},{56,40},{64,80... | collective-permute-start | bytes 786440 | tf_op jit(solution)/shard_map/ppermute | solution.py:263
  25.8 4.3 %collective-permute-start.2 = (bf16[4,256,128]{2,1,0:T(8,128)(2,1)S(1)}, bf16[4,256,128]{2,1,0:T(8,128)(2,1)S(1)}, u32[]{:S(2)}, u32[]{:S(2)}) collective-permute-start(bf16[4,256,128]{2,1,0:T(8,128)(2,1)S(1)} %get-tuple-element.20), channel_id=1, source_target_pairs={{0,24},{8,0},{16,8},{24,16},{32,56},{40,32},{48,40},{56,48},{64,88... | collective-permute-start | bytes 786440 | tf_op jit(solution)/shard_map/ppermute | solution.py:263
  30.1 0.0 collective-permute-done.refs_1_.p1_ref.refs_2_
  30.1 5.5 %collective-permute-done.1.refs_2_.p2_ref.refs_3_ = bf16[4,256,128]{2,1,0:T(8,128)(2,1)S(1)} collective-permute-done((bf16[4,256,128]{2,1,0:T(8,128)(2,1)S(1)}, bf16[4,256,128]{2,1,0:T(8,128)(2,1)S(1)}, u32[]{:S(2)}, u32[]{:S(2)}) %collective-permute-start.1) | collective-permute-done | bytes 262176 | tf_op jit(solution)/shard_map/ppermute | solution.py:263
  35.6 3.8 %collective-permute-done.2.refs_3_.p3_ref.refs_4_ = bf16[4,256,128]{2,1,0:T(8,128)(2,1)S(1)} collective-permute-done((bf16[4,256,128]{2,1,0:T(8,128)(2,1)S(1)}, bf16[4,256,128]{2,1,0:T(8,128)(2,1)S(1)}, u32[]{:S(2)}, u32[]{:S(2)}) %collective-permute-start.2) | collective-permute-done | bytes 262176 | tf_op jit(solution)/shard_map/ppermute | solution.py:263
  39.4 2.7 %collective-permute-start.5 = (bf16[1024,128]{1,0:T(8,128)(2,1)S(1)}, bf16[1024,128]{1,0:T(8,128)(2,1)S(1)}, u32[]{:S(2)}, u32[]{:S(2)}) collective-permute-start(bf16[1024,128]{1,0:T(8,128)(2,1)S(1)} %shard_map.78.refs_0_), channel_id=1, source_target_pairs={{0,6},{1,7},{2,0},{3,1},{4,2},{5,3},{6,4},{7,5},{8,14},{9,15},{10,... | collective-permute-start | bytes 786440 | tf_op jit(solution)/shard_map/ppermute | solution.py:267
  42.2 3.0 %collective-permute-start.4 = (bf16[1024,128]{1,0:T(8,128)(2,1)S(1)}, bf16[1024,128]{1,0:T(8,128)(2,1)S(1)}, u32[]{:S(2)}, u32[]{:S(2)}) collective-permute-start(bf16[1024,128]{1,0:T(8,128)(2,1)S(1)} %shard_map.78.refs_0_), channel_id=1, source_target_pairs={{0,4},{1,5},{2,6},{3,7},{4,0},{5,1},{6,2},{7,3},{8,12},{9,13},{10,... | collective-permute-start | bytes 786440 | tf_op jit(solution)/shard_map/ppermute | solution.py:267
  45.2 4.0 %collective-permute-start.3 = (bf16[1024,128]{1,0:T(8,128)(2,1)S(1)}, bf16[1024,128]{1,0:T(8,128)(2,1)S(1)}, u32[]{:S(2)}, u32[]{:S(2)}) collective-permute-start(bf16[1024,128]{1,0:T(8,128)(2,1)S(1)} %shard_map.78.refs_0_), channel_id=1, source_target_pairs={{0,2},{1,3},{2,4},{3,5},{4,6},{5,7},{6,0},{7,1},{8,10},{9,11},{10,... | collective-permute-start | bytes 786440 | tf_op jit(solution)/shard_map/ppermute | solution.py:267
  49.2 0.0 all-to-all-done.refs_8_
  49.2 0.0 copy-start
  49.2 2.9 %collective-permute-start.10 = (bf16[8,64,512]{2,1,0:T(8,128)(2,1)S(1)}, bf16[8,64,512]{2,1,0:T(8,128)(2,1)S(1)}, u32[]{:S(2)}, u32[]{:S(2)}) collective-permute-start(bf16[8,64,512]{2,1,0:T(8,128)(2,1)S(1)} %all-to-all-done.refs_8_), channel_id=1, source_target_pairs={{0,32},{8,40},{16,48},{24,56},{32,0},{40,8},{48,16},{56,24},{64,96... | collective-permute-start | bytes 1572872 | tf_op jit(solution)/shard_map/ppermute | solution.py:245
  52.2 1.9 %collective-permute-start.6 = (bf16[1024,128]{1,0:T(8,128)(2,1)S(1)}, bf16[1024,128]{1,0:T(8,128)(2,1)S(1)}, u32[]{:S(2)}, u32[]{:S(2)}) collective-permute-start(bf16[1024,128]{1,0:T(8,128)(2,1)S(1)} %shard_map.78.refs_0_), channel_id=1, source_target_pairs={{0,1},{1,0},{2,3},{3,2},{4,5},{5,4},{6,7},{7,6},{8,9},{9,8},{10,11... | collective-permute-start | bytes 786440 | tf_op jit(solution)/shard_map/ppermute | solution.py:269
  54.1 2.3 %collective-permute-done.5.refs_3_ = bf16[1024,128]{1,0:T(8,128)(2,1)S(1)} collective-permute-done((bf16[1024,128]{1,0:T(8,128)(2,1)S(1)}, bf16[1024,128]{1,0:T(8,128)(2,1)S(1)}, u32[]{:S(2)}, u32[]{:S(2)}) %collective-permute-start.5) | collective-permute-done | bytes 262176 | tf_op jit(solution)/shard_map/ppermute | solution.py:267
  56.4 1.9 %collective-permute-start.9 = (bf16[1024,128]{1,0:T(8,128)(2,1)S(1)}, bf16[1024,128]{1,0:T(8,128)(2,1)S(1)}, u32[]{:S(2)}, u32[]{:S(2)}) collective-permute-start(bf16[1024,128]{1,0:T(8,128)(2,1)S(1)} %collective-permute-done.5.refs_3_), channel_id=1, source_target_pairs={{0,1},{1,0},{2,3},{3,2},{4,5},{5,4},{6,7},{7,6},{8,9},{9,8},{10,11... | collective-permute-start | bytes 786440 | tf_op jit(solution)/shard_map/ppermute | solution.py:269
  58.3 0.0 collective-permute-done.4.refs_2_
  58.3 2.4 %collective-permute-start.8 = (bf16[1024,128]{1,0:T(8,128)(2,1)S(1)}, bf16[1024,128]{1,0:T(8,128)(2,1)S(1)}, u32[]{:S(2)}, u32[]{:S(2)}) collective-permute-start(bf16[1024,128]{1,0:T(8,128)(2,1)S(1)} %collective-permute-done.4.refs_2_), channel_id=1, source_target_pairs={{0,1},{1,0},{2,3},{3,2},{4,5},{5,4},{6,7},{7,6},{8,9},{9,8},{10,11... | collective-permute-start | bytes 786440 | tf_op jit(solution)/shard_map/ppermute | solution.py:269
  60.7 0.0 collective-permute-done.3.refs_1_
  60.7 1.9 %collective-permute-start.7 = (bf16[1024,128]{1,0:T(8,128)(2,1)S(1)}, bf16[1024,128]{1,0:T(8,128)(2,1)S(1)}, u32[]{:S(2)}, u32[]{:S(2)}) collective-permute-start(bf16[1024,128]{1,0:T(8,128)(2,1)S(1)} %collective-permute-done.3.refs_1_), channel_id=1, source_target_pairs={{0,1},{1,0},{2,3},{3,2},{4,5},{5,4},{6,7},{7,6},{8,9},{9,8},{10,11... | collective-permute-start | bytes 786440 | tf_op jit(solution)/shard_map/ppermute | solution.py:269
  62.7 0.3 shard_map.79.refs_10_.key_ref.refs_6_
  63.0 0.0 copy-done
  63.0 0.0 collective-permute-done.6.refs_4_
  63.0 0.0 collective-permute-done.9.refs_7_
  63.0 0.0 collective-permute-done.8.refs_6_
  63.0 1.2 collective-permute-done.7.refs_5_
  64.2 0.0 collective-permute-done.10.refs_9_
  64.2 0.0 copy-start.1
  64.2 0.8 copy-done.1
  65.0 3.1 %shard_map.80 = bf16[4,1024,128]{2,1,0:T(8,128)(2,1)S(1)} custom-call(s32[5]{0:T(128)S(1)} %stack.23.place_ref.refs_0_, bf16[1024,128]{1,0:T(8,128)(2,1)S(1)} %shard_map.78.refs_0_, bf16[1024,128]{1,0:T(8,128)(2,1)S(1)} %collective-permute-done.3.refs_1_, bf16[1024,128]{1,0:T(8,128)(2,1)S(1)} %collective-permute-done.4.refs_2_, ...), custom_call_target="tpu_custom_call" | custom-call | flops 1073741824 | bytes 4194304 | tf_op jit(solution)/shard_map/pallas_call | solution.py:45
  68.1 17.0 %all_to_all.25.part_ref = bf16[4,1024,128]{2,1,0:T(8,128)(2,1)S(1)} all-to-all(bf16[4,1024,128]{2,1,0:T(8,128)(2,1)S(1)} %shard_map.80), channel_id=1, replica_groups={{16,8,24,0},{48,40,56,32},{80,72,88,64},{112,104,120,96},{144,136,152,1..., dimensions={0} | all-to-all | bytes 2097152 | tf_op jit(solution)/shard_map/all_to_all | solution.py:31
  85.2 0.8 shard_map.81
  86.0 10.1 %all_to_all.26.refs_8_ = bf16[4,2,128,128]{3,2,1,0:T(8,128)(2,1)S(1)} all-to-all(bf16[4,2,128,128]{3,2,1,0:T(8,128)(2,1)S(1)} %get-tuple-element.23), channel_id=1, replica_groups={{64,32,96,0},{72,40,104,8},{80,48,112,16},{88,56,120,24},{192,160,224,1..., dimensions={0} | all-to-all | bytes 524288 | tf_op jit(solution)/shard_map/all_to_all | solution.py:31
  96.2 0.1 broadcast_select_fusion
  96.2 15.7 %all_to_all.27.refs_9_ = bf16[4,128,128]{2,1,0:T(8,128)(2,1)S(1)} all-to-all(bf16[4,128,128]{2,1,0:T(8,128)(2,1)S(1)} %broadcast_select_fusion), channel_id=1, replica_groups={{256,128,384,0},{264,136,392,8},{272,144,400,16},{280,152,408,24},{288,..., dimensions={0} | all-to-all | bytes 262144 | tf_op jit(solution)/shard_map/all_to_all | solution.py:31
  111.9 1.8 %shard_map.82 = bf16[4,3,256,128]{3,2,1,0:T(8,128)(2,1)S(1)} custom-call(s32[5]{0:T(128)S(1)} %stack.23.place_ref.refs_0_, bf16[4,256,128]{2,1,0:T(8,128)(2,1)S(1)} %get-tuple-element.17.refs_0_.p0_ref.refs_1_, bf16[4,256,128]{2,1,0:T(8,128)(2,1)S(1)} %collective-permute-done.refs_1_.p1_ref.refs_2_, ...), custom_call_target="tpu_custom_call" | custom-call | flops 536870912 | bytes 3145728 | tf_op jit(solution)/shard_map/pallas_call | solution.py:45
  113.7 14.0 %all_to_all.28.in_ref = bf16[4,3,256,128]{3,2,1,0:T(8,128)(2,1)S(1)} all-to-all(bf16[4,3,256,128]{3,2,1,0:T(8,128)(2,1)S(1)} %shard_map.82), channel_id=1, replica_groups={{16,8,24,0},{48,40,56,32},{80,72,88,64},{112,104,120,96},{144,136,152,1..., dimensions={0} | all-to-all | bytes 1572864 | tf_op jit(solution)/shard_map/all_to_all | solution.py:31
  127.7 1.0 shard_map.83
  (4 shorter events, 0.1 us)
Async XLA Ops:
  2.3 46.9 %all-to-all-start = ((bf16[8,64,512]{2,1,0:T(8,128)(2,1)}), bf16[8,64,512]{2,1,0:T(8,128)(2,1)S(1)}, u32[]{:S(2)}, u32[]{:S(2)}) async-start(bf16[8,64,512]{2,1,0:T(8,128)(2,1)} %shard_map.76), calls=%async_computation | async-start | bytes 1048576 | tf_op jit(solution)/shard_map/all_to_all | solution.py:31
  19.4 10.7 %collective-permute-start = (bf16[4,256,128]{2,1,0:T(8,128)(2,1)S(1)}, bf16[4,256,128]{2,1,0:T(8,128)(2,1)S(1)}, u32[]{:S(2)}, u32[]{:S(2)}) collective-permute-start(bf16[4,256,128]{2,1,0:T(8,128)(2,1)S(1)} %get-tuple-element.18), channel_id=1, source_target_pairs={{0,8},{8,16},{16,24},{24,0},{32,40},{40,48},{48,56},{56,32},{64,72... | collective-permute-start | bytes 786440 | tf_op jit(solution)/shard_map/ppermute | solution.py:263
  22.9 12.7 %collective-permute-start.1 = (bf16[4,256,128]{2,1,0:T(8,128)(2,1)S(1)}, bf16[4,256,128]{2,1,0:T(8,128)(2,1)S(1)}, u32[]{:S(2)}, u32[]{:S(2)}) collective-permute-start(bf16[4,256,128]{2,1,0:T(8,128)(2,1)S(1)} %get-tuple-element.19), channel_id=1, source_target_pairs={{0,16},{8,24},{16,0},{24,8},{32,48},{40,56},{48,32},{56,40},{64,80... | collective-permute-start | bytes 786440 | tf_op jit(solution)/shard_map/ppermute | solution.py:263
  25.8 13.6 %collective-permute-start.2 = (bf16[4,256,128]{2,1,0:T(8,128)(2,1)S(1)}, bf16[4,256,128]{2,1,0:T(8,128)(2,1)S(1)}, u32[]{:S(2)}, u32[]{:S(2)}) collective-permute-start(bf16[4,256,128]{2,1,0:T(8,128)(2,1)S(1)} %get-tuple-element.20), channel_id=1, source_target_pairs={{0,24},{8,0},{16,8},{24,16},{32,56},{40,32},{48,40},{56,48},{64,88... | collective-permute-start | bytes 786440 | tf_op jit(solution)/shard_map/ppermute | solution.py:263
  39.4 16.9 %collective-permute-start.5 = (bf16[1024,128]{1,0:T(8,128)(2,1)S(1)}, bf16[1024,128]{1,0:T(8,128)(2,1)S(1)}, u32[]{:S(2)}, u32[]{:S(2)}) collective-permute-start(bf16[1024,128]{1,0:T(8,128)(2,1)S(1)} %shard_map.78.refs_0_), channel_id=1, source_target_pairs={{0,6},{1,7},{2,0},{3,1},{4,2},{5,3},{6,4},{7,5},{8,14},{9,15},{10,... | collective-permute-start | bytes 786440 | tf_op jit(solution)/shard_map/ppermute | solution.py:267
  42.2 16.1 %collective-permute-start.4 = (bf16[1024,128]{1,0:T(8,128)(2,1)S(1)}, bf16[1024,128]{1,0:T(8,128)(2,1)S(1)}, u32[]{:S(2)}, u32[]{:S(2)}) collective-permute-start(bf16[1024,128]{1,0:T(8,128)(2,1)S(1)} %shard_map.78.refs_0_), channel_id=1, source_target_pairs={{0,4},{1,5},{2,6},{3,7},{4,0},{5,1},{6,2},{7,3},{8,12},{9,13},{10,... | collective-permute-start | bytes 786440 | tf_op jit(solution)/shard_map/ppermute | solution.py:267
  45.2 15.5 %collective-permute-start.3 = (bf16[1024,128]{1,0:T(8,128)(2,1)S(1)}, bf16[1024,128]{1,0:T(8,128)(2,1)S(1)}, u32[]{:S(2)}, u32[]{:S(2)}) collective-permute-start(bf16[1024,128]{1,0:T(8,128)(2,1)S(1)} %shard_map.78.refs_0_), channel_id=1, source_target_pairs={{0,2},{1,3},{2,4},{3,5},{4,6},{5,7},{6,0},{7,1},{8,10},{9,11},{10,... | collective-permute-start | bytes 786440 | tf_op jit(solution)/shard_map/ppermute | solution.py:267
  49.2 13.7 %copy-start = (bf16[8,64,512]{2,1,0:T(8,128)(2,1)}, bf16[8,64,512]{2,1,0:T(8,128)(2,1)S(1)}, u32[]{:S(2)}) copy-start(bf16[8,64,512]{2,1,0:T(8,128)(2,1)S(1)} %all-to-all-done.refs_8_) | copy-start | bytes 1572868
  49.2 14.9 %collective-permute-start.10 = (bf16[8,64,512]{2,1,0:T(8,128)(2,1)S(1)}, bf16[8,64,512]{2,1,0:T(8,128)(2,1)S(1)}, u32[]{:S(2)}, u32[]{:S(2)}) collective-permute-start(bf16[8,64,512]{2,1,0:T(8,128)(2,1)S(1)} %all-to-all-done.refs_8_), channel_id=1, source_target_pairs={{0,32},{8,40},{16,48},{24,56},{32,0},{40,8},{48,16},{56,24},{64,96... | collective-permute-start | bytes 1572872 | tf_op jit(solution)/shard_map/ppermute | solution.py:245
  52.2 10.8 %collective-permute-start.6 = (bf16[1024,128]{1,0:T(8,128)(2,1)S(1)}, bf16[1024,128]{1,0:T(8,128)(2,1)S(1)}, u32[]{:S(2)}, u32[]{:S(2)}) collective-permute-start(bf16[1024,128]{1,0:T(8,128)(2,1)S(1)} %shard_map.78.refs_0_), channel_id=1, source_target_pairs={{0,1},{1,0},{2,3},{3,2},{4,5},{5,4},{6,7},{7,6},{8,9},{9,8},{10,11... | collective-permute-start | bytes 786440 | tf_op jit(solution)/shard_map/ppermute | solution.py:269
  56.4 6.6 %collective-permute-start.9 = (bf16[1024,128]{1,0:T(8,128)(2,1)S(1)}, bf16[1024,128]{1,0:T(8,128)(2,1)S(1)}, u32[]{:S(2)}, u32[]{:S(2)}) collective-permute-start(bf16[1024,128]{1,0:T(8,128)(2,1)S(1)} %collective-permute-done.5.refs_3_), channel_id=1, source_target_pairs={{0,1},{1,0},{2,3},{3,2},{4,5},{5,4},{6,7},{7,6},{8,9},{9,8},{10,11... | collective-permute-start | bytes 786440 | tf_op jit(solution)/shard_map/ppermute | solution.py:269
  58.3 4.7 %collective-permute-start.8 = (bf16[1024,128]{1,0:T(8,128)(2,1)S(1)}, bf16[1024,128]{1,0:T(8,128)(2,1)S(1)}, u32[]{:S(2)}, u32[]{:S(2)}) collective-permute-start(bf16[1024,128]{1,0:T(8,128)(2,1)S(1)} %collective-permute-done.4.refs_2_), channel_id=1, source_target_pairs={{0,1},{1,0},{2,3},{3,2},{4,5},{5,4},{6,7},{7,6},{8,9},{9,8},{10,11... | collective-permute-start | bytes 786440 | tf_op jit(solution)/shard_map/ppermute | solution.py:269
  60.7 3.4 %collective-permute-start.7 = (bf16[1024,128]{1,0:T(8,128)(2,1)S(1)}, bf16[1024,128]{1,0:T(8,128)(2,1)S(1)}, u32[]{:S(2)}, u32[]{:S(2)}) collective-permute-start(bf16[1024,128]{1,0:T(8,128)(2,1)S(1)} %collective-permute-done.3.refs_1_), channel_id=1, source_target_pairs={{0,1},{1,0},{2,3},{3,2},{4,5},{5,4},{6,7},{7,6},{8,9},{9,8},{10,11... | collective-permute-start | bytes 786440 | tf_op jit(solution)/shard_map/ppermute | solution.py:269
  64.2 0.8 copy-start.1

commit v8 on v7

--- a/solution.py
+++ b/solution.py
@@ -279,8 +279,8 @@
         2 * tokens * depth * width,
         4 * 1024 * 1024,
         smem=(0,),
-        hbm=(2 * NX + 1, 2 * NX + 2),
-        anywhere=(2 * NX + 3,),
+        hbm=(),
+        anywhere=(2 * NX + 1, 2 * NX + 2, 2 * NX + 3),
         scratch=[pltpu.VMEM((NX, depth // NX, width), BF16), pltpu.SemaphoreType.DMA((NX, 2, 2))],
     )(place, *shares, weight, beside, key_states)
     parts = exchange(parts, y_line)

time: 130 us -> 129 us (level)
  no operation moved by 1% of the time
where the time goes in v8:
time: 129 us; the launch traced here: 128 us
  blocking collectives  56.8 us (44%)
  starting transfers between devices  46.6 us (36%)
  waiting for transfers between devices  12.8 us (10%)
  Pallas kernels  11 us (9%)
    all_to_all x4, blocking collectives, exchange(): return lax.all_to_all(pieces, 'ctx', 0, 0, axis_index_groups=group)  56.8 us
    all_to_all x1, starting transfers between devices, exchange(): return lax.all_to_all(pieces, 'ctx', 0, 0, axis_index_groups=group)  15.1 us
    pallas_call x8, Pallas kernels, run(): pl.pallas_call(kernel, out_shape=out_shape, in_specs=specs, out_specs=out...  11 us
    ppermute x3, starting transfers between devices, local(): packed[d] = lax.ppermute(packed[d], 'ctx', turn)  10.7 us
    ppermute x3, starting transfers between devices, local(): lax.ppermute(mine, 'tp', [(t, (t + 2 * d) % tp) for t in range(tp)])  9.76 us
    ppermute x3, waiting for transfers between devices, local(): packed[d] = lax.ppermute(packed[d], 'ctx', turn)  9.31 us
    ppermute x4, starting transfers between devices, local(): shares = shares + [lax.ppermute(share, 'tp', swap) for share in shares]  8.16 us
    ppermute x1, starting transfers between devices, local(): lax.ppermute(weight, 'ctx', [(i, (i // NY ^ 1) * NY + i % NY) for i in ra...  2.93 us
  transfers between devices with their start and end apart: 12, of which 4 were waited for; matrix products, arithmetic and copies ran while one was open for 0% of the time, Pallas kernels for 2%

profile of v8, /device:TPU:14, one launch (start us, length us, event | category | flops | bytes accessed | tf_op | source)
XLA Modules:
  0.0 128.3 jit_solution(3660398703971758952)
XLA Ops:
  0.6 1.7 %shard_map.76 = bf16[8,64,512]{2,1,0:T(8,128)(2,1)} custom-call(bf16[64,512]{1,0:T(8,128)(2,1)} %w_ref.1), custom_call_target="tpu_custom_call" | custom-call | bytes 1048576 | tf_op jit(solution)/shard_map/pallas_call | solution.py:45
  2.4 15.1 %all-to-all-start = ((bf16[8,64,512]{2,1,0:T(8,128)(2,1)}), bf16[8,64,512]{2,1,0:T(8,128)(2,1)S(1)}, u32[]{:S(2)}, u32[]{:S(2)}) async-start(bf16[8,64,512]{2,1,0:T(8,128)(2,1)} %shard_map.76), calls=%async_computation | async-start | bytes 1048576 | tf_op jit(solution)/shard_map/all_to_all | solution.py:31
  17.5 0.1 stack.23.place_ref.refs_0_
  17.5 1.9 %shard_map.77 = (bf16[4,256,128]{2,1,0:T(8,128)(2,1)S(1)}, bf16[4,256,128]{2,1,0:T(8,128)(2,1)S(1)}, bf16[4,256,128]{2,1,0:T(8,128)(2,1)S(1)}, bf16[4,256,128]{2,1,0:T(8,128)(2,1)S(1)}) custom-call(s32[5]{0:T(128)S(1)} %stack.23.place_ref.refs_0_, bf16[256,512]{1,0:T(8,128)(2,1)} %q_ref.1, bf16[256,512]{1,0:T(8,128)(2,1)} %k_ref.1, bf16[256,512]{1,0:T(8,128)(2,1)} %v_ref.1, ...), custom_call_target="tpu_custom_call" | custom-call | bytes 2097152 | tf_op jit(solution)/shard_map/pallas_call | solution.py:45
  19.4 3.5 %collective-permute-start = (bf16[4,256,128]{2,1,0:T(8,128)(2,1)S(1)}, bf16[4,256,128]{2,1,0:T(8,128)(2,1)S(1)}, u32[]{:S(2)}, u32[]{:S(2)}) collective-permute-start(bf16[4,256,128]{2,1,0:T(8,128)(2,1)S(1)} %get-tuple-element.18), channel_id=1, source_target_pairs={{0,8},{8,16},{16,24},{24,0},{32,40},{40,48},{48,56},{56,32},{64,72... | collective-permute-start | bytes 786440 | tf_op jit(solution)/shard_map/ppermute | solution.py:263
  22.9 2.8 %collective-permute-start.1 = (bf16[4,256,128]{2,1,0:T(8,128)(2,1)S(1)}, bf16[4,256,128]{2,1,0:T(8,128)(2,1)S(1)}, u32[]{:S(2)}, u32[]{:S(2)}) collective-permute-start(bf16[4,256,128]{2,1,0:T(8,128)(2,1)S(1)} %get-tuple-element.19), channel_id=1, source_target_pairs={{0,16},{8,24},{16,0},{24,8},{32,48},{40,56},{48,32},{56,40},{64,80... | collective-permute-start | bytes 786440 | tf_op jit(solution)/shard_map/ppermute | solution.py:263
  25.8 4.3 %collective-permute-start.2 = (bf16[4,256,128]{2,1,0:T(8,128)(2,1)S(1)}, bf16[4,256,128]{2,1,0:T(8,128)(2,1)S(1)}, u32[]{:S(2)}, u32[]{:S(2)}) collective-permute-start(bf16[4,256,128]{2,1,0:T(8,128)(2,1)S(1)} %get-tuple-element.20), channel_id=1, source_target_pairs={{0,24},{8,0},{16,8},{24,16},{32,56},{40,32},{48,40},{56,48},{64,88... | collective-permute-start | bytes 786440 | tf_op jit(solution)/shard_map/ppermute | solution.py:263
  30.1 0.0 collective-permute-done.refs_1_.p1_ref.refs_2_
  30.1 5.5 %collective-permute-done.1.refs_2_.p2_ref.refs_3_ = bf16[4,256,128]{2,1,0:T(8,128)(2,1)S(1)} collective-permute-done((bf16[4,256,128]{2,1,0:T(8,128)(2,1)S(1)}, bf16[4,256,128]{2,1,0:T(8,128)(2,1)S(1)}, u32[]{:S(2)}, u32[]{:S(2)}) %collective-permute-start.1) | collective-permute-done | bytes 262176 | tf_op jit(solution)/shard_map/ppermute | solution.py:263
  35.6 3.8 %collective-permute-done.2.refs_3_.p3_ref.refs_4_ = bf16[4,256,128]{2,1,0:T(8,128)(2,1)S(1)} collective-permute-done((bf16[4,256,128]{2,1,0:T(8,128)(2,1)S(1)}, bf16[4,256,128]{2,1,0:T(8,128)(2,1)S(1)}, u32[]{:S(2)}, u32[]{:S(2)}) %collective-permute-start.2) | collective-permute-done | bytes 262176 | tf_op jit(solution)/shard_map/ppermute | solution.py:263
  39.4 2.7 %collective-permute-start.5 = (bf16[1024,128]{1,0:T(8,128)(2,1)S(1)}, bf16[1024,128]{1,0:T(8,128)(2,1)S(1)}, u32[]{:S(2)}, u32[]{:S(2)}) collective-permute-start(bf16[1024,128]{1,0:T(8,128)(2,1)S(1)} %shard_map.78.refs_0_), channel_id=1, source_target_pairs={{0,6},{1,7},{2,0},{3,1},{4,2},{5,3},{6,4},{7,5},{8,14},{9,15},{10,... | collective-permute-start | bytes 786440 | tf_op jit(solution)/shard_map/ppermute | solution.py:267
  42.2 3.0 %collective-permute-start.4 = (bf16[1024,128]{1,0:T(8,128)(2,1)S(1)}, bf16[1024,128]{1,0:T(8,128)(2,1)S(1)}, u32[]{:S(2)}, u32[]{:S(2)}) collective-permute-start(bf16[1024,128]{1,0:T(8,128)(2,1)S(1)} %shard_map.78.refs_0_), channel_id=1, source_target_pairs={{0,4},{1,5},{2,6},{3,7},{4,0},{5,1},{6,2},{7,3},{8,12},{9,13},{10,... | collective-permute-start | bytes 786440 | tf_op jit(solution)/shard_map/ppermute | solution.py:267
  45.2 4.0 %collective-permute-start.3 = (bf16[1024,128]{1,0:T(8,128)(2,1)S(1)}, bf16[1024,128]{1,0:T(8,128)(2,1)S(1)}, u32[]{:S(2)}, u32[]{:S(2)}) collective-permute-start(bf16[1024,128]{1,0:T(8,128)(2,1)S(1)} %shard_map.78.refs_0_), channel_id=1, source_target_pairs={{0,2},{1,3},{2,4},{3,5},{4,6},{5,7},{6,0},{7,1},{8,10},{9,11},{10,... | collective-permute-start | bytes 786440 | tf_op jit(solution)/shard_map/ppermute | solution.py:267
  49.2 0.0 all-to-all-done.refs_8_
  49.2 2.9 %collective-permute-start.10 = (bf16[8,64,512]{2,1,0:T(8,128)(2,1)S(1)}, bf16[8,64,512]{2,1,0:T(8,128)(2,1)S(1)}, u32[]{:S(2)}, u32[]{:S(2)}) collective-permute-start(bf16[8,64,512]{2,1,0:T(8,128)(2,1)S(1)} %all-to-all-done.refs_8_), channel_id=1, source_target_pairs={{0,32},{8,40},{16,48},{24,56},{32,0},{40,8},{48,16},{56,24},{64,96... | collective-permute-start | bytes 1572872 | tf_op jit(solution)/shard_map/ppermute | solution.py:245
  52.2 1.9 %collective-permute-start.6 = (bf16[1024,128]{1,0:T(8,128)(2,1)S(1)}, bf16[1024,128]{1,0:T(8,128)(2,1)S(1)}, u32[]{:S(2)}, u32[]{:S(2)}) collective-permute-start(bf16[1024,128]{1,0:T(8,128)(2,1)S(1)} %shard_map.78.refs_0_), channel_id=1, source_target_pairs={{0,1},{1,0},{2,3},{3,2},{4,5},{5,4},{6,7},{7,6},{8,9},{9,8},{10,11... | collective-permute-start | bytes 786440 | tf_op jit(solution)/shard_map/ppermute | solution.py:269
  54.1 2.3 %collective-permute-done.5.refs_3_ = bf16[1024,128]{1,0:T(8,128)(2,1)S(1)} collective-permute-done((bf16[1024,128]{1,0:T(8,128)(2,1)S(1)}, bf16[1024,128]{1,0:T(8,128)(2,1)S(1)}, u32[]{:S(2)}, u32[]{:S(2)}) %collective-permute-start.5) | collective-permute-done | bytes 262176 | tf_op jit(solution)/shard_map/ppermute | solution.py:267
  56.4 1.9 %collective-permute-start.9 = (bf16[1024,128]{1,0:T(8,128)(2,1)S(1)}, bf16[1024,128]{1,0:T(8,128)(2,1)S(1)}, u32[]{:S(2)}, u32[]{:S(2)}) collective-permute-start(bf16[1024,128]{1,0:T(8,128)(2,1)S(1)} %collective-permute-done.5.refs_3_), channel_id=1, source_target_pairs={{0,1},{1,0},{2,3},{3,2},{4,5},{5,4},{6,7},{7,6},{8,9},{9,8},{10,11... | collective-permute-start | bytes 786440 | tf_op jit(solution)/shard_map/ppermute | solution.py:269
  58.3 0.0 collective-permute-done.4.refs_2_
  58.3 2.4 %collective-permute-start.8 = (bf16[1024,128]{1,0:T(8,128)(2,1)S(1)}, bf16[1024,128]{1,0:T(8,128)(2,1)S(1)}, u32[]{:S(2)}, u32[]{:S(2)}) collective-permute-start(bf16[1024,128]{1,0:T(8,128)(2,1)S(1)} %collective-permute-done.4.refs_2_), channel_id=1, source_target_pairs={{0,1},{1,0},{2,3},{3,2},{4,5},{5,4},{6,7},{7,6},{8,9},{9,8},{10,11... | collective-permute-start | bytes 786440 | tf_op jit(solution)/shard_map/ppermute | solution.py:269
  60.7 0.0 collective-permute-done.3.refs_1_
  60.8 1.9 %collective-permute-start.7 = (bf16[1024,128]{1,0:T(8,128)(2,1)S(1)}, bf16[1024,128]{1,0:T(8,128)(2,1)S(1)}, u32[]{:S(2)}, u32[]{:S(2)}) collective-permute-start(bf16[1024,128]{1,0:T(8,128)(2,1)S(1)} %collective-permute-done.3.refs_1_), channel_id=1, source_target_pairs={{0,1},{1,0},{2,3},{3,2},{4,5},{5,4},{6,7},{7,6},{8,9},{9,8},{10,11... | collective-permute-start | bytes 786440 | tf_op jit(solution)/shard_map/ppermute | solution.py:269
  62.7 0.3 shard_map.79.refs_10_.key_ref.refs_6_
  63.0 0.0 collective-permute-done.6.refs_4_
  63.0 0.0 collective-permute-done.9.refs_7_
  63.0 0.0 collective-permute-done.8.refs_6_
  63.0 1.2 collective-permute-done.7.refs_5_
  64.2 0.0 collective-permute-done.10.refs_9_
  64.2 3.5 %shard_map.80 = bf16[4,1024,128]{2,1,0:T(8,128)(2,1)S(1)} custom-call(s32[5]{0:T(128)S(1)} %stack.23.place_ref.refs_0_, bf16[1024,128]{1,0:T(8,128)(2,1)S(1)} %shard_map.78.refs_0_, bf16[1024,128]{1,0:T(8,128)(2,1)S(1)} %collective-permute-done.3.refs_1_, bf16[1024,128]{1,0:T(8,128)(2,1)S(1)} %collective-permute-done.4.refs_2_, ...), custom_call_target="tpu_custom_call" | custom-call | flops 1073741824 | bytes 4194304 | tf_op jit(solution)/shard_map/pallas_call | solution.py:45
  67.7 17.0 %all_to_all.25.part_ref = bf16[4,1024,128]{2,1,0:T(8,128)(2,1)S(1)} all-to-all(bf16[4,1024,128]{2,1,0:T(8,128)(2,1)S(1)} %shard_map.80), channel_id=1, replica_groups={{16,8,24,0},{48,40,56,32},{80,72,88,64},{112,104,120,96},{144,136,152,1..., dimensions={0} | all-to-all | bytes 2097152 | tf_op jit(solution)/shard_map/all_to_all | solution.py:31
  84.7 0.8 shard_map.81
  85.6 10.1 %all_to_all.26.refs_8_ = bf16[4,2,128,128]{3,2,1,0:T(8,128)(2,1)S(1)} all-to-all(bf16[4,2,128,128]{3,2,1,0:T(8,128)(2,1)S(1)} %get-tuple-element.23), channel_id=1, replica_groups={{64,32,96,0},{72,40,104,8},{80,48,112,16},{88,56,120,24},{192,160,224,1..., dimensions={0} | all-to-all | bytes 524288 | tf_op jit(solution)/shard_map/all_to_all | solution.py:31
  95.7 0.1 broadcast_select_fusion
  95.8 15.7 %all_to_all.27.refs_9_ = bf16[4,128,128]{2,1,0:T(8,128)(2,1)S(1)} all-to-all(bf16[4,128,128]{2,1,0:T(8,128)(2,1)S(1)} %broadcast_select_fusion), channel_id=1, replica_groups={{256,128,384,0},{264,136,392,8},{272,144,400,16},{280,152,408,24},{288,..., dimensions={0} | all-to-all | bytes 262144 | tf_op jit(solution)/shard_map/all_to_all | solution.py:31
  111.5 1.8 %shard_map.82 = bf16[4,3,256,128]{3,2,1,0:T(8,128)(2,1)S(1)} custom-call(s32[5]{0:T(128)S(1)} %stack.23.place_ref.refs_0_, bf16[4,256,128]{2,1,0:T(8,128)(2,1)S(1)} %get-tuple-element.17.refs_0_.p0_ref.refs_1_, bf16[4,256,128]{2,1,0:T(8,128)(2,1)S(1)} %collective-permute-done.refs_1_.p1_ref.refs_2_, ...), custom_call_target="tpu_custom_call" | custom-call | flops 536870912 | bytes 3145728 | tf_op jit(solution)/shard_map/pallas_call | solution.py:45
  113.3 14.0 %all_to_all.28.in_ref = bf16[4,3,256,128]{3,2,1,0:T(8,128)(2,1)S(1)} all-to-all(bf16[4,3,256,128]{3,2,1,0:T(8,128)(2,1)S(1)} %shard_map.82), channel_id=1, replica_groups={{16,8,24,0},{48,40,56,32},{80,72,88,64},{112,104,120,96},{144,136,152,1..., dimensions={0} | all-to-all | bytes 1572864 | tf_op jit(solution)/shard_map/all_to_all | solution.py:31
  127.3 1.0 shard_map.83
  (4 shorter events, 0.1 us)
Async XLA Ops:
  2.4 46.9 %all-to-all-start = ((bf16[8,64,512]{2,1,0:T(8,128)(2,1)}), bf16[8,64,512]{2,1,0:T(8,128)(2,1)S(1)}, u32[]{:S(2)}, u32[]{:S(2)}) async-start(bf16[8,64,512]{2,1,0:T(8,128)(2,1)} %shard_map.76), calls=%async_computation | async-start | bytes 1048576 | tf_op jit(solution)/shard_map/all_to_all | solution.py:31
  19.4 10.7 %collective-permute-start = (bf16[4,256,128]{2,1,0:T(8,128)(2,1)S(1)}, bf16[4,256,128]{2,1,0:T(8,128)(2,1)S(1)}, u32[]{:S(2)}, u32[]{:S(2)}) collective-permute-start(bf16[4,256,128]{2,1,0:T(8,128)(2,1)S(1)} %get-tuple-element.18), channel_id=1, source_target_pairs={{0,8},{8,16},{16,24},{24,0},{32,40},{40,48},{48,56},{56,32},{64,72... | collective-permute-start | bytes 786440 | tf_op jit(solution)/shard_map/ppermute | solution.py:263
  22.9 12.7 %collective-permute-start.1 = (bf16[4,256,128]{2,1,0:T(8,128)(2,1)S(1)}, bf16[4,256,128]{2,1,0:T(8,128)(2,1)S(1)}, u32[]{:S(2)}, u32[]{:S(2)}) collective-permute-start(bf16[4,256,128]{2,1,0:T(8,128)(2,1)S(1)} %get-tuple-element.19), channel_id=1, source_target_pairs={{0,16},{8,24},{16,0},{24,8},{32,48},{40,56},{48,32},{56,40},{64,80... | collective-permute-start | bytes 786440 | tf_op jit(solution)/shard_map/ppermute | solution.py:263
  25.8 13.6 %collective-permute-start.2 = (bf16[4,256,128]{2,1,0:T(8,128)(2,1)S(1)}, bf16[4,256,128]{2,1,0:T(8,128)(2,1)S(1)}, u32[]{:S(2)}, u32[]{:S(2)}) collective-permute-start(bf16[4,256,128]{2,1,0:T(8,128)(2,1)S(1)} %get-tuple-element.20), channel_id=1, source_target_pairs={{0,24},{8,0},{16,8},{24,16},{32,56},{40,32},{48,40},{56,48},{64,88... | collective-permute-start | bytes 786440 | tf_op jit(solution)/shard_map/ppermute | solution.py:263
  39.4 16.9 %collective-permute-start.5 = (bf16[1024,128]{1,0:T(8,128)(2,1)S(1)}, bf16[1024,128]{1,0:T(8,128)(2,1)S(1)}, u32[]{:S(2)}, u32[]{:S(2)}) collective-permute-start(bf16[1024,128]{1,0:T(8,128)(2,1)S(1)} %shard_map.78.refs_0_), channel_id=1, source_target_pairs={{0,6},{1,7},{2,0},{3,1},{4,2},{5,3},{6,4},{7,5},{8,14},{9,15},{10,... | collective-permute-start | bytes 786440 | tf_op jit(solution)/shard_map/ppermute | solution.py:267
  42.2 16.1 %collective-permute-start.4 = (bf16[1024,128]{1,0:T(8,128)(2,1)S(1)}, bf16[1024,128]{1,0:T(8,128)(2,1)S(1)}, u32[]{:S(2)}, u32[]{:S(2)}) collective-permute-start(bf16[1024,128]{1,0:T(8,128)(2,1)S(1)} %shard_map.78.refs_0_), channel_id=1, source_target_pairs={{0,4},{1,5},{2,6},{3,7},{4,0},{5,1},{6,2},{7,3},{8,12},{9,13},{10,... | collective-permute-start | bytes 786440 | tf_op jit(solution)/shard_map/ppermute | solution.py:267
  45.2 15.5 %collective-permute-start.3 = (bf16[1024,128]{1,0:T(8,128)(2,1)S(1)}, bf16[1024,128]{1,0:T(8,128)(2,1)S(1)}, u32[]{:S(2)}, u32[]{:S(2)}) collective-permute-start(bf16[1024,128]{1,0:T(8,128)(2,1)S(1)} %shard_map.78.refs_0_), channel_id=1, source_target_pairs={{0,2},{1,3},{2,4},{3,5},{4,6},{5,7},{6,0},{7,1},{8,10},{9,11},{10,... | collective-permute-start | bytes 786440 | tf_op jit(solution)/shard_map/ppermute | solution.py:267
  49.2 14.9 %collective-permute-start.10 = (bf16[8,64,512]{2,1,0:T(8,128)(2,1)S(1)}, bf16[8,64,512]{2,1,0:T(8,128)(2,1)S(1)}, u32[]{:S(2)}, u32[]{:S(2)}) collective-permute-start(bf16[8,64,512]{2,1,0:T(8,128)(2,1)S(1)} %all-to-all-done.refs_8_), channel_id=1, source_target_pairs={{0,32},{8,40},{16,48},{24,56},{32,0},{40,8},{48,16},{56,24},{64,96... | collective-permute-start | bytes 1572872 | tf_op jit(solution)/shard_map/ppermute | solution.py:245
  52.2 10.8 %collective-permute-start.6 = (bf16[1024,128]{1,0:T(8,128)(2,1)S(1)}, bf16[1024,128]{1,0:T(8,128)(2,1)S(1)}, u32[]{:S(2)}, u32[]{:S(2)}) collective-permute-start(bf16[1024,128]{1,0:T(8,128)(2,1)S(1)} %shard_map.78.refs_0_), channel_id=1, source_target_pairs={{0,1},{1,0},{2,3},{3,2},{4,5},{5,4},{6,7},{7,6},{8,9},{9,8},{10,11... | collective-permute-start | bytes 786440 | tf_op jit(solution)/shard_map/ppermute | solution.py:269
  56.4 6.6 %collective-permute-start.9 = (bf16[1024,128]{1,0:T(8,128)(2,1)S(1)}, bf16[1024,128]{1,0:T(8,128)(2,1)S(1)}, u32[]{:S(2)}, u32[]{:S(2)}) collective-permute-start(bf16[1024,128]{1,0:T(8,128)(2,1)S(1)} %collective-permute-done.5.refs_3_), channel_id=1, source_target_pairs={{0,1},{1,0},{2,3},{3,2},{4,5},{5,4},{6,7},{7,6},{8,9},{9,8},{10,11... | collective-permute-start | bytes 786440 | tf_op jit(solution)/shard_map/ppermute | solution.py:269
  58.3 4.7 %collective-permute-start.8 = (bf16[1024,128]{1,0:T(8,128)(2,1)S(1)}, bf16[1024,128]{1,0:T(8,128)(2,1)S(1)}, u32[]{:S(2)}, u32[]{:S(2)}) collective-permute-start(bf16[1024,128]{1,0:T(8,128)(2,1)S(1)} %collective-permute-done.4.refs_2_), channel_id=1, source_target_pairs={{0,1},{1,0},{2,3},{3,2},{4,5},{5,4},{6,7},{7,6},{8,9},{9,8},{10,11... | collective-permute-start | bytes 786440 | tf_op jit(solution)/shard_map/ppermute | solution.py:269
  60.8 3.4 %collective-permute-start.7 = (bf16[1024,128]{1,0:T(8,128)(2,1)S(1)}, bf16[1024,128]{1,0:T(8,128)(2,1)S(1)}, u32[]{:S(2)}, u32[]{:S(2)}) collective-permute-start(bf16[1024,128]{1,0:T(8,128)(2,1)S(1)} %collective-permute-done.3.refs_1_), channel_id=1, source_target_pairs={{0,1},{1,0},{2,3},{3,2},{4,5},{5,4},{6,7},{7,6},{8,9},{9,8},{10,11... | collective-permute-start | bytes 786440 | tf_op jit(solution)/shard_map/ppermute | solution.py:269
